TPU v7x, 512 devices: a whole 4x8x8 slice. The times are simulated.
512 devices in a mesh: rep: 8 (over z_hi, x), dp: 64 (over y, z_lo, core).
Axes of the slice: x: 4, y: 8, z: 8 (z_hi: 2, z_lo: 4; z = z_hi * 4 + z_lo), core: 2. Of those that a mesh axis runs over, the one named last changes fastest.
Arguments:
- query_states: bfloat16 [8, 512, 32, 4096], P('rep', 'dp'), may hold values from -6 to 6
- query_lengths: int32 [8, 512], P('rep', 'dp'), may hold values from 1 to 32, as said below
- norm_gain: float32 [4096], replicated, may hold values from 0.5 to 2
- positives: bfloat16 [8, 512, 4096], P('rep', 'dp'), may hold values from -0.25 to 0.25
- mined_pool: bfloat16 [8, 1024, 4096], P('rep', 'dp'), may hold values from -0.25 to 0.25
- hard_ids: int32 [8, 512, 7], P('rep', 'dp'), may hold values from 0 to 1023, as said below
Outputs:
- query_grad: bfloat16 [8, 512, 32, 4096], P('rep', 'dp')
- positive_gradient: float32 [8, 512, 4096], P('rep', 'dp')
- pool_grad: float32 [8, 1024, 4096], P('rep', 'dp')
- gain_grad: float32 [4096], replicated
Inputs may be any that keep to these rules, and one draw needn't show every extreme that they name: `query_lengths`: in each group some query has 32 tokens. `hard_ids`: rows r * 16 to (r + 1) * 16 - 1 of a group's mined passages lie on device r of dp. The 56 ids of one device's queries name at most 2 rows of any one device; in every group one device's rows are named exactly 2 times by the queries of every device.
All inputs are finite; a program needn't handle non-finite values.
Results may differ from a plain program's by a relative error of at most 0.0039.
Values may be sent and summed in bfloat16 or wider, within the bound.
No kernel may reach another device: no remote copies, remote signals or barrier semaphores. Data moves between devices by JAX's collectives and lax.ppermute only.
A program may use at most 64 MiB of HBM per device.

v0:
```python
import jax
import jax.numpy as jnp
from jax import lax
from jax.sharding import PartitionSpec as P

SOFTMAX_WARMTH = 0.02
QUERY_SCALE = 512.0
POOL_SCALE = 16.0
HIGHEST_ACCURACY = lax.Precision.HIGHEST


def embed(states, lengths, gain):
    square = jnp.mean(states * states, axis=-1, keepdims=True)
    normed = states * lax.rsqrt(square + 1e-05) * gain
    positions = jnp.arange(states.shape[1])
    token_mask = (positions[None, :] < lengths[:, None]).astype(jnp.float32)
    pooled = jnp.sum(normed * token_mask[:, :, None], axis=1) / lengths[:, None].astype(jnp.float32)
    return pooled * lax.rsqrt(jnp.sum(pooled * pooled, axis=-1, keepdims=True) + 1e-06)


def row_similarity(left, right):
    return lax.dot_general(
        left, right, (((1,), (1,)), ((), ())), preferred_element_type=jnp.float32
    )


def local(query_states, query_lengths, norm_gain, positives, mined_pool, hard_ids):
    states32 = query_states[0].astype(jnp.float32)
    lengths = query_lengths[0]
    local_key_rows = positives[0]
    pool_rows = mined_pool[0]
    wanted = hard_ids[0].reshape(-1)
    hard_count = hard_ids.shape[2]
    embedded32, pullback = jax.vjp(
        lambda values_in, gain_in: embed(values_in, lengths, gain_in), states32, norm_gain
    )
    embedded_rows = embedded32.astype(jnp.bfloat16)
    embedding_single = embedded_rows.astype(jnp.float32)
    query_count = embedded_rows.shape[0]
    feature_width = embedded_rows.shape[1]
    owners = lax.axis_size("dp")
    requests = wanted.shape[0]
    neg_rows = pool_rows.shape[0]
    capacity = max(2, (requests + owners - 1) // owners + 1)
    block_row_list = lax.all_gather(local_key_rows, "dp", axis=0, tiled=True)
    pooling_weight = jnp.exp(row_similarity(embedded_rows, block_row_list) / SOFTMAX_WARMTH)
    positive_numerator = jnp.dot(
        pooling_weight.astype(jnp.bfloat16), block_row_list, preferred_element_type=jnp.float32
    )
    exp_total, positive_numerator = (jnp.sum(pooling_weight, axis=1), positive_numerator)
    owner_index = wanted // neg_rows
    local_row = wanted % neg_rows
    owner_hits = (owner_index[:, None] == jnp.arange(owners)[None, :]).astype(jnp.int32)
    earlier = jnp.cumsum(owner_hits, axis=0) - owner_hits
    slot_rank = jnp.sum(earlier * owner_hits, axis=1)
    slot_index = owner_index * capacity + slot_rank
    placed = slot_index[:, None] == jnp.arange(owners * capacity)[None, :]
    request = jnp.sum(jnp.where(placed, local_row[:, None], 0), axis=0).reshape(owners, capacity)
    asked_rows = lax.all_to_all(request, "dp", split_axis=0, concat_axis=0, tiled=True)
    served = jnp.take(pool_rows, asked_rows, axis=0)
    fetched = lax.all_to_all(served, "dp", split_axis=0, concat_axis=0, tiled=True)
    received = asked_rows
    hard_rows = jnp.take(fetched.reshape(owners * capacity, feature_width), slot_index, axis=0)
    hard_rows, slot_index, received = (
        hard_rows.reshape(query_count, hard_count, feature_width),
        slot_index,
        received,
    )
    hard_similarity = (
        jnp.einsum("rh,rxh->rx", embedded_rows, hard_rows, preferred_element_type=jnp.float32)
        / SOFTMAX_WARMTH
    )
    exponent_hard = jnp.exp(hard_similarity)
    denominator_totals = exp_total + jnp.sum(exponent_hard, axis=1)
    positive_numerator = positive_numerator + jnp.einsum(
        "qm,qmd->qd",
        exponent_hard.astype(jnp.bfloat16),
        hard_rows,
        preferred_element_type=jnp.float32,
    )
    embedding_gradient = (
        positive_numerator / denominator_totals[:, None] - local_key_rows.astype(jnp.float32)
    ) / SOFTMAX_WARMTH
    states_grad, gain_part = pullback(embedding_gradient)
    query_grad = (QUERY_SCALE * states_grad).astype(jnp.bfloat16)[None]
    gain_grad = lax.psum(gain_part, ("rep", "dp"))
    gathered_totals = lax.all_gather(denominator_totals, "dp", axis=0, tiled=True)
    block_row_list = lax.all_gather(embedded_rows, "dp", axis=0, tiled=True)
    softmax_probs = (
        jnp.exp(row_similarity(block_row_list, local_key_rows) / SOFTMAX_WARMTH)
        / gathered_totals[:, None]
    ).astype(jnp.bfloat16)
    key_running_sum = lax.dot_general(
        softmax_probs, block_row_list, (((0,), (0,)), ((), ())), preferred_element_type=jnp.float32
    )
    positive_gradient = ((key_running_sum - embedding_single) / SOFTMAX_WARMTH)[None]
    hard_summands = (
        (exponent_hard / denominator_totals[:, None])[:, :, None]
        * embedding_single[:, None, :]
        / SOFTMAX_WARMTH
    )
    outgoing = (
        jnp.zeros((owners * capacity, feature_width), jnp.float32)
        .at[slot_index]
        .set(hard_summands.reshape(-1, feature_width))
    )
    returned = lax.all_to_all(
        outgoing.reshape(owners, capacity, feature_width),
        "dp",
        split_axis=0,
        concat_axis=0,
        tiled=True,
    )
    member = (received.reshape(-1)[None, :] == jnp.arange(neg_rows)[:, None]).astype(jnp.float32)
    pool_grad = POOL_SCALE * jnp.dot(
        member, returned.reshape(owners * capacity, feature_width), precision=HIGHEST_ACCURACY
    )
    return (query_grad, positive_gradient, pool_grad[None], gain_grad)


def solution(mesh):
    placed = (
        P("rep", "dp", None, None),
        P("rep", "dp"),
        P(),
        P("rep", "dp", None),
        P("rep", "dp", None),
        P("rep", "dp", None),
    )
    return jax.shard_map(
        local,
        mesh=mesh,
        in_specs=placed,
        out_specs=(P("rep", "dp", None, None), P("rep", "dp", None), P("rep", "dp", None), P()),
        check_vma=False,
    )
```

profile of v0, /device:TPU:1, one launch (start us, length us, event | category | flops | bytes accessed | tf_op | source)
XLA Modules:
  0.0 466.5 jit_solution(10595488684374573259)
XLA Ops:
  7.2 0.7 all-gather.6.cloned.1.call-update
  8.0 0.7 bitcast_convert_fusion
  8.6 0.7 fusion.52
  9.4 2.1 fusion.11
  11.4 2.6 fusion.10
  14.3 0.7 multiply_convert_fusion
  15.9 24.1 %all_to_all.25 = s32[64,1,2]{2,1,0:T(1,128)S(1)} all-to-all(s32[64,1,2]{2,1,0:T(1,128)S(1)} %bitcast.93), channel_id=1, replica_groups=mesh['rep'=8,'dp'=64] {'dp'}, dimensions={0} | all-to-all | bytes 1024 | tf_op jit(solution)/shard_map/all_to_all | solution.py:59
  40.3 1.2 gather_fusion
  41.5 0.7 reshape.322
  42.4 2.0 broadcast_select_fusion
  44.4 4.8 %all-to-all-start.1 = ((bf16[64,2,4096]{2,1,0:T(2,128)(2,1)}), bf16[64,2,4096]{2,1,0:T(2,128)(2,1)S(1)}, u32[]{:S(2)}, u32[]{:S(2)}) async-start(bf16[64,2,4096]{2,1,0:T(2,128)(2,1)} %broadcast_select_fusion), calls=%async_computation.1 | async-start | bytes 2097152 | tf_op jit(solution)/shard_map/all_to_all | solution.py:61
  49.6 1.3 dynamic-slice
  51.6 32.4 %all-to-all-done.1 = bf16[64,2,4096]{2,1,0:T(2,128)(2,1)S(1)} async-done(((bf16[64,2,4096]{2,1,0:T(2,128)(2,1)}), bf16[64,2,4096]{2,1,0:T(2,128)(2,1)S(1)}, u32[]{:S(2)}, u32[]{:S(2)}) %all-to-all-start.1) | async-done | bytes 1048608 | tf_op jit(solution)/shard_map/all_to_all | solution.py:61
  84.0 0.4 reshape.317
  84.4 0.8 gather_fusion.1
  85.4 0.6 fusion.33
  86.1 62.7 %all-gather.6.cloned.1.call-done = bf16[1,512,4096]{2,1,0:T(8,128)(2,1)} async-done(((bf16[1,8,4096]{2,1,0:T(8,128)(2,1)}), bf16[1,512,4096]{2,1,0:T(8,128)(2,1)}) %all-gather.6.cloned.1.call-update) | async-done | bytes 4194320 | tf_op jit(solution)/shard_map/all_gather | solution.py:45
  148.8 3.5 fusion.64
  152.6 1.8 scatter_custom_fusion
  154.4 2.2 reshape.318
  156.6 8.9 %all-to-all-start.2 = ((f32[64,2,4096]{2,1,0:T(2,128)}), f32[64,2,4096]{2,1,0:T(2,128)}, u32[]{:S(2)}, u32[]{:S(2)}) async-start(f32[64,2,4096]{2,1,0:T(2,128)} %reshape.318), calls=%async_computation.2 | async-start | bytes 4194304 | tf_op jit(solution)/shard_map/all_to_all | solution.py:107
  165.5 0.5 broadcast.370
  166.0 0.7 reduce.3
  166.9 164.3 %all-reduce = f32[512]{0:T(512)S(1)} all-reduce(f32[512]{0:T(512)S(1)} %get-tuple-element.6), channel_id=1, replica_groups=mesh['rep'=8,'dp'=64] {'dp'}, use_global_device_ids=true, to_apply=%add | all-reduce | flops 512 | bytes 4096
  331.2 0.4 fusion.32
  331.6 3.0 multiply_reduce_fusion
  334.7 1.5 fusion.13
  336.2 110.3 %psum.7 = f32[4096]{0:T(1024)} all-reduce(f32[4096]{0:T(1024)S(1)} %get-tuple-element.4), channel_id=1, replica_groups=mesh['rep'=8,'dp'=64] {'rep','dp'}, use_global_device_ids=true, to_apply=%region_12.13 | all-reduce | flops 4096 | bytes 32768 | tf_op jit(solution)/shard_map/psum | solution.py:86
  446.5 5.9 %fusion.6 = f32[1,8,4096]{2,1,0:T(8,128)} fusion(bf16[512,4096]{1,0:T(8,128)(2,1)} %all-gather.4.cloned.1.call-done, bf16[1,8,4096]{2,1,0:T(8,128)(2,1)S(1)} %copy-done.3, bf16[8,4096]{1,0:T(8,128)(2,1)S(1)} %copy-done.2, f32[512]{0:T(512)S(1)} %all-reduce), kind=kOutput, calls=%fused_computation.16 | convolution fusion | flops 67219456 | bytes 4458496 | tf_op jit(solution)/shard_map/dot_general | solution.py:93
  452.4 3.1 fusion.15
  455.5 2.7 reshape.319
  458.2 1.5 fusion.4
  (58 shorter events, 2.9 us)
Async XLA Ops:
  7.2 33.1 %copy-start = (bf16[1,16,4096]{2,1,0:T(8,128)(2,1)S(1)}, bf16[1,16,4096]{2,1,0:T(8,128)(2,1)}, u32[]{:S(2)}) copy-start(bf16[1,16,4096]{2,1,0:T(8,128)(2,1)} %param.10) | copy-start | bytes 393220
  7.2 7.9 %copy-start.7 = (s32[1,8,7]{1,0,2:T(1,128)S(1)}, s32[1,8,7]{1,0,2:T(1,128)}, u32[]{:S(2)}) copy-start(s32[1,8,7]{1,0,2:T(1,128)} %param.11) | copy-start | bytes 676
  7.2 141.6 %all-gather.6.cloned.1.call-start = ((), (), s32[]{:S(2)}) async-start(), calls=%async_computation.4 | async-start | bytes 4259840 | tf_op jit(solution)/shard_map/all_gather | solution.py:45
  7.9 438.6 %all-gather.4.cloned.1.call-start = ((), (), s32[]{:S(2)}) async-start(), calls=%async_computation.3 | async-start | bytes 4259840 | tf_op jit(solution)/shard_map/all_gather | solution.py:88
  41.5 7.8 %copy-start.2 = (bf16[8,4096]{1,0:T(8,128)(2,1)S(1)}, bf16[8,4096]{1,0:T(8,128)(2,1)}, u32[]{:S(2)}) copy-start(bf16[8,4096]{1,0:T(8,128)(2,1)} %multiply_convert_fusion) | copy-start | bytes 196612
  44.4 39.6 %all-to-all-start.1 = ((bf16[64,2,4096]{2,1,0:T(2,128)(2,1)}), bf16[64,2,4096]{2,1,0:T(2,128)(2,1)S(1)}, u32[]{:S(2)}, u32[]{:S(2)}) async-start(bf16[64,2,4096]{2,1,0:T(2,128)(2,1)} %broadcast_select_fusion), calls=%async_computation.1 | async-start | bytes 2097152 | tf_op jit(solution)/shard_map/all_to_all | solution.py:61
  85.4 67.1 %copy-start.4 = (bf16[8,7,4096]{2,1,0:T(8,128)(2,1)}, bf16[8,7,4096]{2,1,0:T(8,128)(2,1)S(1)}, u32[]{:S(2)}) copy-start(bf16[8,7,4096]{2,1,0:T(8,128)(2,1)S(1)} %gather.12) | copy-start | bytes 1376260
  154.3 176.9 %copy-start.5 = (bf16[8,7,4096]{2,1,0:T(8,128)(2,1)S(1)}, bf16[8,7,4096]{2,1,0:T(8,128)(2,1)}, u32[]{:S(2)}) copy-start(bf16[8,7,4096]{2,1,0:T(8,128)(2,1)} %copy-done.4) | copy-start | bytes 1376260
  154.3 177.2 %copy-start.3 = (bf16[1,8,4096]{2,1,0:T(8,128)(2,1)S(1)}, bf16[1,8,4096]{2,1,0:T(8,128)(2,1)}, u32[]{:S(2)}) copy-start(bf16[1,8,4096]{2,1,0:T(8,128)(2,1)} %param.9) | copy-start | bytes 196612
  156.6 178.1 %copy-start.1 = (bf16[1,8,32,4096]{3,2,1,0:T(8,128)(2,1)S(1)}, bf16[1,8,32,4096]{3,2,1,0:T(8,128)(2,1)}, u32[]{:S(2)}) copy-start(bf16[1,8,32,4096]{3,2,1,0:T(8,128)(2,1)} %param.6) | copy-start | bytes 6291460
  156.6 178.1 %copy-start.6 = (f32[4096]{0:T(1024)S(1)}, f32[4096]{0:T(1024)}, u32[]{:S(2)}) copy-start(f32[4096]{0:T(1024)} %param.8) | copy-start | bytes 49156
  156.6 298.9 %all-to-all-start.2 = ((f32[64,2,4096]{2,1,0:T(2,128)}), f32[64,2,4096]{2,1,0:T(2,128)}, u32[]{:S(2)}, u32[]{:S(2)}) async-start(f32[64,2,4096]{2,1,0:T(2,128)} %reshape.318), calls=%async_computation.2 | async-start | bytes 4194304 | tf_op jit(solution)/shard_map/all_to_all | solution.py:107
Sparse Core Ops, SparseCore 0:
  10.2 138.5 all-gather.5
  151.5 150.7 all-gather.3
where the time goes:
time: 467 us
  blocking collectives  299 us (64%)
  waiting for transfers between devices  95.7 us (20%)
  other arithmetic  17.1 us (4%)
  between operations  15 us (3%)
  matrix products  14.8 us (3%)
  starting transfers between devices  13.7 us (3%)
  local copies, waits for them, and re-layouts  11.4 us (2%)
    unnamed x1, blocking collectives  164 us
    psum x1, blocking collectives, local(): gain_grad = lax.psum(gain_part, ('rep', 'dp'))  110 us
    all_gather x1, waiting for transfers between devices, local(): block_row_list = lax.all_gather(local_key_rows, 'dp', axis=0, tiled=True)  62.7 us
    all_to_all x1, waiting for transfers between devices, local(): lax.all_to_all(served, 'dp', split_axis=0, concat_axis=0, tiled=True)  32.4 us
    all_to_all x1, blocking collectives, local(): lax.all_to_all(request, 'dp', split_axis=0, concat_axis=0, tiled=True)  24.1 us
  transfers between devices with their start and end apart: 4, of which 2 were waited for; matrix products, arithmetic and copies ran while one was open for 8% of the time, Pallas kernels for 0%

commit v1 on v0

v1 whole, which is shorter than its diff:
```python
import jax
import jax.numpy as jnp
from jax import lax
from jax.sharding import PartitionSpec as P

TEMPERATURE = 0.02
QUERY_SCALE = 512.0
POOL_SCALE = 16.0


def embed(states, lengths, gain):
    square = jnp.mean(states * states, axis=-1, keepdims=True)
    normed = states * lax.rsqrt(square + 1e-05) * gain
    positions = jnp.arange(states.shape[1])
    token_mask = (positions[None, :] < lengths[:, None]).astype(jnp.float32)
    pooled = jnp.sum(normed * token_mask[:, :, None], axis=1) / lengths[:, None].astype(jnp.float32)
    return pooled * lax.rsqrt(jnp.sum(pooled * pooled, axis=-1, keepdims=True) + 1e-06)


def two_parts(x):
    high = x.astype(jnp.bfloat16)
    low = (x - high.astype(jnp.float32)).astype(jnp.bfloat16)
    return high, low


def to_slices(rows, owners):
    r, d = rows.shape
    return rows.reshape(r, owners, d // owners).transpose(1, 0, 2)


def from_slices(slices):
    owners, r, f = slices.shape
    return slices.transpose(1, 0, 2).reshape(r, owners * f)


def local(query_states, query_lengths, norm_gain, positives, mined_pool, hard_ids):
    owners = lax.axis_size("dp")
    me = lax.axis_index("dp")
    core = me % 2
    states32 = query_states[0].astype(jnp.float32)
    lengths = query_lengths[0]
    own_pos = positives[0]
    own_pool = mined_pool[0]
    ids = hard_ids[0]
    queries, hard = ids.shape
    q_all = queries * owners
    pool_all = own_pool.shape[0] * owners
    width = own_pos.shape[1]
    feats = width // owners

    unit, pullback = jax.vjp(lambda s, g: embed(s, lengths, g), states32, norm_gain)
    embedded, embedded_low = two_parts(unit)

    left = jnp.concatenate([embedded, own_pos], axis=0)
    id_parts = jnp.concatenate([ids // 32, ids % 32], axis=1).astype(jnp.bfloat16)
    id_rows = jnp.pad(id_parts, ((0, 0), (0, feats - 2 * hard)))
    out = jnp.concatenate(
        [
            jnp.concatenate([to_slices(left, owners), to_slices(own_pool, owners)], axis=2),
            jnp.concatenate(
                [
                    to_slices(embedded_low, owners),
                    jnp.broadcast_to(id_rows[None], (owners, queries, feats)),
                ],
                axis=2,
            ),
        ],
        axis=1,
    )
    got = lax.all_to_all(out, "dp", 0, 0, tiled=True)
    e_f = got[:, :queries, :feats].reshape(q_all, feats)
    p_f = got[:, queries : 2 * queries, :feats].reshape(q_all, feats)
    m_f = got[:, : 2 * queries, feats:].reshape(pool_all, feats)
    low_f = got[:, 2 * queries :, :feats].reshape(q_all, feats)
    id_got = got[:, 2 * queries :, feats:].reshape(q_all, feats).astype(jnp.int32)
    ids_all = id_got[:, :hard] * 32 + id_got[:, hard : 2 * hard]

    contract = (((1,), (1,)), ((), ()))
    sim = lax.dot_general(e_f, p_f, contract, preferred_element_type=jnp.float32)
    pool_sim = lax.dot_general(e_f, m_f, contract, preferred_element_type=jnp.float32)
    named = ids_all[:, :, None] == jnp.arange(pool_all)[None, None, :]
    hard_sim = jnp.sum(jnp.where(named, pool_sim[:, None, :], 0.0), axis=2)
    part = jnp.concatenate([sim, jnp.pad(hard_sim, ((0, 0), (0, 128 - hard)))], axis=1)
    part = part.reshape(owners // 2, 2, queries, q_all + 128)
    mine = lax.dynamic_index_in_dim(part, core, 1, keepdims=False)
    theirs = lax.dynamic_index_in_dim(part, 1 - core, 1, keepdims=False)
    theirs = lax.ppermute(theirs, "dp", [(i, i ^ 1) for i in range(owners)])
    same_core = [[2 * i + c for i in range(owners // 2)] for c in range(2)]
    pieces = lax.all_to_all(mine + theirs, "dp", 0, 0, tiled=True, axis_index_groups=same_core)
    scores = jnp.sum(pieces, axis=0) / TEMPERATURE

    column = jnp.arange(q_all + 128)
    exps = jnp.where(column[None, :] < q_all + hard, jnp.exp(scores), 0.0)
    soft = exps / jnp.sum(exps, axis=1, keepdims=True)
    own = column[None, :] == (me * queries + jnp.arange(queries))[:, None]
    along = jnp.sum(soft * scores - jnp.where(own, scores, 0.0), axis=1, keepdims=True)
    soft_high, soft_low = two_parts(soft)
    along_high, along_low = two_parts(along)
    tail = jnp.concatenate(
        [soft_high[:, q_all : q_all + hard], soft_low[:, q_all : q_all + hard], along_high, along_low],
        axis=1,
    )
    sent = jnp.concatenate(
        [soft_high[:, :q_all], jnp.pad(tail, ((0, 0), (0, 128 - 2 * hard - 2)))], axis=1
    )
    weights = lax.all_to_all(
        jnp.broadcast_to(sent[None], (owners, queries, q_all + 128)), "dp", 0, 0, tiled=True
    ).reshape(q_all, q_all + 128)
    w_pos = weights[:, :q_all]
    tails = weights[:, q_all:].astype(jnp.float32)
    w_hard = tails[:, :hard] + tails[:, hard : 2 * hard]
    along_all = tails[:, 2 * hard : 2 * hard + 1] + tails[:, 2 * hard + 1 : 2 * hard + 2]
    spread = jnp.sum(jnp.where(named, w_hard[:, :, None], 0.0), axis=1)
    spread_high, spread_low = two_parts(spread)

    e32 = e_f.astype(jnp.float32)
    numerator = jnp.dot(w_pos, p_f, preferred_element_type=jnp.float32) + jnp.dot(
        spread_high, m_f, preferred_element_type=jnp.float32
    )
    emb_grad = (numerator - p_f.astype(jnp.float32)) / TEMPERATURE
    by_column = (((0,), (0,)), ((), ()))
    key_grad = (
        lax.dot_general(w_pos, e_f, by_column, preferred_element_type=jnp.float32) - e32
    ) / TEMPERATURE
    pool_grad = (POOL_SCALE / TEMPERATURE) * (
        lax.dot_general(spread_high, e_f, by_column, preferred_element_type=jnp.float32)
        + lax.dot_general(spread_low, e_f, by_column, preferred_element_type=jnp.float32)
    )
    unit_f = e32 + low_f.astype(jnp.float32)
    gain_part = jnp.sum((emb_grad - along_all * unit_f) * unit_f, axis=0)
    gain_part = gain_part / lax.dynamic_slice_in_dim(norm_gain, me * feats, feats, 0)
    gain_row = jnp.concatenate(two_parts(gain_part), axis=0)
    back = jnp.concatenate(
        [
            jnp.concatenate(
                [
                    emb_grad.reshape(owners, queries, feats),
                    key_grad.reshape(owners, queries, feats),
                ],
                axis=1,
            ),
            pool_grad.reshape(owners, 2 * queries, feats),
        ],
        axis=2,
    ).astype(jnp.bfloat16)
    back = jnp.concatenate(
        [back, jnp.broadcast_to(gain_row[None, None], (owners, 8, 2 * feats))], axis=1
    )
    home = lax.all_to_all(back, "dp", 0, 0, tiled=True)
    emb_home = from_slices(home[:, :queries, :feats]).astype(jnp.float32)
    key_home = from_slices(home[:, queries : 2 * queries, :feats]).astype(jnp.float32)
    pool_home = from_slices(home[:, : 2 * queries, feats:]).astype(jnp.float32)
    gain_home = home[:, 2 * queries, :].astype(jnp.float32)
    gain_group = (gain_home[:, :feats] + gain_home[:, feats:]).reshape(width // 128, 128)
    groups = lax.axis_size("rep")
    gain_groups = lax.all_to_all(
        jnp.broadcast_to(gain_group[None], (groups, width // 128, 128)), "rep", 0, 0, tiled=True
    )
    gain_grad = jnp.sum(gain_groups, axis=0).reshape(width)
    states_grad, _ = pullback(emb_home)
    query_grad = (QUERY_SCALE * states_grad).astype(jnp.bfloat16)
    return query_grad[None], key_home[None], pool_home[None], gain_grad


def solution(mesh):
    placed = (
        P("rep", "dp", None, None),
        P("rep", "dp"),
        P(),
        P("rep", "dp", None),
        P("rep", "dp", None),
        P("rep", "dp", None),
    )
    return jax.shard_map(
        local,
        mesh=mesh,
        in_specs=placed,
        out_specs=(P("rep", "dp", None, None), P("rep", "dp", None), P("rep", "dp", None), P()),
        check_vma=False,
    )
```

time: 467 us -> 180 us (0.39)
  blocking collectives: 299 us -> 20.5 us
  waiting for transfers between devices: 95.7 us -> 59 us
  starting transfers between devices: 13.7 us -> 37.8 us
  other arithmetic: 17.1 us -> 32.5 us
  between operations: 15 us -> 1.06 us
  local copies, waits for them, and re-layouts: 11.4 us -> 22.3 us
  matrix products: 14.8 us -> 5.33 us
    unnamed x1 -> x0, blocking collectives: 164 us -> none
    psum x1 -> x0, blocking collectives: 110 us -> none  [local(): gain_grad = lax.psum(gain_part, ('rep', 'dp'))]
    all_gather x2 -> x0, waiting for transfers between devices: 62.7 us -> none  [the longest x1 62.7 us: local(): block_row_list = lax.all_gather(local_key_rows, 'dp', axis=0, tiled=True)]
    all_to_all x2 -> x4, waiting for transfers between devices: 32.4 us -> 57 us  [the longest x1 18.2 us: local(): lax.all_to_all(mine + theirs, 'dp', 0, 0, tiled=True, axis_index_groups=s...]
    all_to_all x2 -> x4, starting transfers between devices: 13.6 us -> 35.7 us  [the longest x1 14.6 us: local(): got = lax.all_to_all(out, 'dp', 0, 0, tiled=True)]
    dot_general x6 -> x7, matrix products: 14.8 us -> 5.33 us  [the longest x1 1.76 us: local(): lax.dot_general(w_pos, e_f, by_column, preferred_element_type=jnp.float32)]
    reduce_sum x3 -> x6, other arithmetic: 0.41 us -> 8.32 us  [the longest x1 3.08 us: local(): spread = jnp.sum(jnp.where(named, w_hard[:, :, None], 0.0), axis=1)]
  transfers between devices with their start and end apart: 4 -> 5, of which waited for: 2 -> 5; matrix products, arithmetic and copies ran while one was open for 8% -> 4% of each run, Pallas kernels for 0% -> 0%
where the time goes in v1:
time: 180 us; the launch traced here: 178 us
  waiting for transfers between devices  59 us (33%)
  starting transfers between devices  37.8 us (21%)
  other arithmetic  32.5 us (18%)
  local copies, waits for them, and re-layouts  22.3 us (12%)
  blocking collectives  20.5 us (11%)
  matrix products  5.33 us (3%)
    all_to_all x1, blocking collectives, local(): home = lax.all_to_all(back, 'dp', 0, 0, tiled=True)  20.5 us
    all_to_all x1, waiting for transfers between devices, local(): lax.all_to_all(mine + theirs, 'dp', 0, 0, tiled=True, axis_index_groups=s...  18.2 us
    all_to_all x1, waiting for transfers between devices, local(): lax.all_to_all(jnp.broadcast_to(sent[None], (owners, queries, q_all + 128...  15.6 us
    all_to_all x1, waiting for transfers between devices, local(): got = lax.all_to_all(out, 'dp', 0, 0, tiled=True)  15 us
    all_to_all x1, starting transfers between devices, local(): got = lax.all_to_all(out, 'dp', 0, 0, tiled=True)  14.6 us
    all_to_all x1, starting transfers between devices, local(): lax.all_to_all(jnp.broadcast_to(gain_group[None], (groups, width // 128,...  9.76 us
    all_to_all x1, waiting for transfers between devices, local(): lax.all_to_all(jnp.broadcast_to(gain_group[None], (groups, width // 128,...  8.24 us
    all_to_all x1, starting transfers between devices, local(): lax.all_to_all(jnp.broadcast_to(sent[None], (owners, queries, q_all + 128...  6.71 us
  transfers between devices with their start and end apart: 5, of which 5 were waited for; matrix products, arithmetic and copies ran while one was open for 4% of the time, Pallas kernels for 0%

profile of v1, /device:TPU:1, one launch (start us, length us, event | category | flops | bytes accessed | tf_op | source)
XLA Modules:
  0.0 178.5 jit_solution(7357879220585510078)
XLA Ops:
  2.2 2.1 %fusion.3 = f32[8,32]{1,0:T(8,128)S(1)} fusion(bf16[1,8,32,4096]{3,2,1,0:T(8,128)(2,1)} %param.6), kind=kLoop, calls=%fused_computation.9 | loop fusion | flops 3145472 | bytes 2098176 | tf_op jit(solution)/shard_map/jvp()/reduce_sum | solution.py:12
  5.5 1.0 fusion.6
  8.0 1.0 copy.100
  9.0 14.6 %all-to-all-start = ((bf16[64,24,128]{2,1,0:T(8,128)(2,1)}), bf16[64,24,128]{2,1,0:T(8,128)(2,1)S(1)}, u32[]{:S(2)}, u32[]{:S(2)}) async-start(bf16[64,24,128]{2,1,0:T(8,128)(2,1)} %copy.100), calls=%async_computation | async-start | bytes 786432 | tf_op jit(solution)/shard_map/all_to_all | solution.py:70
  23.6 15.0 %all-to-all-done = bf16[64,24,128]{2,1,0:T(8,128)(2,1)S(1)} async-done(((bf16[64,24,128]{2,1,0:T(8,128)(2,1)}), bf16[64,24,128]{2,1,0:T(8,128)(2,1)S(1)}, u32[]{:S(2)}, u32[]{:S(2)}) %all-to-all-start) | async-done | bytes 393248 | tf_op jit(solution)/shard_map/all_to_all | solution.py:70
  40.5 2.4 %select_reduce_fusion.1 = f32[512,7]{0,1:T(8,128)S(1)} fusion(f32[512,1024]{1,0:T(8,128)S(1)} %fusion.52, s32[512,7]{0,1:T(8,128)S(1)} %multiply_add_fusion), kind=kLoop, calls=%fused_computation.1 | loop fusion | flops 11006464 | bytes 2125824 | tf_op jit(solution)/shard_map/reduce_sum | solution.py:82
  43.2 1.2 select_maximum_fusion
  44.4 2.8 %copy.103 = f32[512,640]{1,0:T(8,128)} copy(f32[512,640]{0,1:T(8,128)} %select_maximum_fusion) | data formatting | bytes 2621440 | tf_op jit(solution)/shard_map/concatenate | solution.py:83
  47.2 2.0 %dynamic-slice_bitcast_fusion = f32[32,8,640]{2,1,0:T(8,128)} fusion(f32[32,2,8,640]{3,2,1,0:T(8,128)} %bitcast.107, s32[]{:T(128)S(6)} %select_n.49), kind=kLoop, calls=%fused_computation.29 | loop fusion | bytes 1310724 | tf_op jit(solution)/shard_map/jit(dynamic_index_in_dim)/squeeze | solution.py:86
  49.2 2.2 %collective-permute-start = (f32[32,8,640]{2,1,0:T(8,128)}, f32[32,8,640]{2,1,0:T(8,128)S(1)}, u32[]{:S(2)}, u32[]{:S(2)}) collective-permute-start(f32[32,8,640]{2,1,0:T(8,128)} %dynamic-slice_bitcast_fusion), channel_id=1, source_target_pairs={{0,1},{1,0},{2,3},{3,2},{4,5},{5,4},{6,7},{7,6},{8,9},{9,8},{10,11... | collective-permute-start | bytes 1966088 | tf_op jit(solution)/shard_map/ppermute | solution.py:87
  51.3 2.0 %collective-permute-done = f32[32,8,640]{2,1,0:T(8,128)S(1)} collective-permute-done((f32[32,8,640]{2,1,0:T(8,128)}, f32[32,8,640]{2,1,0:T(8,128)S(1)}, u32[]{:S(2)}, u32[]{:S(2)}) %collective-permute-start) | collective-permute-done | bytes 655392 | tf_op jit(solution)/shard_map/ppermute | solution.py:87
  53.4 2.0 %bitcast_add_fusion = f32[32,8,640]{2,1,0:T(8,128)} fusion(f32[32,8,640]{2,1,0:T(8,128)S(1)} %collective-permute-done, f32[32,2,8,640]{3,2,1,0:T(8,128)} %bitcast.108, s32[]{:T(128)S(6)} %select_n.48), kind=kLoop, calls=%fused_computation.28 | loop fusion | flops 163840 | bytes 1966084 | tf_op jit(solution)/shard_map/add | solution.py:89
  55.3 4.6 %all-to-all-start.1 = ((f32[32,8,640]{2,1,0:T(8,128)}), f32[32,8,640]{2,1,0:T(8,128)S(1)}, u32[]{:S(2)}, u32[]{:S(2)}) async-start(f32[32,8,640]{2,1,0:T(8,128)} %bitcast_add_fusion), calls=%async_computation.1 | async-start | bytes 1310720 | tf_op jit(solution)/shard_map/all_to_all | solution.py:89
  61.1 18.2 %all-to-all-done.1 = f32[32,8,640]{2,1,0:T(8,128)S(1)} async-done(((f32[32,8,640]{2,1,0:T(8,128)}), f32[32,8,640]{2,1,0:T(8,128)S(1)}, u32[]{:S(2)}, u32[]{:S(2)}) %all-to-all-start.1) | async-done | bytes 655392 | tf_op jit(solution)/shard_map/all_to_all | solution.py:89
  83.0 6.7 %all-to-all-start.2 = ((bf16[64,8,640]{2,1,0:T(8,128)(2,1)}), bf16[64,8,640]{2,1,0:T(8,128)(2,1)S(1)}, u32[]{:S(2)}, u32[]{:S(2)}) async-start(bf16[64,8,640]{2,1,0:T(8,128)(2,1)} %broadcast_in_dim.59), calls=%async_computation.2 | async-start | bytes 1310720 | tf_op jit(solution)/shard_map/all_to_all | solution.py:106
  89.7 1.7 copy.112
  91.4 1.6 copy.109
  93.0 1.6 copy.107
  94.6 15.6 %all-to-all-done.2 = bf16[64,8,640]{2,1,0:T(8,128)(2,1)S(1)} async-done(((bf16[64,8,640]{2,1,0:T(8,128)(2,1)}), bf16[64,8,640]{2,1,0:T(8,128)(2,1)S(1)}, u32[]{:S(2)}, u32[]{:S(2)}) %all-to-all-start.2) | async-done | bytes 655392 | tf_op jit(solution)/shard_map/all_to_all | solution.py:106
  111.9 1.7 copy.106
  113.6 3.1 %select_reduce_fusion = f32[512,1024]{1,0:T(8,128)S(1)} fusion(f32[512,7]{0,1:T(8,128)} %copy.106, s32[512,7]{0,1:T(8,128)} %copy-done.7), kind=kLoop, calls=%fused_computation | loop fusion | flops 10485760 | bytes 2125824 | tf_op jit(solution)/shard_map/reduce_sum | solution.py:113
  117.2 1.0 fusion.55
  119.8 1.0 fusion.11
  120.8 1.7 copy.111
  122.5 1.8 fusion.15
  125.2 1.0 copy.108
  127.0 1.1 pad_maximum_fusion
  128.1 20.5 %all_to_all.25 = bf16[64,24,128]{2,1,0:T(8,128)(2,1)S(1)} all-to-all(bf16[64,24,128]{2,1,0:T(8,128)(2,1)S(1)} %pad_maximum_fusion), channel_id=1, replica_groups=mesh['rep'=8,'dp'=64] {'dp'}, dimensions={0} | all-to-all | bytes 786432 | tf_op jit(solution)/shard_map/all_to_all | solution.py:149
  151.0 1.5 fusion.7
  153.2 3.8 %fusion.9 = bf16[1,8,32,4096]{3,2,1,0:T(8,128)(2,1)} fusion(bf16[1,8,32,4096]{3,2,1,0:T(8,128)(2,1)S(1)} %copy-done, f32[8,32]{1,0:T(8,128)S(1)} %multiply_multiply_fusion, f32[8,32]{1,0:T(8,128)} %copy-done.11, f32[4096]{0:T(1024)S(1)} %copy-done.6, f32[8,32]{1,0:T(8,128)} %copy-done.9, f32[8,4096]{1,0:T(8,128)S(1)} %fusion.19), kind=kLoop, calls=%fused_computation.15 | loop fusion | flops 9437184 | bytes 4344832 | tf_op jit(solution)/shard_map/convert_element_type | solution.py:161
  158.6 9.8 %all-to-all-start.4 = ((f32[8,32,128]{2,1,0:T(8,128)}), f32[8,32,128]{2,1,0:T(8,128)S(1)}, u32[]{:S(2)}, u32[]{:S(2)}) async-start(f32[8,32,128]{2,1,0:T(8,128)} %broadcast_in_dim.102), calls=%async_computation.4 | async-start | bytes 262144 | tf_op jit(solution)/shard_map/all_to_all | solution.py:156
  169.6 8.2 %all-to-all-done.4 = f32[8,32,128]{2,1,0:T(8,128)S(1)} async-done(((f32[8,32,128]{2,1,0:T(8,128)}), f32[8,32,128]{2,1,0:T(8,128)S(1)}, u32[]{:S(2)}, u32[]{:S(2)}) %all-to-all-start.4) | async-done | bytes 131104 | tf_op jit(solution)/shard_map/all_to_all | solution.py:156
  (104 shorter events, 23.0 us)
Async XLA Ops:
  0.6 4.9 %copy-start = (bf16[1,8,32,4096]{3,2,1,0:T(8,128)(2,1)S(1)}, bf16[1,8,32,4096]{3,2,1,0:T(8,128)(2,1)}, u32[]{:S(2)}) copy-start(bf16[1,8,32,4096]{3,2,1,0:T(8,128)(2,1)} %param.6) | copy-start | bytes 6291460
  0.6 4.8 %copy-start.6 = (f32[4096]{0:T(1024)S(1)}, f32[4096]{0:T(1024)}, u32[]{:S(2)}) copy-start(f32[4096]{0:T(1024)} %param.8) | copy-start | bytes 49156
  1.5 6.0 %copy-start.14 = (f32[8]{0:T(128)}, f32[8]{0:T(128)S(1)}, u32[]{:S(2)}) copy-start(f32[8]{0:T(128)S(1)} %bitcast_convert_fusion.1) | copy-start | bytes 100
  2.2 2.1 %copy-start.9 = (f32[8,32]{1,0:T(8,128)}, f32[8,32]{1,0:T(8,128)S(1)}, u32[]{:S(2)}) copy-start(f32[8,32]{1,0:T(8,128)S(1)} %fusion.36) | copy-start | bytes 3076
  2.2 4.7 %copy-start.8 = (bf16[1,16,4096]{2,1,0:T(8,128)(2,1)S(1)}, bf16[1,16,4096]{2,1,0:T(8,128)(2,1)}, u32[]{:S(2)}) copy-start(bf16[1,16,4096]{2,1,0:T(8,128)(2,1)} %param.10) | copy-start | bytes 393220
  4.3 0.6 copy-start.12
  4.3 2.8 %copy-start.10 = (bf16[1,8,4096]{2,1,0:T(8,128)(2,1)S(1)}, bf16[1,8,4096]{2,1,0:T(8,128)(2,1)}, u32[]{:S(2)}) copy-start(bf16[1,8,4096]{2,1,0:T(8,128)(2,1)} %param.9) | copy-start | bytes 196612
  4.3 3.0 %copy-start.16 = (s32[1,8,7]{1,0,2:T(1,128)S(1)}, s32[1,8,7]{1,0,2:T(1,128)}, u32[]{:S(2)}) copy-start(s32[1,8,7]{1,0,2:T(1,128)} %param.11) | copy-start | bytes 676
  4.9 0.6 copy-start.11
  6.6 2.4 %copy-start.1 = (f32[8,64,64]{2,1,0:T(8,128)}, f32[8,64,64]{2,1,0:T(8,128)S(1)}, u32[]{:S(2)}) copy-start(f32[8,64,64]{2,1,0:T(8,128)S(1)} %reduce_sum.122) | copy-start | bytes 393220
  6.9 2.2 %copy-start.18 = (f32[8]{0:T(128)}, f32[8]{0:T(128)S(1)}, u32[]{:S(2)}) copy-start(f32[8]{0:T(128)S(1)} %multiply_reduce_fusion.2) | copy-start | bytes 100
  6.9 2.1 %copy-start.17 = (f32[8]{0:T(128)}, f32[8]{0:T(128)S(1)}, u32[]{:S(2)}) copy-start(f32[8]{0:T(128)S(1)} %add_rsqrt_fusion) | copy-start | bytes 100
  9.0 29.7 %all-to-all-start = ((bf16[64,24,128]{2,1,0:T(8,128)(2,1)}), bf16[64,24,128]{2,1,0:T(8,128)(2,1)S(1)}, u32[]{:S(2)}, u32[]{:S(2)}) async-start(bf16[64,24,128]{2,1,0:T(8,128)(2,1)} %copy.100), calls=%async_computation | async-start | bytes 786432 | tf_op jit(solution)/shard_map/all_to_all | solution.py:70
  39.9 3.0 %copy-start.7 = (s32[512,7]{0,1:T(8,128)}, s32[512,7]{0,1:T(8,128)S(1)}, u32[]{:S(2)}) copy-start(s32[512,7]{0,1:T(8,128)S(1)} %multiply_add_fusion) | copy-start | bytes 43012
  49.2 4.2 %collective-permute-start = (f32[32,8,640]{2,1,0:T(8,128)}, f32[32,8,640]{2,1,0:T(8,128)S(1)}, u32[]{:S(2)}, u32[]{:S(2)}) collective-permute-start(f32[32,8,640]{2,1,0:T(8,128)} %dynamic-slice_bitcast_fusion), channel_id=1, source_target_pairs={{0,1},{1,0},{2,3},{3,2},{4,5},{5,4},{6,7},{7,6},{8,9},{9,8},{10,11... | collective-permute-start | bytes 1966088 | tf_op jit(solution)/shard_map/ppermute | solution.py:87
  55.3 23.9 %all-to-all-start.1 = ((f32[32,8,640]{2,1,0:T(8,128)}), f32[32,8,640]{2,1,0:T(8,128)S(1)}, u32[]{:S(2)}, u32[]{:S(2)}) async-start(f32[32,8,640]{2,1,0:T(8,128)} %bitcast_add_fusion), calls=%async_computation.1 | async-start | bytes 1310720 | tf_op jit(solution)/shard_map/all_to_all | solution.py:89
  83.0 27.2 %all-to-all-start.2 = ((bf16[64,8,640]{2,1,0:T(8,128)(2,1)}), bf16[64,8,640]{2,1,0:T(8,128)(2,1)S(1)}, u32[]{:S(2)}, u32[]{:S(2)}) async-start(bf16[64,8,640]{2,1,0:T(8,128)(2,1)} %broadcast_in_dim.59), calls=%async_computation.2 | async-start | bytes 1310720 | tf_op jit(solution)/shard_map/all_to_all | solution.py:106
  113.6 3.6 %copy-start.3 = (f32[512,64]{0,1:T(8,128)S(1)}, f32[512,64]{0,1:T(8,128)}, u32[]{:S(2)}) copy-start(f32[512,64]{0,1:T(8,128)} %copy.112) | copy-start | bytes 393220
  113.6 3.6 %copy-start.4 = (bf16[512,64]{0,1:T(8,128)(2,1)S(1)}, bf16[512,64]{0,1:T(8,128)(2,1)}, u32[]{:S(2)}) copy-start(bf16[512,64]{0,1:T(8,128)(2,1)} %copy.109) | copy-start | bytes 196612
  113.6 3.6 %copy-start.5 = (bf16[512,64]{0,1:T(8,128)(2,1)S(1)}, bf16[512,64]{0,1:T(8,128)(2,1)}, u32[]{:S(2)}) copy-start(bf16[512,64]{0,1:T(8,128)(2,1)} %copy.107) | copy-start | bytes 196612
  113.6 3.6 %copy-start.13 = (f32[512]{0:T(512)S(1)}, f32[512]{0:T(512)}, u32[]{:S(2)}) copy-start(f32[512]{0:T(512)} %fusion.18) | copy-start | bytes 6148
  122.5 26.1 %copy-start.2 = (f32[8,64,64]{2,1,0:T(8,128)S(1)}, f32[8,64,64]{2,1,0:T(8,128)}, u32[]{:S(2)}) copy-start(f32[8,64,64]{2,1,0:T(8,128)} %copy-done.1) | copy-start | bytes 393220
  124.3 24.4 %copy-start.15 = (f32[8]{0:T(128)S(1)}, f32[8]{0:T(128)}, u32[]{:S(2)}) copy-start(f32[8]{0:T(128)} %copy-done.14) | copy-start | bytes 100
  158.6 19.2 %all-to-all-start.4 = ((f32[8,32,128]{2,1,0:T(8,128)}), f32[8,32,128]{2,1,0:T(8,128)S(1)}, u32[]{:S(2)}, u32[]{:S(2)}) async-start(f32[8,32,128]{2,1,0:T(8,128)} %broadcast_in_dim.102), calls=%async_computation.4 | async-start | bytes 262144 | tf_op jit(solution)/shard_map/all_to_all | solution.py:156

commit v2 on v0

v2 whole, which is shorter than its diff:
```python
import jax
import jax.numpy as jnp
from jax import lax
from jax.experimental import pallas as pl
from jax.experimental.pallas import tpu as pltpu
from jax.sharding import PartitionSpec as P

TEMPERATURE = 0.02
QUERY_SCALE = 512.0
POOL_SCALE = 16.0
LANES = 128
HALF = 64
F32 = jnp.float32
BF16 = jnp.bfloat16
BY_COLUMN = (((0,), (0,)), ((), ()))
BY_ROW = (((1,), (1,)), ((), ()))


def swap(x):
    return pltpu.roll(x, HALF, 1)


def left_half(rows):
    return lax.broadcasted_iota(jnp.int32, (rows, LANES), 1) < HALF


def embed_kernel(len_ref, x_ref, gain_ref, pos_ref, pool_ref, ids_ref, out_ref, unit_ref, inv_ref, norm_ref, weight_ref):
    queries, width = unit_ref.shape
    tokens = x_ref.shape[0] // queries
    chunks = width // LANES
    token = lax.broadcasted_iota(jnp.int32, (tokens, 1), 0)

    def one_query(i, carry):
        rows = pl.ds(pl.multiple_of(i * tokens, tokens), tokens)
        square = jnp.zeros((tokens, LANES), F32)
        for k in range(chunks):
            v = x_ref[rows, k * LANES : (k + 1) * LANES].astype(F32)
            square += v * v
        inv = lax.rsqrt(jnp.sum(square, axis=1, keepdims=True) / width + 1e-05)
        inv_ref[rows, :] = jnp.broadcast_to(inv, (tokens, LANES))
        length = len_ref[i]
        weight = jnp.where(token < length, inv, 0.0) / length.astype(F32)
        weight_ref[rows, :] = jnp.broadcast_to(weight, (tokens, LANES))
        return carry

    lax.fori_loop(0, queries, one_query, 0)
    for k in range(chunks):
        cols = slice(k * LANES, (k + 1) * LANES)
        v = x_ref[:, cols].astype(F32) * weight_ref[...]
        v = jnp.sum(v.reshape(queries, tokens, LANES), axis=1)
        unit_ref[:, cols] = v * gain_ref[:, cols]
    pooled = unit_ref[...]
    norm = lax.rsqrt(jnp.sum(pooled * pooled, axis=1, keepdims=True) + 1e-06)
    norm_ref[...] = jnp.broadcast_to(norm, norm_ref.shape)
    ids = ids_ref[...]
    lane = lax.broadcasted_iota(jnp.int32, (queries, LANES), 1)
    id_rows = jnp.zeros((queries, LANES), jnp.int32)
    hard = ids.shape[1]
    for m in range(hard):
        one = ids[:, m : m + 1]
        id_rows = jnp.where(lane == m, one >> 5, id_rows)
        id_rows = jnp.where(lane == hard + m, one & 31, id_rows)
    id_rows = id_rows.astype(F32)
    left8, left16 = left_half(queries), left_half(2 * queries)
    for k in range(chunks):
        cols = slice(k * LANES, (k + 1) * LANES)
        unit = unit_ref[:, cols] * norm
        unit_ref[:, cols] = unit
        high = unit.astype(BF16).astype(F32)
        low = unit - high
        upper = jnp.concatenate([high, pos_ref[:, cols].astype(F32)], axis=0)
        pool = pool_ref[:, cols].astype(F32)
        even = jnp.concatenate(
            [jnp.where(left16, upper, swap(pool)), jnp.where(left8, id_rows, swap(low))], axis=0
        )
        odd = jnp.concatenate(
            [jnp.where(left16, swap(upper), pool), jnp.where(left8, id_rows, low)], axis=0
        )
        out_ref[2 * k] = even.astype(BF16)
        out_ref[2 * k + 1] = odd.astype(BF16)


def similar_kernel(
    hard, core_ref, got_ref, gotx_ref, sim_ref, e_ref, unit_ref, own_ref, p_ref, m_ref, ids_ref
):
    core = core_ref[0]
    chips, _, rows, _ = got_ref.shape
    q = rows // 3
    half = chips * q

    def parts(block):
        n = block.shape[0]
        block = block.astype(F32)
        return (
            block[:, :q].reshape(n * q, LANES),
            block[:, q : 2 * q].reshape(n * q, LANES),
            block[:, 2 * q :].reshape(n * q, LANES),
        )

    left = left_half(half)
    ea, pa, ta = parts(got_ref[:, core])
    eb, pb, tb = parts(gotx_ref[:, core])
    e = jnp.where(left, ea, swap(eb))
    e_ref[...] = e.astype(BF16)
    unit_ref[...] = e + jnp.where(left, swap(ta), tb)
    own_ref[...] = jnp.where(left, pa, swap(pb))
    lane = lax.broadcasted_iota(jnp.int32, (half, LANES), 1)
    ids = ta * 32.0 + pltpu.roll(ta, LANES - hard, 1)
    ids = jnp.where(lane < hard, ids, 0.0).astype(jnp.int32)
    ids_ref[...] = ids
    a = got_ref[...].reshape(2 * chips, rows, LANES).astype(F32)
    b = gotx_ref[...].reshape(2 * chips, rows, LANES).astype(F32)
    n = 2 * chips * q
    p = jnp.where(
        left_half(n), a[:, q : 2 * q].reshape(n, LANES), swap(b[:, q : 2 * q].reshape(n, LANES))
    ).astype(BF16)
    m = jnp.where(
        left_half(2 * n),
        swap(a[:, : 2 * q].reshape(2 * n, LANES)),
        b[:, : 2 * q].reshape(2 * n, LANES),
    ).astype(BF16)
    p_ref[...] = p
    m_ref[...] = m
    eh = e.astype(BF16)
    sim_ref[:, :, :n] = lax.dot_general(eh, p, BY_ROW, preferred_element_type=F32).reshape(chips, q, n)
    pool = lax.dot_general(eh, m, BY_ROW, preferred_element_type=F32)
    tail = jnp.zeros((half, LANES), F32)
    within, tile = ids & (LANES - 1), ids >> 7
    for k in range(2 * n // LANES):
        picked = jnp.take_along_axis(
            pool[:, k * LANES : (k + 1) * LANES], within, axis=1, mode="promise_in_bounds"
        )
        tail = jnp.where(tile == k, picked, tail)
    tail = jnp.where(lane < hard, tail, 0.0)
    sim_ref[:, :, n:] = tail.reshape(chips, q, LANES)


def softmax_kernel(hard, me_ref, in_ref, out_ref):
    copies, q, width = out_ref.shape
    n = width - LANES
    scores = jnp.sum(in_ref[...], axis=0) / TEMPERATURE
    column = lax.broadcasted_iota(jnp.int32, (q, width), 1)
    row = lax.broadcasted_iota(jnp.int32, (q, width), 0)
    exps = jnp.where(column < n + hard, jnp.exp(scores), 0.0)
    soft = exps / jnp.sum(exps, axis=1, keepdims=True)
    own = column == row + me_ref[0] * q
    along = jnp.sum(soft * scores - jnp.where(own, scores, 0.0), axis=1, keepdims=True)
    high = along.astype(BF16).astype(F32)
    sent = jnp.where(column == n + hard, high, soft)
    sent = jnp.where(column == n + hard + 1, along - high, sent)
    sent = sent.astype(BF16)
    for k in range(copies):
        out_ref[k] = sent


def slices_kernel(
    hard, me_ref, w_ref, e_ref, unit_ref, own_ref, p_ref, m_ref, ids_ref, gain_ref, out_ref
):
    me = me_ref[0]
    core, chip = lax.rem(me, 2), lax.div(me, 2)
    chips, q, width = w_ref.shape
    n = width - LANES
    half = chips * q
    w = w_ref[...].astype(F32).reshape(half, width)
    tail = w[:, n:]
    w_pos = w[:, :n].astype(BF16)
    ids = ids_ref[...]
    column = lax.broadcasted_iota(jnp.int32, (half, 2 * n), 1)
    spread = jnp.zeros((half, 2 * n), F32)
    for m in range(hard):
        spread += jnp.where(column == ids[:, m : m + 1], tail[:, m : m + 1], 0.0)
    spread = spread.astype(BF16)
    along = tail[:, hard : hard + 1] + tail[:, hard + 1 : hard + 2]
    e = e_ref[...]
    unit = unit_ref[...]
    numerator = jnp.dot(w_pos, p_ref[...], preferred_element_type=F32)
    numerator += jnp.dot(spread, m_ref[...], preferred_element_type=F32)
    emb_grad = (numerator - own_ref[...]) / TEMPERATURE - along * unit
    key = lax.dot_general(w_pos, e, BY_COLUMN, preferred_element_type=F32)
    pool = lax.dot_general(spread, e, BY_COLUMN, preferred_element_type=F32)
    pool = pool * (POOL_SCALE / TEMPERATURE)
    gain = gain_ref[pl.ds(chip, 1), :]
    gain = jnp.where(core == 0, gain, swap(gain))
    gain_part = jnp.sum(emb_grad * unit, axis=0, keepdims=True) / gain
    gain_high = gain_part.astype(BF16).astype(F32)
    row = lax.broadcasted_iota(jnp.int32, (q, LANES), 0)
    gain_rows = jnp.where(row == 0, gain_high, jnp.where(row == 1, gain_part - gain_high, 0.0))
    e32 = e.astype(F32)
    for d in range(2 * chips):
        k, c = d // 2, d % 2
        rows = slice(k * q, (k + 1) * q)
        mine = core == c
        block = jnp.concatenate(
            [
                jnp.where(mine, emb_grad[rows], 0.0),
                (key[d * q : (d + 1) * q] - jnp.where(mine, e32[rows], 0.0)) / TEMPERATURE,
                pool[2 * d * q : 2 * (d + 1) * q],
                gain_rows,
            ],
            axis=0,
        )
        out_ref[d] = block.astype(BF16)


def gain_kernel(in_ref, out_ref):
    copies, chips, _ = out_ref.shape
    q = in_ref.shape[1] // 5
    for k in range(chips):
        a = in_ref[2 * k].astype(F32)[4 * q : 5 * q]
        b = in_ref[2 * k + 1].astype(F32)[4 * q : 5 * q]
        both = jnp.sum(a + swap(b), axis=0, keepdims=True)
        for r in range(copies):
            out_ref[r, k : k + 1] = both


def backward_kernel(
    me_ref, len_ref, in_ref, x_ref, gain_ref, unit_ref, inv_ref, norm_ref, grad_ref, key_ref, pool_ref, h_ref, row_ref
):
    core = lax.rem(me_ref[0], 2)
    queries, width = unit_ref.shape
    tokens = x_ref.shape[0] // queries
    chunks = width // LANES
    q = queries
    dots = jnp.zeros((q, LANES), F32)
    for k in range(chunks):
        cols = slice(k * LANES, (k + 1) * LANES)
        a = in_ref[2 * k].astype(F32)
        b = in_ref[2 * k + 1].astype(F32)
        b = swap(b)
        both = a + b
        key_ref[:, cols] = both[q : 2 * q]
        pool_ref[:, cols] = both[2 * q : 4 * q]
        g = jnp.where(core == 0, a[:q], b[:q])
        h_ref[:, cols] = g
        dots += g * unit_ref[:, cols]
    along = jnp.sum(dots, axis=1, keepdims=True)
    norm = norm_ref[:, :1]
    for k in range(chunks):
        cols = slice(k * LANES, (k + 1) * LANES)
        h = (h_ref[:, cols] - along * unit_ref[:, cols]) * (norm * gain_ref[:, cols])
        for i in range(q):
            row_ref[i, :, cols] = h[i : i + 1]
    token = lax.broadcasted_iota(jnp.int32, (tokens, 1), 0)

    def one_query(i, carry):
        rows = pl.ds(pl.multiple_of(i * tokens, tokens), tokens)
        length = len_ref[i]
        total = jnp.zeros((tokens, LANES), F32)
        for k in range(chunks):
            cols = slice(k * LANES, (k + 1) * LANES)
            total += x_ref[rows, cols].astype(F32) * row_ref[i, :, cols]
        total = jnp.sum(total, axis=1, keepdims=True)
        inv = inv_ref[rows, :][:, :1]
        scale = jnp.where(token < length, QUERY_SCALE * inv, 0.0) / length.astype(F32)
        back = scale * inv * inv * total / width
        for k in range(chunks):
            cols = slice(k * LANES, (k + 1) * LANES)
            x = x_ref[rows, cols].astype(F32)
            grad_ref[rows, cols] = (scale * row_ref[i, :, cols] - back * x).astype(BF16)
        return carry

    lax.fori_loop(0, queries, one_query, 0)


def call(kernel, outs, args, smem, flops, scratch=()):
    specs = [
        pl.BlockSpec(memory_space=pltpu.SMEM if i in smem else pltpu.VMEM) for i in range(len(args))
    ]
    size = sum(a.size * a.dtype.itemsize for a in args) + sum(
        o.size * o.dtype.itemsize for o in outs
    )
    return pl.pallas_call(
        kernel,
        out_shape=list(outs),
        in_specs=specs,
        out_specs=[pl.BlockSpec(memory_space=pltpu.VMEM)] * len(outs),
        scratch_shapes=list(scratch),
        compiler_params=pltpu.CompilerParams(vmem_limit_bytes=40 * 1024 * 1024),
        cost_estimate=pl.CostEstimate(flops=flops, bytes_accessed=size, transcendentals=0),
    )(*args)


def shape(dims, dtype):
    return jax.ShapeDtypeStruct(dims, dtype)


def local(query_states, query_lengths, norm_gain, positives, mined_pool, hard_ids):
    owners = lax.axis_size("dp")
    groups = lax.axis_size("rep")
    me = lax.axis_index("dp").astype(jnp.int32).reshape(1)
    core = lax.rem(me, 2)
    _, queries, tokens, width = query_states.shape
    hard = hard_ids.shape[2]
    chips = owners // 2
    q_all = queries * owners
    half = q_all // 2
    x = query_states.reshape(queries * tokens, width)
    lengths = query_lengths.reshape(queries)
    gain_row = norm_gain.reshape(1, width)
    gain_tiles = norm_gain.reshape(width // LANES, LANES)
    pair = [(i, i ^ 1) for i in range(owners)]
    same_core = [[2 * i + c for i in range(chips)] for c in range(2)]

    out, unit, inv, norm = call(
        embed_kernel,
        [
            shape((owners, 3 * queries, LANES), BF16),
            shape((queries, width), F32),
            shape((queries * tokens, LANES), F32),
            shape((queries, LANES), F32),
        ],
        [lengths, x, gain_row, positives[0], mined_pool[0], hard_ids[0]],
        (0,),
        8_000_000,
        [pltpu.VMEM((queries * tokens, LANES), F32)],
    )
    got = lax.all_to_all(out, "dp", 0, 0, tiled=True).reshape(chips, 2, 3 * queries, LANES)
    gotx = lax.ppermute(got, "dp", pair)

    def similar(*refs):
        similar_kernel(hard, *refs)

    part, e, unit_f, own, p, m, ids = call(
        similar,
        [
            shape((chips, queries, q_all + LANES), F32),
            shape((half, LANES), BF16),
            shape((half, LANES), F32),
            shape((half, LANES), F32),
            shape((q_all, LANES), BF16),
            shape((2 * q_all, LANES), BF16),
            shape((half, LANES), jnp.int32),
        ],
        [core, got, gotx],
        (0,),
        100_000_000,
    )
    pieces = lax.all_to_all(part, "dp", 0, 0, tiled=True, axis_index_groups=same_core)

    def softmax(*refs):
        softmax_kernel(hard, *refs)

    (sent,) = call(
        softmax, [shape((chips, queries, q_all + LANES), BF16)], [me, pieces], (0,), 1_000_000
    )
    weights = lax.all_to_all(sent, "dp", 0, 0, tiled=True, axis_index_groups=same_core)

    def slices(*refs):
        slices_kernel(hard, *refs)

    (back,) = call(
        slices,
        [shape((owners, 5 * queries, LANES), BF16)],
        [me, weights, e, unit_f, own, p, m, ids, gain_tiles],
        (0,),
        200_000_000,
    )
    home = lax.all_to_all(back, "dp", 0, 0, tiled=True)
    (gain_sent,) = call(
        gain_kernel, [shape((groups, width // LANES, LANES), F32)], [home], (), 100_000
    )
    gain_groups = lax.all_to_all(gain_sent, "rep", 0, 0, tiled=True)
    query_grad, key_grad, pool_grad = call(
        backward_kernel,
        [
            shape((queries * tokens, width), BF16),
            shape((queries, width), F32),
            shape((2 * queries, width), F32),
        ],
        [me, lengths, home, x, gain_row, unit, inv, norm],
        (0, 1),
        10_000_000,
        [pltpu.VMEM((queries, width), F32), pltpu.VMEM((queries, 1, width), F32)],
    )
    gain_grad = jnp.sum(gain_groups, axis=0).reshape(width)
    return (
        query_grad.reshape(query_states.shape),
        key_grad[None],
        pool_grad[None],
        gain_grad,
    )


def solution(mesh):
    placed = (
        P("rep", "dp", None, None),
        P("rep", "dp"),
        P(),
        P("rep", "dp", None),
        P("rep", "dp", None),
        P("rep", "dp", None),
    )
    return jax.shard_map(
        local,
        mesh=mesh,
        in_specs=placed,
        out_specs=(P("rep", "dp", None, None), P("rep", "dp", None), P("rep", "dp", None), P()),
        check_vma=False,
    )
```

time: 467 us -> 135 us (0.29)
  blocking collectives: 299 us -> 98.2 us
  waiting for transfers between devices: 95.7 us -> 6.58 us
  other arithmetic: 17.1 us -> 0.62 us
  matrix products: 14.8 us -> 0 us
  between operations: 15 us -> 0.69 us
  Pallas kernels: 0 us -> 10.6 us
  local copies, waits for them, and re-layouts: 11.4 us -> 5.48 us
    unnamed x1 -> x0, blocking collectives: 164 us -> none
    psum x1 -> x0, blocking collectives: 110 us -> none  [local(): gain_grad = lax.psum(gain_part, ('rep', 'dp'))]
    all_to_all x1 -> x4, blocking collectives: 24.1 us -> 98.2 us  [the longest x1 29.4 us: local(): lax.all_to_all(out, 'dp', 0, 0, tiled=True)]
    all_gather x2 -> x0, waiting for transfers between devices: 62.7 us -> none  [the longest x1 62.7 us: local(): block_row_list = lax.all_gather(local_key_rows, 'dp', axis=0, tiled=True)]
    all_to_all x2 -> x1, waiting for transfers between devices: 32.4 us -> 5.15 us  [local(): gain_groups = lax.all_to_all(gain_sent, 'rep', 0, 0, tiled=True)]
    dot_general x6 -> x0, matrix products: 14.8 us -> none  [the longest x1 5.95 us: local(): lax.dot_general(softmax_probs, block_row_list, (((0,), (0,)), ((), ())),...]
    pallas_call x0 -> x6, Pallas kernels: none -> 10.6 us  [call(): pl.pallas_call(kernel, out_shape=list(outs), in_specs=specs, out_specs=[p...]
    reduce_sum x7 -> x1, other arithmetic: 6.81 us -> 0.62 us  [local(): gain_grad = jnp.sum(gain_groups, axis=0).reshape(width)]
  transfers between devices with their start and end apart: 4 -> 2, of which waited for: 2 -> 2; matrix products, arithmetic and copies ran while one was open for 8% -> 0% of each run, Pallas kernels for 0% -> 3%
where the time goes in v2:
time: 135 us; the launch traced here: 134 us
  blocking collectives  98.2 us (73%)
  starting transfers between devices  11.9 us (9%)
  Pallas kernels  10.6 us (8%)
  waiting for transfers between devices  6.58 us (5%)
  local copies, waits for them, and re-layouts  5.48 us (4%)
    all_to_all x1, blocking collectives, local(): lax.all_to_all(out, 'dp', 0, 0, tiled=True)  29.4 us
    all_to_all x1, blocking collectives, local(): home = lax.all_to_all(back, 'dp', 0, 0, tiled=True)  26.2 us
    all_to_all x1, blocking collectives, local(): lax.all_to_all(part, 'dp', 0, 0, tiled=True, axis_index_groups=same_core)  23.8 us
    all_to_all x1, blocking collectives, local(): lax.all_to_all(sent, 'dp', 0, 0, tiled=True, axis_index_groups=same_core)  18.8 us
    pallas_call x6, Pallas kernels, call(): pl.pallas_call(kernel, out_shape=list(outs), in_specs=specs, out_specs=[p...  10.6 us
    all_to_all x1, starting transfers between devices, local(): gain_groups = lax.all_to_all(gain_sent, 'rep', 0, 0, tiled=True)  9.77 us
    unnamed x17, local copies, waits for them, and re-layouts  5.48 us
    all_to_all x1, waiting for transfers between devices, local(): gain_groups = lax.all_to_all(gain_sent, 'rep', 0, 0, tiled=True)  5.15 us
  transfers between devices with their start and end apart: 2, of which 2 were waited for; matrix products, arithmetic and copies ran while one was open for 0% of the time, Pallas kernels for 3%

profile of v2, /device:TPU:1, one launch (start us, length us, event | category | flops | bytes accessed | tf_op | source)
XLA Modules:
  0.0 134.1 jit_solution(14608146051559436361)
XLA Ops:
  0.6 0.8 copy.10
  1.4 0.0 copy-start
  1.4 1.6 %copy-done = bf16[1,8,32,4096]{3,2,1,0:T(8,128)(2,1)S(1)} copy-done((bf16[1,8,32,4096]{3,2,1,0:T(8,128)(2,1)S(1)}, bf16[1,8,32,4096]{3,2,1,0:T(8,128)(2,1)}, u32[]{:S(2)}) %copy-start) | copy-done | bytes 2097176
  3.0 0.0 copy-start.2
  3.0 0.7 copy-done.2
  3.7 0.0 copy-start.4
  3.7 0.9 copy-done.4
  4.6 0.0 copy-start.5
  4.6 0.8 copy-done.5
  5.4 0.0 copy-start.6
  5.4 0.7 copy-done.6
  6.1 2.7 %shard_map.93 = (bf16[64,24,128]{2,1,0:T(8,128)(2,1)S(1)}, f32[8,4096]{1,0:T(8,128)S(1)}, f32[256,128]{1,0:T(8,128)S(1)}, f32[8,128]{1,0:T(8,128)S(1)}) custom-call(s32[8]{0:T(128)S(1)} %bitcast.23, bf16[256,4096]{1,0:T(8,128)(2,1)S(1)} %bitcast.13, f32[1,4096]{1,0:T(1,128)S(1)} %bitcast.17, bf16[8,4096]{1,0:T(8,128)(2,1)S(1)} %bitcast.21, ...), custom_call_target="tpu_custom_call" | custom-call | flops 8000000 | bytes 2969856 | tf_op jit(solution)/shard_map/pallas_call | solution.py:272
  8.8 0.0 copy-start.3
  8.9 29.4 %all_to_all.25 = bf16[64,24,128]{2,1,0:T(8,128)(2,1)S(1)} all-to-all(bf16[64,24,128]{2,1,0:T(8,128)(2,1)S(1)} %get-tuple-element.18), channel_id=1, replica_groups=mesh['rep'=8,'dp'=64] {'dp'}, dimensions={0} | all-to-all | bytes 786432 | tf_op jit(solution)/shard_map/all_to_all | solution.py:317
  38.3 2.2 %collective-permute-start = (bf16[32,2,24,128]{3,2,1,0:T(8,128)(2,1)S(1)}, bf16[32,2,24,128]{3,2,1,0:T(8,128)(2,1)S(1)}, u32[]{:S(2)}, u32[]{:S(2)}) collective-permute-start(bf16[32,2,24,128]{3,2,1,0:T(8,128)(2,1)S(1)} %bitcast.15), channel_id=1, source_target_pairs={{0,1},{1,0},{2,3},{3,2},{4,5},{5,4},{6,7},{7,6},{8,9},{9,8},{10,11... | collective-permute-start | bytes 1179656 | tf_op jit(solution)/shard_map/ppermute | solution.py:318
  40.5 1.4 %collective-permute-done.refs_2_ = bf16[32,2,24,128]{3,2,1,0:T(8,128)(2,1)S(1)} collective-permute-done((bf16[32,2,24,128]{3,2,1,0:T(8,128)(2,1)S(1)}, bf16[32,2,24,128]{3,2,1,0:T(8,128)(2,1)S(1)}, u32[]{:S(2)}, u32[]{:S(2)}) %collective-permute-start) | collective-permute-done | bytes 393248 | tf_op jit(solution)/shard_map/ppermute | solution.py:318
  41.9 1.1 shard_map.94
  43.0 23.8 %all_to_all.26.refs_1_ = f32[32,8,640]{2,1,0:T(8,128)S(1)} all-to-all(f32[32,8,640]{2,1,0:T(8,128)S(1)} %get-tuple-element.19), channel_id=1, replica_groups={{0,2,4,6,8,10,12,14,16,18,20,22,24,26,28,30,32,34,36,38,40,42,44,46,48,..., dimensions={0} | all-to-all | bytes 1310720 | tf_op jit(solution)/shard_map/all_to_all | solution.py:338
  66.8 0.2 shard_map.95
  67.0 18.8 %all_to_all.27.refs_1_ = bf16[32,8,640]{2,1,0:T(8,128)(2,1)S(1)} all-to-all(bf16[32,8,640]{2,1,0:T(8,128)(2,1)S(1)} %shard_map.95), channel_id=1, replica_groups={{0,2,4,6,8,10,12,14,16,18,20,22,24,26,28,30,32,34,36,38,40,42,44,46,48,..., dimensions={0} | all-to-all | bytes 655360 | tf_op jit(solution)/shard_map/all_to_all | solution.py:346
  85.8 0.0 copy-done.3
  85.8 0.0 copy-start.1
  85.8 0.0 copy-start.7
  85.8 1.6 %shard_map.96 = bf16[64,40,128]{2,1,0:T(8,128)(2,1)S(1)} custom-call(s32[1]{0:T(128)} %bitcast.refs_0_.me_ref, bf16[32,8,640]{2,1,0:T(8,128)(2,1)S(1)} %all_to_all.27.refs_1_, bf16[256,128]{1,0:T(8,128)(2,1)S(1)} %get-tuple-element.20.refs_2_, f32[256,128]{1,0:T(8,128)S(1)} %get-tuple-element.21.refs_3_, f32[256,128]{1,0:T(8,128)S(1)} %get-tuple-element.22.refs_4_, ...), custom_call_target="tpu_custom_call" | custom-call | flops 200000000 | bytes 1851396 | tf_op jit(solution)/shard_map/pallas_call | solution.py:272
  87.4 26.2 %all_to_all.28.in_ref = bf16[64,40,128]{2,1,0:T(8,128)(2,1)S(1)} all-to-all(bf16[64,40,128]{2,1,0:T(8,128)(2,1)S(1)} %shard_map.96), channel_id=1, replica_groups=mesh['rep'=8,'dp'=64] {'dp'}, dimensions={0} | all-to-all | bytes 1310720 | tf_op jit(solution)/shard_map/all_to_all | solution.py:358
  113.6 0.8 shard_map.98
  114.4 9.8 %all-to-all-start.4 = ((f32[8,32,128]{2,1,0:T(8,128)}), f32[8,32,128]{2,1,0:T(8,128)S(1)}, u32[]{:S(2)}, u32[]{:S(2)}) async-start(f32[8,32,128]{2,1,0:T(8,128)} %shard_map.98), calls=%async_computation.4 | async-start | bytes 262144 | tf_op jit(solution)/shard_map/all_to_all | solution.py:362
  124.1 0.0 copy-done.1
  124.1 0.0 copy-done.7
  124.1 4.2 %shard_map.97 = (bf16[256,4096]{1,0:T(8,128)(2,1)}, f32[8,4096]{1,0:T(8,128)}, f32[16,4096]{1,0:T(8,128)}) custom-call(s32[1]{0:T(128)} %bitcast.refs_0_.me_ref, s32[8]{0:T(128)S(1)} %bitcast.24, bf16[64,40,128]{2,1,0:T(8,128)(2,1)S(1)} %all_to_all.28.in_ref, bf16[256,4096]{1,0:T(8,128)(2,1)S(1)} %bitcast.14, f32[1,4096]{1,0:T(1,128)S(1)} %bitcast.19, ...), custom_call_target="tpu_custom_call" | custom-call | flops 10000000 | bytes 5525540 | tf_op jit(solution)/shard_map/pallas_call | solution.py:272
  128.3 5.2 %all-to-all-done.4 = f32[8,32,128]{2,1,0:T(8,128)S(1)} async-done(((f32[8,32,128]{2,1,0:T(8,128)}), f32[8,32,128]{2,1,0:T(8,128)S(1)}, u32[]{:S(2)}, u32[]{:S(2)}) %all-to-all-start.4) | async-done | bytes 131104 | tf_op jit(solution)/shard_map/all_to_all | solution.py:362
  133.5 0.6 reduce_sum.9
Async XLA Ops:
  1.4 1.6 %copy-start = (bf16[1,8,32,4096]{3,2,1,0:T(8,128)(2,1)S(1)}, bf16[1,8,32,4096]{3,2,1,0:T(8,128)(2,1)}, u32[]{:S(2)}) copy-start(bf16[1,8,32,4096]{3,2,1,0:T(8,128)(2,1)} %param.6) | copy-start | bytes 6291460
  3.0 0.7 copy-start.2
  3.7 0.9 copy-start.4
  4.6 0.8 copy-start.5
  5.4 0.7 copy-start.6
  8.8 76.9 %copy-start.3 = (f32[4096]{0:T(1024)S(1)}, f32[4096]{0:T(1024)}, u32[]{:S(2)}) copy-start(f32[4096]{0:T(1024)} %param.8) | copy-start | bytes 49156
  38.3 3.6 %collective-permute-start = (bf16[32,2,24,128]{3,2,1,0:T(8,128)(2,1)S(1)}, bf16[32,2,24,128]{3,2,1,0:T(8,128)(2,1)S(1)}, u32[]{:S(2)}, u32[]{:S(2)}) collective-permute-start(bf16[32,2,24,128]{3,2,1,0:T(8,128)(2,1)S(1)} %bitcast.15), channel_id=1, source_target_pairs={{0,1},{1,0},{2,3},{3,2},{4,5},{5,4},{6,7},{7,6},{8,9},{9,8},{10,11... | collective-permute-start | bytes 1179656 | tf_op jit(solution)/shard_map/ppermute | solution.py:318
  85.8 38.4 %copy-start.1 = (bf16[1,8,32,4096]{3,2,1,0:T(8,128)(2,1)S(1)}, bf16[1,8,32,4096]{3,2,1,0:T(8,128)(2,1)}, u32[]{:S(2)}) copy-start(bf16[1,8,32,4096]{3,2,1,0:T(8,128)(2,1)} %param.6) | copy-start | bytes 6291460
  85.8 38.4 %copy-start.7 = (s32[1,8]{1,0:T(1,128)S(1)}, s32[1,8]{1,0:T(1,128)}, u32[]{:S(2)}) copy-start(s32[1,8]{1,0:T(1,128)} %param.7) | copy-start | bytes 100
  114.4 19.1 %all-to-all-start.4 = ((f32[8,32,128]{2,1,0:T(8,128)}), f32[8,32,128]{2,1,0:T(8,128)S(1)}, u32[]{:S(2)}, u32[]{:S(2)}) async-start(f32[8,32,128]{2,1,0:T(8,128)} %shard_map.98), calls=%async_computation.4 | async-start | bytes 262144 | tf_op jit(solution)/shard_map/all_to_all | solution.py:362

commit v3 on v2

v3 whole, which is shorter than its diff:
```python
import jax
import jax.numpy as jnp
from jax import lax
from jax.experimental import pallas as pl
from jax.experimental.pallas import tpu as pltpu
from jax.sharding import PartitionSpec as P

TEMPERATURE = 0.02
QUERY_SCALE = 512.0
POOL_SCALE = 16.0
LANES = 128
F32 = jnp.float32
BF16 = jnp.bfloat16
BY_COLUMN = (((0,), (0,)), ((), ()))
BY_ROW = (((1,), (1,)), ((), ()))


def embed_kernel(
    core_ref, len_hbm, x_hbm, gain_hbm, pos_hbm, pool_hbm, ids_hbm, out_ref, unit_ref, inv_ref, norm_ref,
    len_ref, x_ref, gain_ref, pos_ref, pool_ref, ids_ref, weight_ref, x_sem, small_sem,
):
    queries, width = unit_ref.shape
    tokens = x_ref.shape[1]
    chunks = width // LANES
    small = [
        pltpu.make_async_copy(src, dst, small_sem.at[n])
        for n, (src, dst) in enumerate(
            [
                (len_hbm, len_ref),
                (gain_hbm, gain_ref),
                (pos_hbm, pos_ref),
                (pool_hbm, pool_ref),
                (ids_hbm, ids_ref),
            ]
        )
    ]
    small[0].start()
    states = [
        pltpu.make_async_copy(x_hbm.at[0, i], x_ref.at[i], x_sem.at[i]) for i in range(queries)
    ]
    for copy in states:
        copy.start()
    for copy in small[1:]:
        copy.start()
    small[0].wait()
    token = lax.broadcasted_iota(jnp.int32, (tokens, 1), 0)

    def one_query(i, carry):
        pltpu.make_async_copy(x_hbm.at[0, i], x_ref.at[i], x_sem.at[i]).wait()
        square = jnp.zeros((tokens, LANES), F32)
        for k in range(chunks):
            v = x_ref[i, :, k * LANES : (k + 1) * LANES].astype(F32)
            square += v * v
        inv = lax.rsqrt(jnp.sum(square, axis=1, keepdims=True) / width + 1e-05)
        inv_ref[i] = jnp.broadcast_to(inv, (tokens, LANES))
        length = len_ref[0, i]
        weight = jnp.where(token < length, inv, 0.0) / length.astype(F32)
        weight_ref[i] = jnp.broadcast_to(weight, (tokens, LANES))
        return carry

    lax.fori_loop(0, queries, one_query, 0)
    for copy in small[1:]:
        copy.wait()
    for k in range(chunks):
        cols = slice(k * LANES, (k + 1) * LANES)
        v = jnp.sum(x_ref[:, :, cols].astype(F32) * weight_ref[...], axis=1)
        unit_ref[:, cols] = v * gain_ref[:, cols]
    pooled = unit_ref[...]
    norm = lax.rsqrt(jnp.sum(pooled * pooled, axis=1, keepdims=True) + 1e-06)
    norm_ref[...] = jnp.broadcast_to(norm, norm_ref.shape)
    ids = ids_ref[0]
    hard = ids.shape[1]
    bits = (2 * queries - 1).bit_length()
    half = chunks * 2 * queries
    owner = ids >> bits
    other = jnp.where((owner & 1) == core_ref[0], 0, half)
    place = other + ((owner >> 1) << bits) + (ids & (2 * queries - 1))
    lane = lax.broadcasted_iota(jnp.int32, (queries, LANES), 1)
    id_rows = jnp.zeros((queries, LANES), jnp.int32)
    for m in range(hard):
        one = place[:, m : m + 1]
        id_rows = jnp.where(lane == m, one >> 5, id_rows)
        id_rows = jnp.where(lane == hard + m, one & 31, id_rows)
    id_rows = id_rows.astype(F32)
    for k in range(chunks):
        cols = slice(k * LANES, (k + 1) * LANES)
        unit = unit_ref[:, cols] * norm
        unit_ref[:, cols] = unit
        rows = [unit, id_rows, pos_ref[0, :, cols].astype(F32), pool_ref[0, :, cols].astype(F32)]
        out_ref[k] = jnp.concatenate(rows, axis=0).astype(BF16)


def rows_of(block, first, last):
    return block[:, first:last].reshape(block.shape[0] * (last - first), LANES)


def ids_of(block, q, hard):
    rows = rows_of(block, q, 2 * q)
    lane = lax.broadcasted_iota(jnp.int32, rows.shape, 1)
    ids = rows * 32.0 + pltpu.roll(rows, LANES - hard, 1)
    return jnp.where(lane < hard, ids, 0.0).astype(jnp.int32)


def similar_kernel(hard, got_ref, gotx_ref, sim_ref):
    chips, rows, _ = got_ref.shape
    q = rows // 5
    half = chips * q
    n = 2 * half
    a = got_ref[...].astype(F32)
    b = gotx_ref[...].astype(F32)
    e = rows_of(a, 0, q).astype(BF16)
    p = jnp.concatenate([rows_of(a, 2 * q, 3 * q), rows_of(b, 2 * q, 3 * q)], axis=0).astype(BF16)
    m = jnp.concatenate([rows_of(a, 3 * q, 5 * q), rows_of(b, 3 * q, 5 * q)], axis=0).astype(BF16)
    ids = ids_of(a, q, hard)
    sim_ref[:, :, :n] = lax.dot_general(e, p, BY_ROW, preferred_element_type=F32).reshape(chips, q, n)
    pool = lax.dot_general(e, m, BY_ROW, preferred_element_type=F32)
    tail = jnp.zeros((half, LANES), F32)
    within, tile = ids & (LANES - 1), ids >> 7
    for k in range(2 * n // LANES):
        picked = jnp.take_along_axis(
            pool[:, k * LANES : (k + 1) * LANES], within, axis=1, mode="promise_in_bounds"
        )
        tail = jnp.where(tile == k, picked, tail)
    lane = lax.broadcasted_iota(jnp.int32, (half, LANES), 1)
    tail = jnp.where(lane < hard, tail, 0.0)
    sim_ref[:, :, n:] = tail.reshape(chips, q, LANES)


def softmax_kernel(hard, chip_ref, in_ref, out_ref):
    copies, q, width = out_ref.shape
    n = width - LANES
    scores = jnp.sum(in_ref[...], axis=0) / TEMPERATURE
    column = lax.broadcasted_iota(jnp.int32, (q, width), 1)
    row = lax.broadcasted_iota(jnp.int32, (q, width), 0)
    exps = jnp.where(column < n + hard, jnp.exp(scores), 0.0)
    soft = exps / jnp.sum(exps, axis=1, keepdims=True)
    own = column == row + chip_ref[0] * q
    along = jnp.sum(soft * scores - jnp.where(own, scores, 0.0), axis=1, keepdims=True)
    high = along.astype(BF16).astype(F32)
    sent = jnp.where(column == n + hard, high, soft)
    sent = jnp.where(column == n + hard + 1, along - high, sent)
    sent = sent.astype(BF16)
    for k in range(copies):
        out_ref[k] = sent


def slices_kernel(hard, chip_ref, w_ref, wx_ref, got_ref, gotx_ref, gain_ref, out_ref):
    chips, q, width = w_ref.shape
    n = width - LANES
    half = chips * q
    w = w_ref[...].astype(F32).reshape(half, width)
    wx = wx_ref[...].astype(F32).reshape(half, width)
    a = got_ref[...].astype(F32)
    b = gotx_ref[...].astype(F32)
    tail = jnp.concatenate([w[:, n:], wx[:, n:]], axis=0)
    from_own = jnp.concatenate([w[:, :half], wx[:, half:n]], axis=0).astype(BF16)
    from_other = jnp.concatenate([w[:, half:n], wx[:, :half]], axis=0).astype(BF16)
    idsx = ids_of(b, q, hard)
    ids = jnp.concatenate([ids_of(a, q, hard), idsx ^ n], axis=0)
    column = lax.broadcasted_iota(jnp.int32, (n, n), 1)
    own_spread = jnp.zeros((n, n), F32)
    other_spread = jnp.zeros((n, n), F32)
    for m in range(hard):
        one, weight = ids[:, m : m + 1], tail[:, m : m + 1]
        own_spread += jnp.where(column == one, weight, 0.0)
        other_spread += jnp.where(column == one - n, weight, 0.0)
    own_spread = own_spread.astype(BF16)
    other_spread = other_spread.astype(BF16)
    along = tail[:, hard : hard + 1] + tail[:, hard + 1 : hard + 2]
    e32 = jnp.concatenate([rows_of(a, 0, q), rows_of(b, 0, q)], axis=0)
    e = e32.astype(BF16)
    own_pos, other_pos = rows_of(a, 2 * q, 3 * q), rows_of(b, 2 * q, 3 * q)

    def dot(left, right):
        return jnp.dot(left, right.astype(BF16), preferred_element_type=F32)

    numerator = dot(from_own, own_pos) + dot(from_other, other_pos)
    numerator += dot(own_spread, rows_of(a, 3 * q, 5 * q))
    numerator += dot(other_spread, rows_of(b, 3 * q, 5 * q))
    pos = jnp.concatenate([own_pos, other_pos], axis=0)
    emb_grad = (numerator - pos) / TEMPERATURE - along * e32
    key = lax.dot_general(from_own, e, BY_COLUMN, preferred_element_type=F32)
    key = (key - e32[:half]) / TEMPERATURE
    pool = lax.dot_general(own_spread, e, BY_COLUMN, preferred_element_type=F32)
    pool = pool * (POOL_SCALE / TEMPERATURE)
    gain = gain_ref[pl.ds(chip_ref[0], 1), :]
    gain_part = jnp.sum(emb_grad * e32, axis=0, keepdims=True) / gain
    gain_high = gain_part.astype(BF16).astype(F32)
    row = lax.broadcasted_iota(jnp.int32, (q, LANES), 0)
    gain_rows = jnp.where(row == 0, gain_high, jnp.where(row == 1, gain_part - gain_high, 0.0))
    for k in range(chips):
        rows = slice(k * q, (k + 1) * q)
        block = [emb_grad[rows], key[rows], pool[2 * k * q : 2 * (k + 1) * q], gain_rows]
        out_ref[k] = jnp.concatenate(block, axis=0).astype(BF16)


def gain_kernel(in_ref, out_ref):
    copies, chips, _ = out_ref.shape
    q = in_ref.shape[1] // 5
    for k in range(chips):
        rows = in_ref[k].astype(F32)[4 * q : 5 * q]
        both = jnp.sum(rows, axis=0, keepdims=True)
        for r in range(copies):
            out_ref[r, k : k + 1] = both


def backward_kernel(
    len_ref, in_ref, x_ref, gain_ref, unit_ref, inv_ref, norm_ref, grad_ref, key_ref, pool_ref, h_ref, row_ref
):
    queries, width = unit_ref.shape
    tokens = x_ref.shape[1]
    chunks = width // LANES
    q = queries
    dots = jnp.zeros((q, LANES), F32)
    for k in range(chunks):
        cols = slice(k * LANES, (k + 1) * LANES)
        block = in_ref[k].astype(F32)
        key_ref[:, cols] = block[q : 2 * q]
        pool_ref[:, cols] = block[2 * q : 4 * q]
        g = block[:q]
        h_ref[:, cols] = g
        dots += g * unit_ref[:, cols]
    along = jnp.sum(dots, axis=1, keepdims=True)
    norm = norm_ref[:, :1]
    for k in range(chunks):
        cols = slice(k * LANES, (k + 1) * LANES)
        h = (h_ref[:, cols] - along * unit_ref[:, cols]) * (norm * gain_ref[:, cols])
        for i in range(q):
            row_ref[i, :, cols] = h[i : i + 1]
    token = lax.broadcasted_iota(jnp.int32, (tokens, 1), 0)

    def one_query(i, carry):
        length = len_ref[i]
        total = jnp.zeros((tokens, LANES), F32)
        for k in range(chunks):
            cols = slice(k * LANES, (k + 1) * LANES)
            total += x_ref[i, :, cols].astype(F32) * row_ref[i, :, cols]
        total = jnp.sum(total, axis=1, keepdims=True)
        inv = inv_ref[i][:, :1]
        scale = jnp.where(token < length, QUERY_SCALE * inv, 0.0) / length.astype(F32)
        back = scale * inv * inv * total / width
        for k in range(chunks):
            cols = slice(k * LANES, (k + 1) * LANES)
            x = x_ref[i, :, cols].astype(F32)
            grad_ref[i, :, cols] = (scale * row_ref[i, :, cols] - back * x).astype(BF16)
        return carry

    lax.fori_loop(0, queries, one_query, 0)


def call(kernel, outs, args, flops, smem=(), hbm=(), scratch=()):
    def space(i):
        return pltpu.SMEM if i in smem else pltpu.HBM if i in hbm else pltpu.VMEM

    size = sum(a.size * a.dtype.itemsize for a in args) + sum(
        o.size * o.dtype.itemsize for o in outs
    )
    return pl.pallas_call(
        kernel,
        out_shape=list(outs),
        in_specs=[pl.BlockSpec(memory_space=space(i)) for i in range(len(args))],
        out_specs=[pl.BlockSpec(memory_space=pltpu.VMEM)] * len(outs),
        scratch_shapes=list(scratch),
        compiler_params=pltpu.CompilerParams(vmem_limit_bytes=40 * 1024 * 1024),
        cost_estimate=pl.CostEstimate(flops=flops, bytes_accessed=size, transcendentals=0),
    )(*args)


def shape(dims, dtype):
    return jax.ShapeDtypeStruct(dims, dtype)


def local(query_states, query_lengths, norm_gain, positives, mined_pool, hard_ids):
    owners = lax.axis_size("dp")
    groups = lax.axis_size("rep")
    me = lax.axis_index("dp").astype(jnp.int32).reshape(1)
    core, chip = lax.rem(me, 2), lax.div(me, 2)
    _, queries, tokens, width = query_states.shape
    hard = hard_ids.shape[2]
    chips = owners // 2
    q_all = queries * owners
    lengths = query_lengths.reshape(queries)
    gain_row = norm_gain.reshape(1, width)
    gain_tiles = norm_gain.reshape(chips, LANES)
    pair = [(i, i ^ 1) for i in range(owners)]
    same_core = [[2 * i + c for i in range(chips)] for c in range(2)]

    def among_chips(x):
        return lax.all_to_all(x, "dp", 0, 0, tiled=True, axis_index_groups=same_core)

    def bound(kernel):
        return lambda *refs: kernel(hard, *refs)

    out, unit, inv, norm = call(
        embed_kernel,
        [
            shape((chips, 5 * queries, LANES), BF16),
            shape((queries, width), F32),
            shape((queries, tokens, LANES), F32),
            shape((queries, LANES), F32),
        ],
        [core, query_lengths, query_states, gain_row, positives, mined_pool, hard_ids],
        8_000_000,
        (0,),
        (1, 2, 3, 4, 5, 6),
        [
            pltpu.SMEM((1, queries), jnp.int32),
            pltpu.VMEM((queries, tokens, width), BF16),
            pltpu.VMEM((1, width), F32),
            pltpu.VMEM((1, queries, width), BF16),
            pltpu.VMEM((1, 2 * queries, width), BF16),
            pltpu.VMEM((1, queries, hard), jnp.int32),
            pltpu.VMEM((queries, tokens, LANES), F32),
            pltpu.SemaphoreType.DMA((queries,)),
            pltpu.SemaphoreType.DMA((5,)),
        ],
    )
    got = among_chips(out)
    gotx = lax.ppermute(got, "dp", pair)

    (part,) = call(
        bound(similar_kernel),
        [shape((chips, queries, q_all + LANES), F32)],
        [got, gotx],
        100_000_000,
    )
    pieces = among_chips(part)
    (sent,) = call(
        bound(softmax_kernel),
        [shape((chips, queries, q_all + LANES), BF16)],
        [chip, pieces],
        1_000_000,
        (0,),
    )
    weights = among_chips(sent)
    weightsx = lax.ppermute(weights, "dp", pair)

    (back,) = call(
        bound(slices_kernel),
        [shape((chips, 5 * queries, LANES), BF16)],
        [chip, weights, weightsx, got, gotx, gain_tiles],
        400_000_000,
        (0,),
    )
    home = among_chips(back)
    (gain_sent,) = call(
        gain_kernel, [shape((groups, width // LANES, LANES), F32)], [home], 100_000
    )
    gain_groups = lax.all_to_all(gain_sent, "rep", 0, 0, tiled=True)
    query_grad, key_grad, pool_grad = call(
        backward_kernel,
        [
            shape((queries, tokens, width), BF16),
            shape((queries, width), F32),
            shape((2 * queries, width), F32),
        ],
        [lengths, home, query_states[0], gain_row, unit, inv, norm],
        10_000_000,
        (0,),
        (),
        [pltpu.VMEM((queries, width), F32), pltpu.VMEM((queries, 1, width), F32)],
    )
    gain_grad = jnp.sum(gain_groups, axis=0).reshape(width)
    return query_grad[None], key_grad[None], pool_grad[None], gain_grad


def solution(mesh):
    placed = (
        P("rep", "dp", None, None),
        P("rep", "dp"),
        P(),
        P("rep", "dp", None),
        P("rep", "dp", None),
        P("rep", "dp", None),
    )
    return jax.shard_map(
        local,
        mesh=mesh,
        in_specs=placed,
        out_specs=(P("rep", "dp", None, None), P("rep", "dp", None), P("rep", "dp", None), P()),
        check_vma=False,
    )
```

time: 135 us -> 133 us (0.985); the launches traced: 134 us -> 130 us
  blocking collectives: 98.2 us -> 61.2 us
  waiting for transfers between devices: 6.58 us -> 27.3 us
  starting transfers between devices: 11.9 us -> 22.5 us
  Pallas kernels: 10.6 us -> 12.4 us
    all_to_all x4 -> x3, blocking collectives: 98.2 us -> 61.2 us  [among_chips(): lax.all_to_all(x, 'dp', 0, 0, tiled=True, axis_index_groups=same_core)]
    all_to_all x0 -> x1, waiting for transfers between devices: none -> 19.6 us  [among_chips(): lax.all_to_all(x, 'dp', 0, 0, tiled=True, axis_index_groups=same_core)]
    ppermute x0 -> x1, starting transfers between devices: none -> 4.3 us  [local(): weightsx = lax.ppermute(weights, 'dp', pair)]
    all_to_all x0 -> x1, starting transfers between devices: none -> 3.9 us  [among_chips(): lax.all_to_all(x, 'dp', 0, 0, tiled=True, axis_index_groups=same_core)]
    ppermute x1, starting transfers between devices: 2.17 us -> 4.51 us  [local(): gotx = lax.ppermute(got, 'dp', pair)]
    pallas_call x6, Pallas kernels: 10.6 us -> 12.4 us  [call(): pl.pallas_call(kernel, out_shape=list(outs), in_specs=[pl.BlockSpec(memor...]
    unnamed x17 -> x25, local copies, waits for them, and re-layouts: 5.48 us -> 5.51 us
  transfers between devices with their start and end apart: 2 -> 4, of which waited for: 2 -> 4; matrix products, arithmetic and copies ran while one was open for 0% -> 0% of each run, Pallas kernels for 3% -> 3%
where the time goes in v3:
time: 133 us; the launch traced here: 130 us
  blocking collectives  61.2 us (46%)
  waiting for transfers between devices  27.3 us (21%)
  starting transfers between devices  22.5 us (17%)
  Pallas kernels  12.4 us (9%)
  local copies, waits for them, and re-layouts  5.51 us (4%)
    all_to_all x3, blocking collectives, among_chips(): lax.all_to_all(x, 'dp', 0, 0, tiled=True, axis_index_groups=same_core)  61.2 us
    all_to_all x1, waiting for transfers between devices, among_chips(): lax.all_to_all(x, 'dp', 0, 0, tiled=True, axis_index_groups=same_core)  19.6 us
    pallas_call x6, Pallas kernels, call(): pl.pallas_call(kernel, out_shape=list(outs), in_specs=[pl.BlockSpec(memor...  12.4 us
    all_to_all x1, starting transfers between devices, local(): gain_groups = lax.all_to_all(gain_sent, 'rep', 0, 0, tiled=True)  9.77 us
    unnamed x25, local copies, waits for them, and re-layouts  5.51 us
    all_to_all x1, waiting for transfers between devices, local(): gain_groups = lax.all_to_all(gain_sent, 'rep', 0, 0, tiled=True)  5.23 us
    ppermute x1, starting transfers between devices, local(): gotx = lax.ppermute(got, 'dp', pair)  4.51 us
    ppermute x1, starting transfers between devices, local(): weightsx = lax.ppermute(weights, 'dp', pair)  4.3 us
  transfers between devices with their start and end apart: 4, of which 4 were waited for; matrix products, arithmetic and copies ran while one was open for 0% of the time, Pallas kernels for 3%

profile of v3, /device:TPU:1, one launch (start us, length us, event | category | flops | bytes accessed | tf_op | source)
XLA Modules:
  0.0 130.3 jit_solution(17436556419837034678)
XLA Ops:
  0.6 0.8 copy.10.ids_hbm
  1.4 1.6 %copy-done = bf16[1,8,32,4096]{3,2,1,0:T(8,128)(2,1)S(1)} copy-done((bf16[1,8,32,4096]{3,2,1,0:T(8,128)(2,1)S(1)}, bf16[1,8,32,4096]{3,2,1,0:T(8,128)(2,1)}, u32[]{:S(2)}) %copy-start) | copy-done | bytes 2097176
  3.0 0.7 copy-done.2
  3.7 0.9 copy-done.4
  4.6 0.8 copy-done.7
  5.5 0.7 copy-done.10
  6.1 2.7 %shard_map.93 = (bf16[32,40,128]{2,1,0:T(8,128)(2,1)S(1)}, f32[8,4096]{1,0:T(8,128)S(1)}, f32[8,32,128]{2,1,0:T(8,128)S(1)}, f32[8,128]{1,0:T(8,128)S(1)}) custom-call(s32[1]{0:T(128)S(6)} %rem.9.core_ref, s32[1,8]{1,0:T(1,128)S(1)} %copy-done.10, bf16[1,8,32,4096]{3,2,1,0:T(8,128)(2,1)S(1)} %copy-done, f32[1,4096]{1,0:T(1,128)S(1)} %bitcast.10, ...), custom_call_target="tpu_custom_call" | custom-call | flops 8000000 | bytes 2904324 | tf_op jit(solution)/shard_map/pallas_call | solution.py:258
  8.8 0.0 copy-start.5
  8.8 0.0 copy-start.8
  8.8 26.3 %all_to_all.25.refs_0_.refs_3_ = bf16[32,40,128]{2,1,0:T(8,128)(2,1)S(1)} all-to-all(bf16[32,40,128]{2,1,0:T(8,128)(2,1)S(1)} %get-tuple-element.11), channel_id=1, replica_groups={{0,2,4,6,8,10,12,14,16,18,20,22,24,26,28,30,32,34,36,38,40,42,44,46,48,..., dimensions={0} | all-to-all | bytes 655360 | tf_op jit(solution)/shard_map/all_to_all | solution.py:289
  35.2 4.5 %collective-permute-start = (bf16[32,40,128]{2,1,0:T(8,128)(2,1)S(1)}, bf16[32,40,128]{2,1,0:T(8,128)(2,1)S(1)}, u32[]{:S(2)}, u32[]{:S(2)}) collective-permute-start(bf16[32,40,128]{2,1,0:T(8,128)(2,1)S(1)} %all_to_all.25.refs_0_.refs_3_), channel_id=1, source_target_pairs={{0,1},{1,0},{2,3},{3,2},{4,5},{5,4},{6,7},{7,6},{8,9},{9,8},{10,11... | collective-permute-start | bytes 983048 | tf_op jit(solution)/shard_map/ppermute | solution.py:319
  39.7 1.2 collective-permute-done.refs_1_.refs_4_
  40.9 0.0 copy-done.5
  40.9 0.0 copy-done.8
  40.9 1.7 %shard_map.94 = f32[32,8,640]{2,1,0:T(8,128)} custom-call(bf16[32,40,128]{2,1,0:T(8,128)(2,1)S(1)} %all_to_all.25.refs_0_.refs_3_, bf16[32,40,128]{2,1,0:T(8,128)(2,1)S(1)} %collective-permute-done.refs_1_.refs_4_), custom_call_target="tpu_custom_call" | custom-call | flops 100000000 | bytes 1310720 | tf_op jit(solution)/shard_map/pallas_call | solution.py:258
  42.6 3.9 %all-to-all-start.1 = ((f32[32,8,640]{2,1,0:T(8,128)}), f32[32,8,640]{2,1,0:T(8,128)S(1)}, u32[]{:S(2)}, u32[]{:S(2)}) async-start(f32[32,8,640]{2,1,0:T(8,128)} %shard_map.94), calls=%async_computation.1 | async-start | bytes 1310720 | tf_op jit(solution)/shard_map/all_to_all | solution.py:289
  46.5 0.0 copy-start.1
  46.5 19.6 %all-to-all-done.1.refs_1_ = f32[32,8,640]{2,1,0:T(8,128)S(1)} async-done(((f32[32,8,640]{2,1,0:T(8,128)}), f32[32,8,640]{2,1,0:T(8,128)S(1)}, u32[]{:S(2)}, u32[]{:S(2)}) %all-to-all-start.1) | async-done | bytes 655392 | tf_op jit(solution)/shard_map/all_to_all | solution.py:289
  66.1 0.2 shard_map.95
  66.3 0.0 copy-start.6
  66.3 0.0 copy-start.9
  66.3 0.0 copy-start.11
  66.3 18.5 %all_to_all.26.refs_1_ = bf16[32,8,640]{2,1,0:T(8,128)(2,1)S(1)} all-to-all(bf16[32,8,640]{2,1,0:T(8,128)(2,1)S(1)} %shard_map.95), channel_id=1, replica_groups={{0,2,4,6,8,10,12,14,16,18,20,22,24,26,28,30,32,34,36,38,40,42,44,46,48,..., dimensions={0} | all-to-all | bytes 655360 | tf_op jit(solution)/shard_map/all_to_all | solution.py:289
  84.8 4.3 %collective-permute-start.1 = (bf16[32,8,640]{2,1,0:T(8,128)(2,1)S(1)}, bf16[32,8,640]{2,1,0:T(8,128)(2,1)S(1)}, u32[]{:S(2)}, u32[]{:S(2)}) collective-permute-start(bf16[32,8,640]{2,1,0:T(8,128)(2,1)S(1)} %all_to_all.26.refs_1_), channel_id=1, source_target_pairs={{0,1},{1,0},{2,3},{3,2},{4,5},{5,4},{6,7},{7,6},{8,9},{9,8},{10,11... | collective-permute-start | bytes 983048 | tf_op jit(solution)/shard_map/ppermute | solution.py:336
  89.1 1.2 collective-permute-done.1.refs_2_
  90.4 3.1 %shard_map.96 = bf16[32,40,128]{2,1,0:T(8,128)(2,1)S(1)} custom-call(s32[1]{0:T(128)S(6)} %div.18.refs_0_, bf16[32,8,640]{2,1,0:T(8,128)(2,1)S(1)} %all_to_all.26.refs_1_, bf16[32,8,640]{2,1,0:T(8,128)(2,1)S(1)} %collective-permute-done.1.refs_2_, bf16[32,40,128]{2,1,0:T(8,128)(2,1)S(1)} %all_to_all.25.refs_0_.refs_3_, ...), custom_call_target="tpu_custom_call" | custom-call | flops 400000000 | bytes 1654788 | tf_op jit(solution)/shard_map/pallas_call | solution.py:258
  93.5 16.4 %all_to_all.27.in_ref = bf16[32,40,128]{2,1,0:T(8,128)(2,1)S(1)} all-to-all(bf16[32,40,128]{2,1,0:T(8,128)(2,1)S(1)} %shard_map.96), channel_id=1, replica_groups={{0,2,4,6,8,10,12,14,16,18,20,22,24,26,28,30,32,34,36,38,40,42,44,46,48,..., dimensions={0} | all-to-all | bytes 655360 | tf_op jit(solution)/shard_map/all_to_all | solution.py:289
  109.8 0.7 shard_map.98
  110.6 9.8 %all-to-all-start.4 = ((f32[8,32,128]{2,1,0:T(8,128)}), f32[8,32,128]{2,1,0:T(8,128)S(1)}, u32[]{:S(2)}, u32[]{:S(2)}) async-start(f32[8,32,128]{2,1,0:T(8,128)} %shard_map.98), calls=%async_computation.4 | async-start | bytes 262144 | tf_op jit(solution)/shard_map/all_to_all | solution.py:349
  120.4 4.1 %shard_map.97 = (bf16[8,32,4096]{2,1,0:T(8,128)(2,1)}, f32[8,4096]{1,0:T(8,128)}, f32[16,4096]{1,0:T(8,128)}) custom-call(s32[8]{0:T(128)S(1)} %bitcast.13, bf16[32,40,128]{2,1,0:T(8,128)(2,1)S(1)} %all_to_all.27.in_ref, bf16[8,32,4096]{2,1,0:T(8,128)(2,1)S(1)} %bitcast.9, f32[1,4096]{1,0:T(1,128)S(1)} %bitcast.12, ...), custom_call_target="tpu_custom_call" | custom-call | flops 10000000 | bytes 5197856 | tf_op jit(solution)/shard_map/pallas_call | solution.py:258
  124.4 5.2 %all-to-all-done.4 = f32[8,32,128]{2,1,0:T(8,128)S(1)} async-done(((f32[8,32,128]{2,1,0:T(8,128)}), f32[8,32,128]{2,1,0:T(8,128)S(1)}, u32[]{:S(2)}, u32[]{:S(2)}) %all-to-all-start.4) | async-done | bytes 131104 | tf_op jit(solution)/shard_map/all_to_all | solution.py:349
  129.7 0.6 reduce_sum.9
  (11 shorter events, 0.0 us)
Async XLA Ops:
  1.4 1.6 %copy-start = (bf16[1,8,32,4096]{3,2,1,0:T(8,128)(2,1)S(1)}, bf16[1,8,32,4096]{3,2,1,0:T(8,128)(2,1)}, u32[]{:S(2)}) copy-start(bf16[1,8,32,4096]{3,2,1,0:T(8,128)(2,1)} %x_hbm.1) | copy-start | bytes 6291460
  3.0 0.7 copy-start.2
  3.7 0.9 copy-start.4
  4.6 0.8 copy-start.7
  5.4 0.7 copy-start.10
  8.8 32.1 %copy-start.5 = (f32[8,32,128]{2,1,0:T(8,128)}, f32[8,32,128]{2,1,0:T(8,128)S(1)}, u32[]{:S(2)}) copy-start(f32[8,32,128]{2,1,0:T(8,128)S(1)} %get-tuple-element.13.inv_ref) | copy-start | bytes 393220
  8.8 32.1 %copy-start.8 = (f32[8,128]{1,0:T(8,128)}, f32[8,128]{1,0:T(8,128)S(1)}, u32[]{:S(2)}) copy-start(f32[8,128]{1,0:T(8,128)S(1)} %get-tuple-element.14.norm_ref) | copy-start | bytes 12292
  35.1 55.2 %copy-start.3 = (f32[4096]{0:T(1024)S(1)}, f32[4096]{0:T(1024)}, u32[]{:S(2)}) copy-start(f32[4096]{0:T(1024)} %param.8) | copy-start | bytes 49156
  35.2 5.7 %collective-permute-start = (bf16[32,40,128]{2,1,0:T(8,128)(2,1)S(1)}, bf16[32,40,128]{2,1,0:T(8,128)(2,1)S(1)}, u32[]{:S(2)}, u32[]{:S(2)}) collective-permute-start(bf16[32,40,128]{2,1,0:T(8,128)(2,1)S(1)} %all_to_all.25.refs_0_.refs_3_), channel_id=1, source_target_pairs={{0,1},{1,0},{2,3},{3,2},{4,5},{5,4},{6,7},{7,6},{8,9},{9,8},{10,11... | collective-permute-start | bytes 983048 | tf_op jit(solution)/shard_map/ppermute | solution.py:319
  42.6 23.5 %all-to-all-start.1 = ((f32[32,8,640]{2,1,0:T(8,128)}), f32[32,8,640]{2,1,0:T(8,128)S(1)}, u32[]{:S(2)}, u32[]{:S(2)}) async-start(f32[32,8,640]{2,1,0:T(8,128)} %shard_map.94), calls=%async_computation.1 | async-start | bytes 1310720 | tf_op jit(solution)/shard_map/all_to_all | solution.py:289
  46.5 73.9 %copy-start.1 = (bf16[1,8,32,4096]{3,2,1,0:T(8,128)(2,1)S(1)}, bf16[1,8,32,4096]{3,2,1,0:T(8,128)(2,1)}, u32[]{:S(2)}) copy-start(bf16[1,8,32,4096]{3,2,1,0:T(8,128)(2,1)} %x_hbm.1) | copy-start | bytes 6291460
  66.3 54.1 %copy-start.6 = (f32[8,32,128]{2,1,0:T(8,128)S(1)}, f32[8,32,128]{2,1,0:T(8,128)}, u32[]{:S(2)}) copy-start(f32[8,32,128]{2,1,0:T(8,128)} %copy-done.5) | copy-start | bytes 393220
  66.3 54.1 %copy-start.9 = (f32[8,128]{1,0:T(8,128)S(1)}, f32[8,128]{1,0:T(8,128)}, u32[]{:S(2)}) copy-start(f32[8,128]{1,0:T(8,128)} %copy-done.8) | copy-start | bytes 12292
  66.3 54.1 %copy-start.11 = (s32[1,8]{1,0:T(1,128)S(1)}, s32[1,8]{1,0:T(1,128)}, u32[]{:S(2)}) copy-start(s32[1,8]{1,0:T(1,128)} %len_hbm.1) | copy-start | bytes 100
  84.8 5.5 %collective-permute-start.1 = (bf16[32,8,640]{2,1,0:T(8,128)(2,1)S(1)}, bf16[32,8,640]{2,1,0:T(8,128)(2,1)S(1)}, u32[]{:S(2)}, u32[]{:S(2)}) collective-permute-start(bf16[32,8,640]{2,1,0:T(8,128)(2,1)S(1)} %all_to_all.26.refs_1_), channel_id=1, source_target_pairs={{0,1},{1,0},{2,3},{3,2},{4,5},{5,4},{6,7},{7,6},{8,9},{9,8},{10,11... | collective-permute-start | bytes 983048 | tf_op jit(solution)/shard_map/ppermute | solution.py:336
  110.6 19.1 %all-to-all-start.4 = ((f32[8,32,128]{2,1,0:T(8,128)}), f32[8,32,128]{2,1,0:T(8,128)S(1)}, u32[]{:S(2)}, u32[]{:S(2)}) async-start(f32[8,32,128]{2,1,0:T(8,128)} %shard_map.98), calls=%async_computation.4 | async-start | bytes 262144 | tf_op jit(solution)/shard_map/all_to_all | solution.py:349

commit v4 on v3

--- a/solution.py
+++ b/solution.py
@@ -68,20 +68,23 @@
     pooled = unit_ref[...]
     norm = lax.rsqrt(jnp.sum(pooled * pooled, axis=1, keepdims=True) + 1e-06)
     norm_ref[...] = jnp.broadcast_to(norm, norm_ref.shape)
-    ids = ids_ref[0]
-    hard = ids.shape[1]
+    ids = ids_ref[:, 0, :]
+    hard = ids.shape[0]
     bits = (2 * queries - 1).bit_length()
     half = chunks * 2 * queries
     owner = ids >> bits
     other = jnp.where((owner & 1) == core_ref[0], 0, half)
     place = other + ((owner >> 1) << bits) + (ids & (2 * queries - 1))
-    lane = lax.broadcasted_iota(jnp.int32, (queries, LANES), 1)
-    id_rows = jnp.zeros((queries, LANES), jnp.int32)
-    for m in range(hard):
-        one = place[:, m : m + 1]
-        id_rows = jnp.where(lane == m, one >> 5, id_rows)
-        id_rows = jnp.where(lane == hard + m, one & 31, id_rows)
-    id_rows = id_rows.astype(F32)
+    row = lax.broadcasted_iota(jnp.int32, (hard, LANES), 0)
+    lane = lax.broadcasted_iota(jnp.int32, (hard, LANES), 1)
+
+    def lay(x, first):
+        to = (lane == row + first).astype(F32).astype(BF16)
+        return lax.dot_general(
+            x.astype(F32).astype(BF16), to, BY_COLUMN, preferred_element_type=F32
+        )
+
+    id_rows = lay(place >> 5, 0) + lay(place & 31, hard)
     for k in range(chunks):
         cols = slice(k * LANES, (k + 1) * LANES)
         unit = unit_ref[:, cols] * norm
@@ -248,7 +251,7 @@
     lax.fori_loop(0, queries, one_query, 0)
 
 
-def call(kernel, outs, args, flops, smem=(), hbm=(), scratch=()):
+def call(kernel, outs, args, flops, smem=(), hbm=(), scratch=(), vmem=40):
     def space(i):
         return pltpu.SMEM if i in smem else pltpu.HBM if i in hbm else pltpu.VMEM
 
@@ -261,7 +264,7 @@
         in_specs=[pl.BlockSpec(memory_space=space(i)) for i in range(len(args))],
         out_specs=[pl.BlockSpec(memory_space=pltpu.VMEM)] * len(outs),
         scratch_shapes=list(scratch),
-        compiler_params=pltpu.CompilerParams(vmem_limit_bytes=40 * 1024 * 1024),
+        compiler_params=pltpu.CompilerParams(vmem_limit_bytes=vmem * 1024 * 1024),
         cost_estimate=pl.CostEstimate(flops=flops, bytes_accessed=size, transcendentals=0),
     )(*args)
 
@@ -299,7 +302,7 @@
             shape((queries, tokens, LANES), F32),
             shape((queries, LANES), F32),
         ],
-        [core, query_lengths, query_states, gain_row, positives, mined_pool, hard_ids],
+        [core, query_lengths, query_states, gain_row, positives, mined_pool, hard_ids.transpose(2, 0, 1)],
         8_000_000,
         (0,),
         (1, 2, 3, 4, 5, 6),
@@ -309,11 +312,12 @@
             pltpu.VMEM((1, width), F32),
             pltpu.VMEM((1, queries, width), BF16),
             pltpu.VMEM((1, 2 * queries, width), BF16),
-            pltpu.VMEM((1, queries, hard), jnp.int32),
+            pltpu.VMEM((hard, 1, queries), jnp.int32),
             pltpu.VMEM((queries, tokens, LANES), F32),
             pltpu.SemaphoreType.DMA((queries,)),
             pltpu.SemaphoreType.DMA((5,)),
         ],
+        60,
     )
     got = among_chips(out)
     gotx = lax.ppermute(got, "dp", pair)

time: 133 us -> 129 us (0.970)
  local copies, waits for them, and re-layouts: 5.51 us -> 0.04 us
    unnamed x25 -> x12, local copies, waits for them, and re-layouts: 5.51 us -> 0.04 us
where the time goes in v4:
time: 129 us; the launch traced here: 126 us
  blocking collectives  61.4 us (48%)
  waiting for transfers between devices  27.3 us (21%)
  starting transfers between devices  22.5 us (17%)
  Pallas kernels  13.7 us (11%)
    all_to_all x3, blocking collectives, among_chips(): lax.all_to_all(x, 'dp', 0, 0, tiled=True, axis_index_groups=same_core)  61.4 us
    all_to_all x1, waiting for transfers between devices, among_chips(): lax.all_to_all(x, 'dp', 0, 0, tiled=True, axis_index_groups=same_core)  19.6 us
    pallas_call x6, Pallas kernels, call(): pl.pallas_call(kernel, out_shape=list(outs), in_specs=[pl.BlockSpec(memor...  13.7 us
    all_to_all x1, starting transfers between devices, local(): gain_groups = lax.all_to_all(gain_sent, 'rep', 0, 0, tiled=True)  9.76 us
    all_to_all x1, waiting for transfers between devices, local(): gain_groups = lax.all_to_all(gain_sent, 'rep', 0, 0, tiled=True)  5.22 us
    ppermute x1, starting transfers between devices, local(): gotx = lax.ppermute(got, 'dp', pair)  4.51 us
    ppermute x1, starting transfers between devices, local(): weightsx = lax.ppermute(weights, 'dp', pair)  4.3 us
    all_to_all x1, starting transfers between devices, among_chips(): lax.all_to_all(x, 'dp', 0, 0, tiled=True, axis_index_groups=same_core)  3.9 us
  transfers between devices with their start and end apart: 4, of which 4 were waited for; matrix products, arithmetic and copies ran while one was open for 0% of the time, Pallas kernels for 3%

profile of v4, /device:TPU:1, one launch (start us, length us, event | category | flops | bytes accessed | tf_op | source)
XLA Modules:
  0.0 126.3 jit_solution(5291931758118539948)
XLA Ops:
  0.6 4.0 %shard_map.93 = (bf16[32,40,128]{2,1,0:T(8,128)(2,1)}, f32[8,4096]{1,0:T(8,128)}, f32[8,32,128]{2,1,0:T(8,128)}, f32[8,128]{1,0:T(8,128)}) custom-call(s32[1]{0:T(128)S(6)} %rem.9.core_ref, s32[1,8]{1,0:T(1,128)} %len_hbm.1, bf16[1,8,32,4096]{3,2,1,0:T(8,128)(2,1)} %x_hbm.1, f32[1,4096]{1,0:T(1,128)} %bitcast.11, bf16[1,8,4096]{2,1,0:T(8,128)(2,1)} %pos_hbm.1, ...), custom_call_target="tpu_custom_call" | custom-call | flops 8000000 | bytes 2904324 | tf_op jit(solution)/shard_map/pallas_call | solution.py:261
  4.6 26.5 %all_to_all.25.refs_0_.refs_3_ = bf16[32,40,128]{2,1,0:T(8,128)(2,1)S(1)} all-to-all(bf16[32,40,128]{2,1,0:T(8,128)(2,1)} %get-tuple-element.11), channel_id=1, replica_groups={{0,2,4,6,8,10,12,14,16,18,20,22,24,26,28,30,32,34,36,38,40,42,44,46,48,..., dimensions={0} | all-to-all | bytes 655360 | tf_op jit(solution)/shard_map/all_to_all | solution.py:292
  31.1 0.0 copy-start.1
  31.1 4.5 %collective-permute-start = (bf16[32,40,128]{2,1,0:T(8,128)(2,1)S(1)}, bf16[32,40,128]{2,1,0:T(8,128)(2,1)S(1)}, u32[]{:S(2)}, u32[]{:S(2)}) collective-permute-start(bf16[32,40,128]{2,1,0:T(8,128)(2,1)S(1)} %all_to_all.25.refs_0_.refs_3_), channel_id=1, source_target_pairs={{0,1},{1,0},{2,3},{3,2},{4,5},{5,4},{6,7},{7,6},{8,9},{9,8},{10,11... | collective-permute-start | bytes 983048 | tf_op jit(solution)/shard_map/ppermute | solution.py:323
  35.7 1.2 collective-permute-done.refs_1_.refs_4_
  36.9 1.7 %shard_map.94 = f32[32,8,640]{2,1,0:T(8,128)} custom-call(bf16[32,40,128]{2,1,0:T(8,128)(2,1)S(1)} %all_to_all.25.refs_0_.refs_3_, bf16[32,40,128]{2,1,0:T(8,128)(2,1)S(1)} %collective-permute-done.refs_1_.refs_4_), custom_call_target="tpu_custom_call" | custom-call | flops 100000000 | bytes 1310720 | tf_op jit(solution)/shard_map/pallas_call | solution.py:261
  38.5 3.9 %all-to-all-start.1 = ((f32[32,8,640]{2,1,0:T(8,128)}), f32[32,8,640]{2,1,0:T(8,128)S(1)}, u32[]{:S(2)}, u32[]{:S(2)}) async-start(f32[32,8,640]{2,1,0:T(8,128)} %shard_map.94), calls=%async_computation.1 | async-start | bytes 1310720 | tf_op jit(solution)/shard_map/all_to_all | solution.py:292
  42.4 0.0 copy-start
  42.5 0.0 copy-start.2
  42.5 19.6 %all-to-all-done.1.refs_1_ = f32[32,8,640]{2,1,0:T(8,128)S(1)} async-done(((f32[32,8,640]{2,1,0:T(8,128)}), f32[32,8,640]{2,1,0:T(8,128)S(1)}, u32[]{:S(2)}, u32[]{:S(2)}) %all-to-all-start.1) | async-done | bytes 655392 | tf_op jit(solution)/shard_map/all_to_all | solution.py:292
  62.0 0.2 shard_map.95
  62.3 0.0 copy-start.3
  62.3 0.0 copy-start.4
  62.3 0.0 copy-start.5
  62.3 18.5 %all_to_all.26.refs_1_ = bf16[32,8,640]{2,1,0:T(8,128)(2,1)S(1)} all-to-all(bf16[32,8,640]{2,1,0:T(8,128)(2,1)S(1)} %shard_map.95), channel_id=1, replica_groups={{0,2,4,6,8,10,12,14,16,18,20,22,24,26,28,30,32,34,36,38,40,42,44,46,48,..., dimensions={0} | all-to-all | bytes 655360 | tf_op jit(solution)/shard_map/all_to_all | solution.py:292
  80.8 4.3 %collective-permute-start.1 = (bf16[32,8,640]{2,1,0:T(8,128)(2,1)S(1)}, bf16[32,8,640]{2,1,0:T(8,128)(2,1)S(1)}, u32[]{:S(2)}, u32[]{:S(2)}) collective-permute-start(bf16[32,8,640]{2,1,0:T(8,128)(2,1)S(1)} %all_to_all.26.refs_1_), channel_id=1, source_target_pairs={{0,1},{1,0},{2,3},{3,2},{4,5},{5,4},{6,7},{7,6},{8,9},{9,8},{10,11... | collective-permute-start | bytes 983048 | tf_op jit(solution)/shard_map/ppermute | solution.py:340
  85.1 1.2 collective-permute-done.1.refs_2_
  86.3 0.0 copy-done.1
  86.4 3.1 %shard_map.96 = bf16[32,40,128]{2,1,0:T(8,128)(2,1)S(1)} custom-call(s32[1]{0:T(128)S(6)} %div.18.refs_0_, bf16[32,8,640]{2,1,0:T(8,128)(2,1)S(1)} %all_to_all.26.refs_1_, bf16[32,8,640]{2,1,0:T(8,128)(2,1)S(1)} %collective-permute-done.1.refs_2_, bf16[32,40,128]{2,1,0:T(8,128)(2,1)S(1)} %all_to_all.25.refs_0_.refs_3_, ...), custom_call_target="tpu_custom_call" | custom-call | flops 400000000 | bytes 1654788 | tf_op jit(solution)/shard_map/pallas_call | solution.py:261
  89.5 16.4 %all_to_all.27.in_ref = bf16[32,40,128]{2,1,0:T(8,128)(2,1)S(1)} all-to-all(bf16[32,40,128]{2,1,0:T(8,128)(2,1)S(1)} %shard_map.96), channel_id=1, replica_groups={{0,2,4,6,8,10,12,14,16,18,20,22,24,26,28,30,32,34,36,38,40,42,44,46,48,..., dimensions={0} | all-to-all | bytes 655360 | tf_op jit(solution)/shard_map/all_to_all | solution.py:292
  105.8 0.7 shard_map.98
  106.5 9.8 %all-to-all-start.4 = ((f32[8,32,128]{2,1,0:T(8,128)}), f32[8,32,128]{2,1,0:T(8,128)S(1)}, u32[]{:S(2)}, u32[]{:S(2)}) async-start(f32[8,32,128]{2,1,0:T(8,128)} %shard_map.98), calls=%async_computation.4 | async-start | bytes 262144 | tf_op jit(solution)/shard_map/all_to_all | solution.py:353
  116.3 0.0 copy-done
  116.3 0.0 copy-done.2
  116.3 0.0 copy-done.3
  116.3 0.0 copy-done.4
  116.3 0.0 copy-done.5
  116.3 4.1 %shard_map.97 = (bf16[8,32,4096]{2,1,0:T(8,128)(2,1)}, f32[8,4096]{1,0:T(8,128)}, f32[16,4096]{1,0:T(8,128)}) custom-call(s32[8]{0:T(128)S(1)} %bitcast.14, bf16[32,40,128]{2,1,0:T(8,128)(2,1)S(1)} %all_to_all.27.in_ref, bf16[8,32,4096]{2,1,0:T(8,128)(2,1)S(1)} %bitcast.10, f32[1,4096]{1,0:T(1,128)S(1)} %bitcast.13, f32[8,4096]{1,0:T(8,128)S(1)} %copy-done.2, ...), custom_call_target="tpu_custom_call" | custom-call | flops 10000000 | bytes 5197856 | tf_op jit(solution)/shard_map/pallas_call | solution.py:261
  120.4 5.2 %all-to-all-done.4 = f32[8,32,128]{2,1,0:T(8,128)S(1)} async-done(((f32[8,32,128]{2,1,0:T(8,128)}), f32[8,32,128]{2,1,0:T(8,128)S(1)}, u32[]{:S(2)}, u32[]{:S(2)}) %all-to-all-start.4) | async-done | bytes 131104 | tf_op jit(solution)/shard_map/all_to_all | solution.py:353
  125.6 0.6 reduce_sum.9
Async XLA Ops:
  31.1 55.2 %copy-start.1 = (f32[4096]{0:T(1024)S(1)}, f32[4096]{0:T(1024)}, u32[]{:S(2)}) copy-start(f32[4096]{0:T(1024)} %param.8) | copy-start | bytes 49156
  31.1 5.7 %collective-permute-start = (bf16[32,40,128]{2,1,0:T(8,128)(2,1)S(1)}, bf16[32,40,128]{2,1,0:T(8,128)(2,1)S(1)}, u32[]{:S(2)}, u32[]{:S(2)}) collective-permute-start(bf16[32,40,128]{2,1,0:T(8,128)(2,1)S(1)} %all_to_all.25.refs_0_.refs_3_), channel_id=1, source_target_pairs={{0,1},{1,0},{2,3},{3,2},{4,5},{5,4},{6,7},{7,6},{8,9},{9,8},{10,11... | collective-permute-start | bytes 983048 | tf_op jit(solution)/shard_map/ppermute | solution.py:323
  38.5 23.5 %all-to-all-start.1 = ((f32[32,8,640]{2,1,0:T(8,128)}), f32[32,8,640]{2,1,0:T(8,128)S(1)}, u32[]{:S(2)}, u32[]{:S(2)}) async-start(f32[32,8,640]{2,1,0:T(8,128)} %shard_map.94), calls=%async_computation.1 | async-start | bytes 1310720 | tf_op jit(solution)/shard_map/all_to_all | solution.py:292
  42.4 73.9 %copy-start = (bf16[1,8,32,4096]{3,2,1,0:T(8,128)(2,1)S(1)}, bf16[1,8,32,4096]{3,2,1,0:T(8,128)(2,1)}, u32[]{:S(2)}) copy-start(bf16[1,8,32,4096]{3,2,1,0:T(8,128)(2,1)} %x_hbm.1) | copy-start | bytes 6291460
  42.5 73.8 %copy-start.2 = (f32[8,4096]{1,0:T(8,128)S(1)}, f32[8,4096]{1,0:T(8,128)}, u32[]{:S(2)}) copy-start(f32[8,4096]{1,0:T(8,128)} %get-tuple-element.12.unit_ref) | copy-start | bytes 393220
  62.3 54.1 %copy-start.3 = (f32[8,32,128]{2,1,0:T(8,128)S(1)}, f32[8,32,128]{2,1,0:T(8,128)}, u32[]{:S(2)}) copy-start(f32[8,32,128]{2,1,0:T(8,128)} %get-tuple-element.13.inv_ref) | copy-start | bytes 393220
  62.3 54.1 %copy-start.4 = (f32[8,128]{1,0:T(8,128)S(1)}, f32[8,128]{1,0:T(8,128)}, u32[]{:S(2)}) copy-start(f32[8,128]{1,0:T(8,128)} %get-tuple-element.14.norm_ref) | copy-start | bytes 12292
  62.3 54.1 %copy-start.5 = (s32[1,8]{1,0:T(1,128)S(1)}, s32[1,8]{1,0:T(1,128)}, u32[]{:S(2)}) copy-start(s32[1,8]{1,0:T(1,128)} %len_hbm.1) | copy-start | bytes 100
  80.8 5.5 %collective-permute-start.1 = (bf16[32,8,640]{2,1,0:T(8,128)(2,1)S(1)}, bf16[32,8,640]{2,1,0:T(8,128)(2,1)S(1)}, u32[]{:S(2)}, u32[]{:S(2)}) collective-permute-start(bf16[32,8,640]{2,1,0:T(8,128)(2,1)S(1)} %all_to_all.26.refs_1_), channel_id=1, source_target_pairs={{0,1},{1,0},{2,3},{3,2},{4,5},{5,4},{6,7},{7,6},{8,9},{9,8},{10,11... | collective-permute-start | bytes 983048 | tf_op jit(solution)/shard_map/ppermute | solution.py:340
  106.5 19.1 %all-to-all-start.4 = ((f32[8,32,128]{2,1,0:T(8,128)}), f32[8,32,128]{2,1,0:T(8,128)S(1)}, u32[]{:S(2)}, u32[]{:S(2)}) async-start(f32[8,32,128]{2,1,0:T(8,128)} %shard_map.98), calls=%async_computation.4 | async-start | bytes 262144 | tf_op jit(solution)/shard_map/all_to_all | solution.py:353

commit v5 on v4

--- a/solution.py
+++ b/solution.py
@@ -11,6 +11,7 @@
 LANES = 128
 F32 = jnp.float32
 BF16 = jnp.bfloat16
+F16 = jnp.float16
 BY_COLUMN = (((0,), (0,)), ((), ()))
 BY_ROW = (((1,), (1,)), ((), ()))
 
@@ -115,7 +116,8 @@
     p = jnp.concatenate([rows_of(a, 2 * q, 3 * q), rows_of(b, 2 * q, 3 * q)], axis=0).astype(BF16)
     m = jnp.concatenate([rows_of(a, 3 * q, 5 * q), rows_of(b, 3 * q, 5 * q)], axis=0).astype(BF16)
     ids = ids_of(a, q, hard)
-    sim_ref[:, :, :n] = lax.dot_general(e, p, BY_ROW, preferred_element_type=F32).reshape(chips, q, n)
+    sim = lax.dot_general(e, p, BY_ROW, preferred_element_type=F32) / TEMPERATURE
+    sim_ref[:, :, :n] = sim.reshape(chips, q, n)
     pool = lax.dot_general(e, m, BY_ROW, preferred_element_type=F32)
     tail = jnp.zeros((half, LANES), F32)
     within, tile = ids & (LANES - 1), ids >> 7
@@ -125,14 +127,14 @@
         )
         tail = jnp.where(tile == k, picked, tail)
     lane = lax.broadcasted_iota(jnp.int32, (half, LANES), 1)
-    tail = jnp.where(lane < hard, tail, 0.0)
+    tail = jnp.where(lane < hard, tail / TEMPERATURE, 0.0)
     sim_ref[:, :, n:] = tail.reshape(chips, q, LANES)
 
 
 def softmax_kernel(hard, chip_ref, in_ref, out_ref):
     copies, q, width = out_ref.shape
     n = width - LANES
-    scores = jnp.sum(in_ref[...], axis=0) / TEMPERATURE
+    scores = in_ref[...]
     column = lax.broadcasted_iota(jnp.int32, (q, width), 1)
     row = lax.broadcasted_iota(jnp.int32, (q, width), 0)
     exps = jnp.where(column < n + hard, jnp.exp(scores), 0.0)
@@ -328,11 +330,11 @@
         [got, gotx],
         100_000_000,
     )
-    pieces = among_chips(part)
+    scores = jnp.sum(among_chips(part.astype(F16)).astype(F32), axis=0)
     (sent,) = call(
         bound(softmax_kernel),
         [shape((chips, queries, q_all + LANES), BF16)],
-        [chip, pieces],
+        [chip, scores],
         1_000_000,
         (0,),
     )

time: 129 us -> 122 us (0.946)
  waiting for transfers between devices: 27.3 us -> 21.3 us
    all_to_all x1, waiting for transfers between devices: 19.6 us -> 13.6 us  [among_chips(): lax.all_to_all(x, 'dp', 0, 0, tiled=True, axis_index_groups=same_core)]
where the time goes in v5:
time: 122 us; the launch traced here: 119 us
  blocking collectives  60.4 us (50%)
  starting transfers between devices  22.5 us (18%)
  waiting for transfers between devices  21.3 us (17%)
  Pallas kernels  12.9 us (11%)
  other arithmetic  1.44 us (1%)
    all_to_all x3, blocking collectives, among_chips(): lax.all_to_all(x, 'dp', 0, 0, tiled=True, axis_index_groups=same_core)  60.4 us
    all_to_all x1, waiting for transfers between devices, among_chips(): lax.all_to_all(x, 'dp', 0, 0, tiled=True, axis_index_groups=same_core)  13.6 us
    pallas_call x6, Pallas kernels, call(): pl.pallas_call(kernel, out_shape=list(outs), in_specs=[pl.BlockSpec(memor...  12.9 us
    all_to_all x1, starting transfers between devices, local(): gain_groups = lax.all_to_all(gain_sent, 'rep', 0, 0, tiled=True)  9.77 us
    all_to_all x1, waiting for transfers between devices, local(): gain_groups = lax.all_to_all(gain_sent, 'rep', 0, 0, tiled=True)  5.22 us
    ppermute x1, starting transfers between devices, local(): gotx = lax.ppermute(got, 'dp', pair)  4.51 us
    ppermute x1, starting transfers between devices, local(): weightsx = lax.ppermute(weights, 'dp', pair)  4.32 us
    all_to_all x1, starting transfers between devices, among_chips(): lax.all_to_all(x, 'dp', 0, 0, tiled=True, axis_index_groups=same_core)  3.87 us
  transfers between devices with their start and end apart: 4, of which 4 were waited for; matrix products, arithmetic and copies ran while one was open for 0% of the time, Pallas kernels for 3%

profile of v5, /device:TPU:1, one launch (start us, length us, event | category | flops | bytes accessed | tf_op | source)
XLA Modules:
  0.0 119.3 jit_solution(15687817428137267019)
XLA Ops:
  0.6 4.0 %shard_map.93 = (bf16[32,40,128]{2,1,0:T(8,128)(2,1)}, f32[8,4096]{1,0:T(8,128)}, f32[8,32,128]{2,1,0:T(8,128)}, f32[8,128]{1,0:T(8,128)}) custom-call(s32[1]{0:T(128)S(6)} %rem.9.core_ref, s32[1,8]{1,0:T(1,128)} %len_hbm.1, bf16[1,8,32,4096]{3,2,1,0:T(8,128)(2,1)} %x_hbm.1, f32[1,4096]{1,0:T(1,128)} %bitcast.11, bf16[1,8,4096]{2,1,0:T(8,128)(2,1)} %pos_hbm.1, ...), custom_call_target="tpu_custom_call" | custom-call | flops 8000000 | bytes 2904324 | tf_op jit(solution)/shard_map/pallas_call | solution.py:263
  4.6 26.5 %all_to_all.25.refs_0_.refs_3_ = bf16[32,40,128]{2,1,0:T(8,128)(2,1)S(1)} all-to-all(bf16[32,40,128]{2,1,0:T(8,128)(2,1)} %get-tuple-element.11), channel_id=1, replica_groups={{0,2,4,6,8,10,12,14,16,18,20,22,24,26,28,30,32,34,36,38,40,42,44,46,48,..., dimensions={0} | all-to-all | bytes 655360 | tf_op jit(solution)/shard_map/all_to_all | solution.py:294
  31.1 0.0 copy-start.1
  31.1 4.5 %collective-permute-start = (bf16[32,40,128]{2,1,0:T(8,128)(2,1)S(1)}, bf16[32,40,128]{2,1,0:T(8,128)(2,1)S(1)}, u32[]{:S(2)}, u32[]{:S(2)}) collective-permute-start(bf16[32,40,128]{2,1,0:T(8,128)(2,1)S(1)} %all_to_all.25.refs_0_.refs_3_), channel_id=1, source_target_pairs={{0,1},{1,0},{2,3},{3,2},{4,5},{5,4},{6,7},{7,6},{8,9},{9,8},{10,11... | collective-permute-start | bytes 983048 | tf_op jit(solution)/shard_map/ppermute | solution.py:325
  35.7 1.2 %collective-permute-done.refs_1_.refs_4_ = bf16[32,40,128]{2,1,0:T(8,128)(2,1)S(1)} collective-permute-done((bf16[32,40,128]{2,1,0:T(8,128)(2,1)S(1)}, bf16[32,40,128]{2,1,0:T(8,128)(2,1)S(1)}, u32[]{:S(2)}, u32[]{:S(2)}) %collective-permute-start) | collective-permute-done | bytes 327712 | tf_op jit(solution)/shard_map/ppermute | solution.py:325
  36.9 0.8 shard_map.94
  37.7 0.8 convert_element_type.6
  38.5 3.9 %all-to-all-start.1 = ((f16[32,8,640]{2,1,0:T(8,128)(2,1)}), f16[32,8,640]{2,1,0:T(8,128)(2,1)S(1)}, u32[]{:S(2)}, u32[]{:S(2)}) async-start(f16[32,8,640]{2,1,0:T(8,128)(2,1)} %convert_element_type.6), calls=%async_computation.1 | async-start | bytes 655360 | tf_op jit(solution)/shard_map/all_to_all | solution.py:294
  42.4 13.6 %all-to-all-done.1 = f16[32,8,640]{2,1,0:T(8,128)(2,1)S(1)} async-done(((f16[32,8,640]{2,1,0:T(8,128)(2,1)}), f16[32,8,640]{2,1,0:T(8,128)(2,1)S(1)}, u32[]{:S(2)}, u32[]{:S(2)}) %all-to-all-start.1) | async-done | bytes 327712 | tf_op jit(solution)/shard_map/all_to_all | solution.py:294
  56.0 0.1 convert_reduce_fusion.refs_1_
  56.0 0.0 copy-start
  56.0 0.0 copy-start.2
  56.1 0.0 copy-start.3
  56.1 0.0 copy-start.4
  56.1 0.0 copy-start.5
  56.1 0.2 shard_map.95
  56.3 17.5 %all_to_all.26.refs_1_ = bf16[32,8,640]{2,1,0:T(8,128)(2,1)S(1)} all-to-all(bf16[32,8,640]{2,1,0:T(8,128)(2,1)S(1)} %shard_map.95), channel_id=1, replica_groups={{0,2,4,6,8,10,12,14,16,18,20,22,24,26,28,30,32,34,36,38,40,42,44,46,48,..., dimensions={0} | all-to-all | bytes 655360 | tf_op jit(solution)/shard_map/all_to_all | solution.py:294
  73.8 4.3 %collective-permute-start.1 = (bf16[32,8,640]{2,1,0:T(8,128)(2,1)S(1)}, bf16[32,8,640]{2,1,0:T(8,128)(2,1)S(1)}, u32[]{:S(2)}, u32[]{:S(2)}) collective-permute-start(bf16[32,8,640]{2,1,0:T(8,128)(2,1)S(1)} %all_to_all.26.refs_1_), channel_id=1, source_target_pairs={{0,1},{1,0},{2,3},{3,2},{4,5},{5,4},{6,7},{7,6},{8,9},{9,8},{10,11... | collective-permute-start | bytes 983048 | tf_op jit(solution)/shard_map/ppermute | solution.py:342
  78.1 1.2 %collective-permute-done.1.refs_2_ = bf16[32,8,640]{2,1,0:T(8,128)(2,1)S(1)} collective-permute-done((bf16[32,8,640]{2,1,0:T(8,128)(2,1)S(1)}, bf16[32,8,640]{2,1,0:T(8,128)(2,1)S(1)}, u32[]{:S(2)}, u32[]{:S(2)}) %collective-permute-start.1) | collective-permute-done | bytes 327712 | tf_op jit(solution)/shard_map/ppermute | solution.py:342
  79.3 0.0 copy-done.1
  79.3 3.1 %shard_map.96 = bf16[32,40,128]{2,1,0:T(8,128)(2,1)S(1)} custom-call(s32[1]{0:T(128)S(6)} %div.18.refs_0_, bf16[32,8,640]{2,1,0:T(8,128)(2,1)S(1)} %all_to_all.26.refs_1_, bf16[32,8,640]{2,1,0:T(8,128)(2,1)S(1)} %collective-permute-done.1.refs_2_, bf16[32,40,128]{2,1,0:T(8,128)(2,1)S(1)} %all_to_all.25.refs_0_.refs_3_, ...), custom_call_target="tpu_custom_call" | custom-call | flops 400000000 | bytes 1654788 | tf_op jit(solution)/shard_map/pallas_call | solution.py:263
  82.5 16.4 %all_to_all.27.in_ref = bf16[32,40,128]{2,1,0:T(8,128)(2,1)S(1)} all-to-all(bf16[32,40,128]{2,1,0:T(8,128)(2,1)S(1)} %shard_map.96), channel_id=1, replica_groups={{0,2,4,6,8,10,12,14,16,18,20,22,24,26,28,30,32,34,36,38,40,42,44,46,48,..., dimensions={0} | all-to-all | bytes 655360 | tf_op jit(solution)/shard_map/all_to_all | solution.py:294
  98.8 0.7 shard_map.98
  99.5 9.8 %all-to-all-start.4 = ((f32[8,32,128]{2,1,0:T(8,128)}), f32[8,32,128]{2,1,0:T(8,128)S(1)}, u32[]{:S(2)}, u32[]{:S(2)}) async-start(f32[8,32,128]{2,1,0:T(8,128)} %shard_map.98), calls=%async_computation.4 | async-start | bytes 262144 | tf_op jit(solution)/shard_map/all_to_all | solution.py:355
  109.3 0.0 copy-done
  109.3 0.0 copy-done.2
  109.3 0.0 copy-done.3
  109.3 0.0 copy-done.4
  109.3 0.0 copy-done.5
  109.4 4.1 %shard_map.97 = (bf16[8,32,4096]{2,1,0:T(8,128)(2,1)}, f32[8,4096]{1,0:T(8,128)}, f32[16,4096]{1,0:T(8,128)}) custom-call(s32[8]{0:T(128)S(1)} %bitcast.14, bf16[32,40,128]{2,1,0:T(8,128)(2,1)S(1)} %all_to_all.27.in_ref, bf16[8,32,4096]{2,1,0:T(8,128)(2,1)S(1)} %bitcast.10, f32[1,4096]{1,0:T(1,128)S(1)} %bitcast.13, f32[8,4096]{1,0:T(8,128)S(1)} %copy-done.2, ...), custom_call_target="tpu_custom_call" | custom-call | flops 10000000 | bytes 5197856 | tf_op jit(solution)/shard_map/pallas_call | solution.py:263
  113.4 5.2 %all-to-all-done.4 = f32[8,32,128]{2,1,0:T(8,128)S(1)} async-done(((f32[8,32,128]{2,1,0:T(8,128)}), f32[8,32,128]{2,1,0:T(8,128)S(1)}, u32[]{:S(2)}, u32[]{:S(2)}) %all-to-all-start.4) | async-done | bytes 131104 | tf_op jit(solution)/shard_map/all_to_all | solution.py:355
  118.6 0.6 reduce_sum.19
Async XLA Ops:
  31.1 48.2 %copy-start.1 = (f32[4096]{0:T(1024)S(1)}, f32[4096]{0:T(1024)}, u32[]{:S(2)}) copy-start(f32[4096]{0:T(1024)} %param.8) | copy-start | bytes 49156
  31.1 5.7 %collective-permute-start = (bf16[32,40,128]{2,1,0:T(8,128)(2,1)S(1)}, bf16[32,40,128]{2,1,0:T(8,128)(2,1)S(1)}, u32[]{:S(2)}, u32[]{:S(2)}) collective-permute-start(bf16[32,40,128]{2,1,0:T(8,128)(2,1)S(1)} %all_to_all.25.refs_0_.refs_3_), channel_id=1, source_target_pairs={{0,1},{1,0},{2,3},{3,2},{4,5},{5,4},{6,7},{7,6},{8,9},{9,8},{10,11... | collective-permute-start | bytes 983048 | tf_op jit(solution)/shard_map/ppermute | solution.py:325
  38.5 17.5 %all-to-all-start.1 = ((f16[32,8,640]{2,1,0:T(8,128)(2,1)}), f16[32,8,640]{2,1,0:T(8,128)(2,1)S(1)}, u32[]{:S(2)}, u32[]{:S(2)}) async-start(f16[32,8,640]{2,1,0:T(8,128)(2,1)} %convert_element_type.6), calls=%async_computation.1 | async-start | bytes 655360 | tf_op jit(solution)/shard_map/all_to_all | solution.py:294
  56.0 53.3 %copy-start = (bf16[1,8,32,4096]{3,2,1,0:T(8,128)(2,1)S(1)}, bf16[1,8,32,4096]{3,2,1,0:T(8,128)(2,1)}, u32[]{:S(2)}) copy-start(bf16[1,8,32,4096]{3,2,1,0:T(8,128)(2,1)} %x_hbm.1) | copy-start | bytes 6291460
  56.0 53.3 %copy-start.2 = (f32[8,4096]{1,0:T(8,128)S(1)}, f32[8,4096]{1,0:T(8,128)}, u32[]{:S(2)}) copy-start(f32[8,4096]{1,0:T(8,128)} %get-tuple-element.12.unit_ref) | copy-start | bytes 393220
  56.1 53.3 %copy-start.3 = (f32[8,32,128]{2,1,0:T(8,128)S(1)}, f32[8,32,128]{2,1,0:T(8,128)}, u32[]{:S(2)}) copy-start(f32[8,32,128]{2,1,0:T(8,128)} %get-tuple-element.13.inv_ref) | copy-start | bytes 393220
  56.1 53.3 %copy-start.4 = (f32[8,128]{1,0:T(8,128)S(1)}, f32[8,128]{1,0:T(8,128)}, u32[]{:S(2)}) copy-start(f32[8,128]{1,0:T(8,128)} %get-tuple-element.14.norm_ref) | copy-start | bytes 12292
  56.1 53.3 %copy-start.5 = (s32[1,8]{1,0:T(1,128)S(1)}, s32[1,8]{1,0:T(1,128)}, u32[]{:S(2)}) copy-start(s32[1,8]{1,0:T(1,128)} %len_hbm.1) | copy-start | bytes 100
  73.8 5.6 %collective-permute-start.1 = (bf16[32,8,640]{2,1,0:T(8,128)(2,1)S(1)}, bf16[32,8,640]{2,1,0:T(8,128)(2,1)S(1)}, u32[]{:S(2)}, u32[]{:S(2)}) collective-permute-start(bf16[32,8,640]{2,1,0:T(8,128)(2,1)S(1)} %all_to_all.26.refs_1_), channel_id=1, source_target_pairs={{0,1},{1,0},{2,3},{3,2},{4,5},{5,4},{6,7},{7,6},{8,9},{9,8},{10,11... | collective-permute-start | bytes 983048 | tf_op jit(solution)/shard_map/ppermute | solution.py:342
  99.5 19.1 %all-to-all-start.4 = ((f32[8,32,128]{2,1,0:T(8,128)}), f32[8,32,128]{2,1,0:T(8,128)S(1)}, u32[]{:S(2)}, u32[]{:S(2)}) async-start(f32[8,32,128]{2,1,0:T(8,128)} %shard_map.98), calls=%async_computation.4 | async-start | bytes 262144 | tf_op jit(solution)/shard_map/all_to_all | solution.py:355

commit v6 on v5

--- a/solution.py
+++ b/solution.py
@@ -18,7 +18,7 @@
 
 def embed_kernel(
     core_ref, len_hbm, x_hbm, gain_hbm, pos_hbm, pool_hbm, ids_hbm, out_ref, unit_ref, inv_ref, norm_ref,
-    len_ref, x_ref, gain_ref, pos_ref, pool_ref, ids_ref, weight_ref, x_sem, small_sem,
+    len_ref, x_ref, gain_ref, pos_ref, pool_ref, ids_ref, row_ref, x_sem, small_sem,
 ):
     queries, width = unit_ref.shape
     tokens = x_ref.shape[1]
@@ -56,18 +56,23 @@
         inv_ref[i] = jnp.broadcast_to(inv, (tokens, LANES))
         length = len_ref[0, i]
         weight = jnp.where(token < length, inv, 0.0) / length.astype(F32)
-        weight_ref[i] = jnp.broadcast_to(weight, (tokens, LANES))
+        for k in range(chunks):
+            cols = slice(k * LANES, (k + 1) * LANES)
+            v = x_ref[i, :, cols].astype(F32) * weight
+            row_ref[i, :, cols] = jnp.sum(v, axis=0, keepdims=True)
         return carry
 
     lax.fori_loop(0, queries, one_query, 0)
     for copy in small[1:]:
         copy.wait()
+    square = jnp.zeros((queries, LANES), F32)
     for k in range(chunks):
         cols = slice(k * LANES, (k + 1) * LANES)
-        v = jnp.sum(x_ref[:, :, cols].astype(F32) * weight_ref[...], axis=1)
-        unit_ref[:, cols] = v * gain_ref[:, cols]
-    pooled = unit_ref[...]
-    norm = lax.rsqrt(jnp.sum(pooled * pooled, axis=1, keepdims=True) + 1e-06)
+        pooled = jnp.concatenate([row_ref[i, :, cols] for i in range(queries)], axis=0)
+        pooled = pooled * gain_ref[:, cols]
+        unit_ref[:, cols] = pooled
+        square += pooled * pooled
+    norm = lax.rsqrt(jnp.sum(square, axis=1, keepdims=True) + 1e-06)
     norm_ref[...] = jnp.broadcast_to(norm, norm_ref.shape)
     ids = ids_ref[:, 0, :]
     hard = ids.shape[0]
@@ -149,47 +154,65 @@
         out_ref[k] = sent
 
 
-def slices_kernel(hard, chip_ref, w_ref, wx_ref, got_ref, gotx_ref, gain_ref, out_ref):
-    chips, q, width = w_ref.shape
-    n = width - LANES
-    half = chips * q
-    w = w_ref[...].astype(F32).reshape(half, width)
-    wx = wx_ref[...].astype(F32).reshape(half, width)
-    a = got_ref[...].astype(F32)
-    b = gotx_ref[...].astype(F32)
-    tail = jnp.concatenate([w[:, n:], wx[:, n:]], axis=0)
-    from_own = jnp.concatenate([w[:, :half], wx[:, half:n]], axis=0).astype(BF16)
-    from_other = jnp.concatenate([w[:, half:n], wx[:, :half]], axis=0).astype(BF16)
-    idsx = ids_of(b, q, hard)
-    ids = jnp.concatenate([ids_of(a, q, hard), idsx ^ n], axis=0)
-    column = lax.broadcasted_iota(jnp.int32, (n, n), 1)
-    own_spread = jnp.zeros((n, n), F32)
-    other_spread = jnp.zeros((n, n), F32)
+def share(w, ids, hard, own_cols, other_cols, a, b, e, pos):
+    q = a.shape[1] // 5
+    half = w.shape[0]
+    n = 2 * half
+    tail = w[:, n:]
+    from_own, from_other = w[:, own_cols].astype(BF16), w[:, other_cols].astype(BF16)
+    column = lax.broadcasted_iota(jnp.int32, (half, n), 1)
+    own_spread = jnp.zeros((half, n), F32)
+    other_spread = jnp.zeros((half, n), F32)
     for m in range(hard):
         one, weight = ids[:, m : m + 1], tail[:, m : m + 1]
         own_spread += jnp.where(column == one, weight, 0.0)
         other_spread += jnp.where(column == one - n, weight, 0.0)
     own_spread = own_spread.astype(BF16)
     other_spread = other_spread.astype(BF16)
+
+    def dot(left, block, first, last):
+        return jnp.dot(left, rows_of(block, first, last).astype(BF16), preferred_element_type=F32)
+
+    numerator = dot(from_own, a, 2 * q, 3 * q) + dot(from_other, b, 2 * q, 3 * q)
+    numerator += dot(own_spread, a, 3 * q, 5 * q) + dot(other_spread, b, 3 * q, 5 * q)
     along = tail[:, hard : hard + 1] + tail[:, hard + 1 : hard + 2]
-    e32 = jnp.concatenate([rows_of(a, 0, q), rows_of(b, 0, q)], axis=0)
-    e = e32.astype(BF16)
-    own_pos, other_pos = rows_of(a, 2 * q, 3 * q), rows_of(b, 2 * q, 3 * q)
-
-    def dot(left, right):
-        return jnp.dot(left, right.astype(BF16), preferred_element_type=F32)
-
-    numerator = dot(from_own, own_pos) + dot(from_other, other_pos)
-    numerator += dot(own_spread, rows_of(a, 3 * q, 5 * q))
-    numerator += dot(other_spread, rows_of(b, 3 * q, 5 * q))
-    pos = jnp.concatenate([own_pos, other_pos], axis=0)
-    emb_grad = (numerator - pos) / TEMPERATURE - along * e32
-    key = lax.dot_general(from_own, e, BY_COLUMN, preferred_element_type=F32)
-    key = (key - e32[:half]) / TEMPERATURE
-    pool = lax.dot_general(own_spread, e, BY_COLUMN, preferred_element_type=F32)
-    pool = pool * (POOL_SCALE / TEMPERATURE)
-    gain = gain_ref[pl.ds(chip_ref[0], 1), :]
-    gain_part = jnp.sum(emb_grad * e32, axis=0, keepdims=True) / gain
+    emb_grad = (numerator - pos) / TEMPERATURE - along * e
+    eh = e.astype(BF16)
+    key = lax.dot_general(from_own, eh, BY_COLUMN, preferred_element_type=F32)
+    pool = lax.dot_general(own_spread, eh, BY_COLUMN, preferred_element_type=F32)
+    return emb_grad, key, pool, jnp.sum(emb_grad * e, axis=0, keepdims=True)
+
+
+def own_kernel(hard, w_ref, got_ref, gotx_ref, emb_ref, key_ref, pool_ref, gain_ref):
+    chips, q, width = w_ref.shape
+    half = chips * q
+    a = got_ref[...].astype(F32)
+    b = gotx_ref[...].astype(F32)
+    w = w_ref[...].astype(F32).reshape(half, width)
+    e = rows_of(a, 0, q)
+    emb_ref[...], key, pool_ref[...], gain_ref[...] = share(
+        w, ids_of(a, q, hard), hard, slice(0, half), slice(half, 2 * half), a, b, e, rows_of(a, 2 * q, 3 * q)
+    )
+    key_ref[...] = key - e
+
+
+def slices_kernel(
+    hard, chip_ref, wx_ref, got_ref, gotx_ref, gain_ref, emb_ref, key_ref, pool_ref, part_ref, out_ref
+):
+    chips, q, width = wx_ref.shape
+    half = chips * q
+    a = got_ref[...].astype(F32)
+    b = gotx_ref[...].astype(F32)
+    w = wx_ref[...].astype(F32).reshape(half, width)
+    ids = ids_of(b, q, hard) ^ (2 * half)
+    e = rows_of(b, 0, q)
+    _, key, pool, gain_part = share(
+        w, ids, hard, slice(half, 2 * half), slice(0, half), a, b, e, rows_of(b, 2 * q, 3 * q)
+    )
+    emb_grad = emb_ref[...]
+    key = (key + key_ref[...]) / TEMPERATURE
+    pool = (pool + pool_ref[...]) * (POOL_SCALE / TEMPERATURE)
+    gain_part = (gain_part + part_ref[...]) / gain_ref[pl.ds(chip_ref[0], 1), :]
     gain_high = gain_part.astype(BF16).astype(F32)
     row = lax.broadcasted_iota(jnp.int32, (q, LANES), 0)
     gain_rows = jnp.where(row == 0, gain_high, jnp.where(row == 1, gain_part - gain_high, 0.0))
@@ -315,7 +338,7 @@
             pltpu.VMEM((1, queries, width), BF16),
             pltpu.VMEM((1, 2 * queries, width), BF16),
             pltpu.VMEM((hard, 1, queries), jnp.int32),
-            pltpu.VMEM((queries, tokens, LANES), F32),
+            pltpu.VMEM((queries, 1, width), F32),
             pltpu.SemaphoreType.DMA((queries,)),
             pltpu.SemaphoreType.DMA((5,)),
         ],
@@ -341,11 +364,23 @@
     weights = among_chips(sent)
     weightsx = lax.ppermute(weights, "dp", pair)
 
+    half = q_all // 2
+    shares = call(
+        bound(own_kernel),
+        [
+            shape((half, LANES), F32),
+            shape((half, LANES), F32),
+            shape((q_all, LANES), F32),
+            shape((1, LANES), F32),
+        ],
+        [weights, got, gotx],
+        200_000_000,
+    )
     (back,) = call(
         bound(slices_kernel),
         [shape((chips, 5 * queries, LANES), BF16)],
-        [chip, weights, weightsx, got, gotx, gain_tiles],
-        400_000_000,
+        [chip, weightsx, got, gotx, gain_tiles, *shares],
+        200_000_000,
         (0,),
     )
     home = among_chips(back)

time: 122 us -> 120 us (0.984)
    ppermute x1, waiting for transfers between devices: 1.23 us -> 0.01 us  [local(): weightsx = lax.ppermute(weights, 'dp', pair)]
    pallas_call x6 -> x7, Pallas kernels: 12.9 us -> 12.8 us  [call(): pl.pallas_call(kernel, out_shape=list(outs), in_specs=[pl.BlockSpec(memor...]
  transfers between devices with their start and end apart: 4 -> 4, of which waited for: 4 -> 3; matrix products, arithmetic and copies ran while one was open for 0% -> 0% of each run, Pallas kernels for 3% -> 5%
where the time goes in v6:
time: 120 us; the launch traced here: 118 us
  blocking collectives  60.7 us (51%)
  starting transfers between devices  22.5 us (19%)
  waiting for transfers between devices  20.1 us (17%)
  Pallas kernels  12.8 us (11%)
  other arithmetic  1.44 us (1%)
    all_to_all x3, blocking collectives, among_chips(): lax.all_to_all(x, 'dp', 0, 0, tiled=True, axis_index_groups=same_core)  60.7 us
    all_to_all x1, waiting for transfers between devices, among_chips(): lax.all_to_all(x, 'dp', 0, 0, tiled=True, axis_index_groups=same_core)  13.6 us
    pallas_call x7, Pallas kernels, call(): pl.pallas_call(kernel, out_shape=list(outs), in_specs=[pl.BlockSpec(memor...  12.8 us
    all_to_all x1, starting transfers between devices, local(): gain_groups = lax.all_to_all(gain_sent, 'rep', 0, 0, tiled=True)  9.76 us
    all_to_all x1, waiting for transfers between devices, local(): gain_groups = lax.all_to_all(gain_sent, 'rep', 0, 0, tiled=True)  5.22 us
    ppermute x1, starting transfers between devices, local(): weightsx = lax.ppermute(weights, 'dp', pair)  4.46 us
    ppermute x1, starting transfers between devices, local(): gotx = lax.ppermute(got, 'dp', pair)  4.38 us
    all_to_all x1, starting transfers between devices, among_chips(): lax.all_to_all(x, 'dp', 0, 0, tiled=True, axis_index_groups=same_core)  3.88 us
  transfers between devices with their start and end apart: 4, of which 3 were waited for; matrix products, arithmetic and copies ran while one was open for 0% of the time, Pallas kernels for 5%

profile of v6, /device:TPU:1, one launch (start us, length us, event | category | flops | bytes accessed | tf_op | source)
XLA Modules:
  0.0 118.3 jit_solution(8001403676158660551)
XLA Ops:
  0.6 3.6 %shard_map.93 = (bf16[32,40,128]{2,1,0:T(8,128)(2,1)}, f32[8,4096]{1,0:T(8,128)}, f32[8,32,128]{2,1,0:T(8,128)}, f32[8,128]{1,0:T(8,128)}) custom-call(s32[1]{0:T(128)S(6)} %rem.9.core_ref, s32[1,8]{1,0:T(1,128)} %len_hbm.1, bf16[1,8,32,4096]{3,2,1,0:T(8,128)(2,1)} %x_hbm.1, f32[1,4096]{1,0:T(1,128)} %bitcast.11, bf16[1,8,4096]{2,1,0:T(8,128)(2,1)} %pos_hbm.1, ...), custom_call_target="tpu_custom_call" | custom-call | flops 8000000 | bytes 2904324 | tf_op jit(solution)/shard_map/pallas_call | solution.py:286
  4.3 26.5 %all_to_all.25.refs_0_.refs_1_.refs_2_ = bf16[32,40,128]{2,1,0:T(8,128)(2,1)S(1)} all-to-all(bf16[32,40,128]{2,1,0:T(8,128)(2,1)} %get-tuple-element.15), channel_id=1, replica_groups={{0,2,4,6,8,10,12,14,16,18,20,22,24,26,28,30,32,34,36,38,40,42,44,46,48,..., dimensions={0} | all-to-all | bytes 655360 | tf_op jit(solution)/shard_map/all_to_all | solution.py:317
  30.8 4.4 %collective-permute-start = (bf16[32,40,128]{2,1,0:T(8,128)(2,1)S(1)}, bf16[32,40,128]{2,1,0:T(8,128)(2,1)S(1)}, u32[]{:S(2)}, u32[]{:S(2)}) collective-permute-start(bf16[32,40,128]{2,1,0:T(8,128)(2,1)S(1)} %all_to_all.25.refs_0_.refs_1_.refs_2_), channel_id=1, source_target_pairs={{0,1},{1,0},{2,3},{3,2},{4,5},{5,4},{6,7},{7,6},{8,9},{9,8},{10,11... | collective-permute-start | bytes 983048 | tf_op jit(solution)/shard_map/ppermute | solution.py:348
  35.2 1.2 %collective-permute-done.refs_1_.refs_2_.refs_3_ = bf16[32,40,128]{2,1,0:T(8,128)(2,1)S(1)} collective-permute-done((bf16[32,40,128]{2,1,0:T(8,128)(2,1)S(1)}, bf16[32,40,128]{2,1,0:T(8,128)(2,1)S(1)}, u32[]{:S(2)}, u32[]{:S(2)}) %collective-permute-start) | collective-permute-done | bytes 327712 | tf_op jit(solution)/shard_map/ppermute | solution.py:348
  36.4 0.8 shard_map.94
  37.2 0.0 copy-start.1
  37.2 0.8 convert_element_type.6
  38.0 3.9 %all-to-all-start.1 = ((f16[32,8,640]{2,1,0:T(8,128)(2,1)}), f16[32,8,640]{2,1,0:T(8,128)(2,1)S(1)}, u32[]{:S(2)}, u32[]{:S(2)}) async-start(f16[32,8,640]{2,1,0:T(8,128)(2,1)} %convert_element_type.6), calls=%async_computation.1 | async-start | bytes 655360 | tf_op jit(solution)/shard_map/all_to_all | solution.py:317
  41.9 13.6 %all-to-all-done.1 = f16[32,8,640]{2,1,0:T(8,128)(2,1)S(1)} async-done(((f16[32,8,640]{2,1,0:T(8,128)(2,1)}), f16[32,8,640]{2,1,0:T(8,128)(2,1)S(1)}, u32[]{:S(2)}, u32[]{:S(2)}) %all-to-all-start.1) | async-done | bytes 327712 | tf_op jit(solution)/shard_map/all_to_all | solution.py:317
  55.5 0.1 convert_reduce_fusion.refs_1_
  55.6 0.2 shard_map.95
  55.8 17.3 %all_to_all.26.refs_0_ = bf16[32,8,640]{2,1,0:T(8,128)(2,1)S(1)} all-to-all(bf16[32,8,640]{2,1,0:T(8,128)(2,1)S(1)} %shard_map.95), channel_id=1, replica_groups={{0,2,4,6,8,10,12,14,16,18,20,22,24,26,28,30,32,34,36,38,40,42,44,46,48,..., dimensions={0} | all-to-all | bytes 655360 | tf_op jit(solution)/shard_map/all_to_all | solution.py:317
  73.1 0.0 copy-start
  73.1 0.0 copy-start.2
  73.1 0.0 copy-start.3
  73.1 0.0 copy-start.5
  73.1 4.5 %collective-permute-start.1 = (bf16[32,8,640]{2,1,0:T(8,128)(2,1)S(1)}, bf16[32,8,640]{2,1,0:T(8,128)(2,1)S(1)}, u32[]{:S(2)}, u32[]{:S(2)}) collective-permute-start(bf16[32,8,640]{2,1,0:T(8,128)(2,1)S(1)} %all_to_all.26.refs_0_), channel_id=1, source_target_pairs={{0,1},{1,0},{2,3},{3,2},{4,5},{5,4},{6,7},{7,6},{8,9},{9,8},{10,11... | collective-permute-start | bytes 983048 | tf_op jit(solution)/shard_map/ppermute | solution.py:365
  77.6 1.7 %shard_map.96 = (f32[256,128]{1,0:T(8,128)S(1)}, f32[256,128]{1,0:T(8,128)S(1)}, f32[512,128]{1,0:T(8,128)S(1)}, f32[1,128]{1,0:T(1,128)S(1)}) custom-call(bf16[32,8,640]{2,1,0:T(8,128)(2,1)S(1)} %all_to_all.26.refs_0_, bf16[32,40,128]{2,1,0:T(8,128)(2,1)S(1)} %all_to_all.25.refs_0_.refs_1_.refs_2_, ...), custom_call_target="tpu_custom_call" | custom-call | flops 200000000 | bytes 1507840 | tf_op jit(solution)/shard_map/pallas_call | solution.py:286
  79.3 0.0 collective-permute-done.1.refs_1_
  79.3 0.0 copy-done.1
  79.3 1.7 %shard_map.97 = bf16[32,40,128]{2,1,0:T(8,128)(2,1)S(1)} custom-call(s32[1]{0:T(128)S(6)} %div.18.refs_0_, bf16[32,8,640]{2,1,0:T(8,128)(2,1)S(1)} %collective-permute-done.1.refs_1_, bf16[32,40,128]{2,1,0:T(8,128)(2,1)S(1)} %all_to_all.25.refs_0_.refs_1_.refs_2_, bf16[32,40,128]{2,1,0:T(8,128)(2,1)S(1)} %collective-permute-done.refs_1_.refs_2_.refs_3_, ...), custom_call_target="tpu_custom_call" | custom-call | flops 200000000 | bytes 1851908 | tf_op jit(solution)/shard_map/pallas_call | solution.py:286
  81.0 16.8 %all_to_all.27.in_ref = bf16[32,40,128]{2,1,0:T(8,128)(2,1)S(1)} all-to-all(bf16[32,40,128]{2,1,0:T(8,128)(2,1)S(1)} %shard_map.97), channel_id=1, replica_groups={{0,2,4,6,8,10,12,14,16,18,20,22,24,26,28,30,32,34,36,38,40,42,44,46,48,..., dimensions={0} | all-to-all | bytes 655360 | tf_op jit(solution)/shard_map/all_to_all | solution.py:317
  97.8 0.7 shard_map.99
  98.5 9.8 %all-to-all-start.4 = ((f32[8,32,128]{2,1,0:T(8,128)}), f32[8,32,128]{2,1,0:T(8,128)S(1)}, u32[]{:S(2)}, u32[]{:S(2)}) async-start(f32[8,32,128]{2,1,0:T(8,128)} %shard_map.99), calls=%async_computation.4 | async-start | bytes 262144 | tf_op jit(solution)/shard_map/all_to_all | solution.py:390
  108.3 0.0 copy-done
  108.3 0.0 copy-done.2
  108.3 0.0 copy-done.3
  108.3 0.0 copy-done.4
  108.3 0.0 copy-done.5
  108.4 4.1 %shard_map.98 = (bf16[8,32,4096]{2,1,0:T(8,128)(2,1)}, f32[8,4096]{1,0:T(8,128)}, f32[16,4096]{1,0:T(8,128)}) custom-call(s32[8]{0:T(128)S(1)} %bitcast.14, bf16[32,40,128]{2,1,0:T(8,128)(2,1)S(1)} %all_to_all.27.in_ref, bf16[8,32,4096]{2,1,0:T(8,128)(2,1)S(1)} %bitcast.10, f32[1,4096]{1,0:T(1,128)S(1)} %bitcast.13, f32[8,4096]{1,0:T(8,128)S(1)} %copy-done.2, ...), custom_call_target="tpu_custom_call" | custom-call | flops 10000000 | bytes 5197856 | tf_op jit(solution)/shard_map/pallas_call | solution.py:286
  112.4 5.2 %all-to-all-done.4 = f32[8,32,128]{2,1,0:T(8,128)S(1)} async-done(((f32[8,32,128]{2,1,0:T(8,128)}), f32[8,32,128]{2,1,0:T(8,128)S(1)}, u32[]{:S(2)}, u32[]{:S(2)}) %all-to-all-start.4) | async-done | bytes 131104 | tf_op jit(solution)/shard_map/all_to_all | solution.py:390
  117.6 0.6 reduce_sum.19
  (1 shorter events, 0.0 us)
Async XLA Ops:
  30.8 5.6 %collective-permute-start = (bf16[32,40,128]{2,1,0:T(8,128)(2,1)S(1)}, bf16[32,40,128]{2,1,0:T(8,128)(2,1)S(1)}, u32[]{:S(2)}, u32[]{:S(2)}) collective-permute-start(bf16[32,40,128]{2,1,0:T(8,128)(2,1)S(1)} %all_to_all.25.refs_0_.refs_1_.refs_2_), channel_id=1, source_target_pairs={{0,1},{1,0},{2,3},{3,2},{4,5},{5,4},{6,7},{7,6},{8,9},{9,8},{10,11... | collective-permute-start | bytes 983048 | tf_op jit(solution)/shard_map/ppermute | solution.py:348
  37.2 42.1 %copy-start.1 = (f32[4096]{0:T(1024)S(1)}, f32[4096]{0:T(1024)}, u32[]{:S(2)}) copy-start(f32[4096]{0:T(1024)} %param.8) | copy-start | bytes 49156
  38.0 17.5 %all-to-all-start.1 = ((f16[32,8,640]{2,1,0:T(8,128)(2,1)}), f16[32,8,640]{2,1,0:T(8,128)(2,1)S(1)}, u32[]{:S(2)}, u32[]{:S(2)}) async-start(f16[32,8,640]{2,1,0:T(8,128)(2,1)} %convert_element_type.6), calls=%async_computation.1 | async-start | bytes 655360 | tf_op jit(solution)/shard_map/all_to_all | solution.py:317
  73.1 35.2 %copy-start = (bf16[1,8,32,4096]{3,2,1,0:T(8,128)(2,1)S(1)}, bf16[1,8,32,4096]{3,2,1,0:T(8,128)(2,1)}, u32[]{:S(2)}) copy-start(bf16[1,8,32,4096]{3,2,1,0:T(8,128)(2,1)} %x_hbm.1) | copy-start | bytes 6291460
  73.1 35.2 %copy-start.2 = (f32[8,4096]{1,0:T(8,128)S(1)}, f32[8,4096]{1,0:T(8,128)}, u32[]{:S(2)}) copy-start(f32[8,4096]{1,0:T(8,128)} %get-tuple-element.20.unit_ref) | copy-start | bytes 393220
  73.1 35.2 %copy-start.3 = (f32[8,32,128]{2,1,0:T(8,128)S(1)}, f32[8,32,128]{2,1,0:T(8,128)}, u32[]{:S(2)}) copy-start(f32[8,32,128]{2,1,0:T(8,128)} %get-tuple-element.21.inv_ref) | copy-start | bytes 393220
  73.1 35.2 %copy-start.4 = (f32[8,128]{1,0:T(8,128)S(1)}, f32[8,128]{1,0:T(8,128)}, u32[]{:S(2)}) copy-start(f32[8,128]{1,0:T(8,128)} %get-tuple-element.22.norm_ref) | copy-start | bytes 12292
  73.1 35.2 %copy-start.5 = (s32[1,8]{1,0:T(1,128)S(1)}, s32[1,8]{1,0:T(1,128)}, u32[]{:S(2)}) copy-start(s32[1,8]{1,0:T(1,128)} %len_hbm.1) | copy-start | bytes 100
  73.1 6.2 %collective-permute-start.1 = (bf16[32,8,640]{2,1,0:T(8,128)(2,1)S(1)}, bf16[32,8,640]{2,1,0:T(8,128)(2,1)S(1)}, u32[]{:S(2)}, u32[]{:S(2)}) collective-permute-start(bf16[32,8,640]{2,1,0:T(8,128)(2,1)S(1)} %all_to_all.26.refs_0_), channel_id=1, source_target_pairs={{0,1},{1,0},{2,3},{3,2},{4,5},{5,4},{6,7},{7,6},{8,9},{9,8},{10,11... | collective-permute-start | bytes 983048 | tf_op jit(solution)/shard_map/ppermute | solution.py:365
  98.5 19.1 %all-to-all-start.4 = ((f32[8,32,128]{2,1,0:T(8,128)}), f32[8,32,128]{2,1,0:T(8,128)S(1)}, u32[]{:S(2)}, u32[]{:S(2)}) async-start(f32[8,32,128]{2,1,0:T(8,128)} %shard_map.99), calls=%async_computation.4 | async-start | bytes 262144 | tf_op jit(solution)/shard_map/all_to_all | solution.py:390

commit v7 on v6

--- a/solution.py
+++ b/solution.py
@@ -17,7 +17,7 @@
 
 
 def embed_kernel(
-    core_ref, len_hbm, x_hbm, gain_hbm, pos_hbm, pool_hbm, ids_hbm, out_ref, unit_ref, inv_ref, norm_ref,
+    me_ref, len_hbm, x_hbm, gain_hbm, pos_hbm, pool_hbm, ids_hbm, out_ref, unit_ref, inv_ref, norm_ref,
     len_ref, x_ref, gain_ref, pos_ref, pool_ref, ids_ref, row_ref, x_sem, small_sem,
 ):
     queries, width = unit_ref.shape
@@ -79,7 +79,7 @@
     bits = (2 * queries - 1).bit_length()
     half = chunks * 2 * queries
     owner = ids >> bits
-    other = jnp.where((owner & 1) == core_ref[0], 0, half)
+    other = jnp.where((owner & 1) == (me_ref[0] & 1), 0, half)
     place = other + ((owner >> 1) << bits) + (ids & (2 * queries - 1))
     row = lax.broadcasted_iota(jnp.int32, (hard, LANES), 0)
     lane = lax.broadcasted_iota(jnp.int32, (hard, LANES), 1)
@@ -136,7 +136,7 @@
     sim_ref[:, :, n:] = tail.reshape(chips, q, LANES)
 
 
-def softmax_kernel(hard, chip_ref, in_ref, out_ref):
+def softmax_kernel(hard, me_ref, in_ref, out_ref):
     copies, q, width = out_ref.shape
     n = width - LANES
     scores = in_ref[...]
@@ -144,7 +144,7 @@
     row = lax.broadcasted_iota(jnp.int32, (q, width), 0)
     exps = jnp.where(column < n + hard, jnp.exp(scores), 0.0)
     soft = exps / jnp.sum(exps, axis=1, keepdims=True)
-    own = column == row + chip_ref[0] * q
+    own = column == row + (me_ref[0] >> 1) * q
     along = jnp.sum(soft * scores - jnp.where(own, scores, 0.0), axis=1, keepdims=True)
     high = along.astype(BF16).astype(F32)
     sent = jnp.where(column == n + hard, high, soft)
@@ -197,7 +197,7 @@
 
 
 def slices_kernel(
-    hard, chip_ref, wx_ref, got_ref, gotx_ref, gain_ref, emb_ref, key_ref, pool_ref, part_ref, out_ref
+    hard, me_ref, wx_ref, got_ref, gotx_ref, gain_ref, emb_ref, key_ref, pool_ref, part_ref, out_ref
 ):
     chips, q, width = wx_ref.shape
     half = chips * q
@@ -212,7 +212,7 @@
     emb_grad = emb_ref[...]
     key = (key + key_ref[...]) / TEMPERATURE
     pool = (pool + pool_ref[...]) * (POOL_SCALE / TEMPERATURE)
-    gain_part = (gain_part + part_ref[...]) / gain_ref[pl.ds(chip_ref[0], 1), :]
+    gain_part = (gain_part + part_ref[...]) / gain_ref[pl.ds(me_ref[0] >> 1, 1), :]
     gain_high = gain_part.astype(BF16).astype(F32)
     row = lax.broadcasted_iota(jnp.int32, (q, LANES), 0)
     gain_rows = jnp.where(row == 0, gain_high, jnp.where(row == 1, gain_part - gain_high, 0.0))
@@ -223,13 +223,11 @@
 
 
 def gain_kernel(in_ref, out_ref):
-    copies, chips, _ = out_ref.shape
+    copies, _, _ = out_ref.shape
     q = in_ref.shape[1] // 5
-    for k in range(chips):
-        rows = in_ref[k].astype(F32)[4 * q : 5 * q]
-        both = jnp.sum(rows, axis=0, keepdims=True)
-        for r in range(copies):
-            out_ref[r, k : k + 1] = both
+    both = jnp.sum(in_ref[:, 4 * q :].astype(F32), axis=1)
+    for r in range(copies):
+        out_ref[r] = both
 
 
 def backward_kernel(
@@ -302,7 +300,6 @@
     owners = lax.axis_size("dp")
     groups = lax.axis_size("rep")
     me = lax.axis_index("dp").astype(jnp.int32).reshape(1)
-    core, chip = lax.rem(me, 2), lax.div(me, 2)
     _, queries, tokens, width = query_states.shape
     hard = hard_ids.shape[2]
     chips = owners // 2
@@ -327,7 +324,7 @@
             shape((queries, tokens, LANES), F32),
             shape((queries, LANES), F32),
         ],
-        [core, query_lengths, query_states, gain_row, positives, mined_pool, hard_ids.transpose(2, 0, 1)],
+        [me, query_lengths, query_states, gain_row, positives, mined_pool, hard_ids.transpose(2, 0, 1)],
         8_000_000,
         (0,),
         (1, 2, 3, 4, 5, 6),
@@ -357,7 +354,7 @@
     (sent,) = call(
         bound(softmax_kernel),
         [shape((chips, queries, q_all + LANES), BF16)],
-        [chip, scores],
+        [me, scores],
         1_000_000,
         (0,),
     )
@@ -379,7 +376,7 @@
     (back,) = call(
         bound(slices_kernel),
         [shape((chips, 5 * queries, LANES), BF16)],
-        [chip, weightsx, got, gotx, gain_tiles, *shares],
+        [me, weightsx, got, gotx, gain_tiles, *shares],
         200_000_000,
         (0,),
     )

time: 120 us -> 118 us (0.983)
  blocking collectives: 60.7 us -> 77.2 us
  waiting for transfers between devices: 20.1 us -> 6.46 us
  starting transfers between devices: 22.5 us -> 18.6 us
    all_to_all x3 -> x4, blocking collectives: 60.7 us -> 77.2 us  [among_chips(): lax.all_to_all(x, 'dp', 0, 0, tiled=True, axis_index_groups=same_core)]
    all_to_all x1 -> x0, waiting for transfers between devices: 13.6 us -> none  [among_chips(): lax.all_to_all(x, 'dp', 0, 0, tiled=True, axis_index_groups=same_core)]
    all_to_all x1 -> x0, starting transfers between devices: 3.88 us -> none  [among_chips(): lax.all_to_all(x, 'dp', 0, 0, tiled=True, axis_index_groups=same_core)]
  transfers between devices with their start and end apart: 4 -> 3, of which waited for: 3 -> 2; matrix products, arithmetic and copies ran while one was open for 0% -> 0% of each run, Pallas kernels for 5% -> 5%
where the time goes in v7:
time: 118 us; the launch traced here: 117 us
  blocking collectives  77.2 us (65%)
  starting transfers between devices  18.6 us (16%)
  Pallas kernels  12.8 us (11%)
  waiting for transfers between devices  6.46 us (5%)
    all_to_all x4, blocking collectives, among_chips(): lax.all_to_all(x, 'dp', 0, 0, tiled=True, axis_index_groups=same_core)  77.2 us
    pallas_call x7, Pallas kernels, call(): pl.pallas_call(kernel, out_shape=list(outs), in_specs=[pl.BlockSpec(memor...  12.8 us
    all_to_all x1, starting transfers between devices, local(): gain_groups = lax.all_to_all(gain_sent, 'rep', 0, 0, tiled=True)  9.76 us
    all_to_all x1, waiting for transfers between devices, local(): gain_groups = lax.all_to_all(gain_sent, 'rep', 0, 0, tiled=True)  5.22 us
    ppermute x1, starting transfers between devices, local(): weightsx = lax.ppermute(weights, 'dp', pair)  4.47 us
    ppermute x1, starting transfers between devices, local(): gotx = lax.ppermute(got, 'dp', pair)  4.38 us
  transfers between devices with their start and end apart: 3, of which 2 were waited for; matrix products, arithmetic and copies ran while one was open for 0% of the time, Pallas kernels for 5%

profile of v7, /device:TPU:1, one launch (start us, length us, event | category | flops | bytes accessed | tf_op | source)
XLA Modules:
  0.0 116.6 jit_solution(14829764998979459642)
XLA Ops:
  0.6 3.6 %shard_map.93 = (bf16[32,40,128]{2,1,0:T(8,128)(2,1)}, f32[8,4096]{1,0:T(8,128)}, f32[8,32,128]{2,1,0:T(8,128)}, f32[8,128]{1,0:T(8,128)}) custom-call(s32[1]{0:T(128)} %bitcast.1.me_ref.refs_0_, s32[1,8]{1,0:T(1,128)} %len_hbm.1, bf16[1,8,32,4096]{3,2,1,0:T(8,128)(2,1)} %x_hbm.1, f32[1,4096]{1,0:T(1,128)} %bitcast.11, bf16[1,8,4096]{2,1,0:T(8,128)(2,1)} %pos_hbm.1, ...), custom_call_target="tpu_custom_call" | custom-call | flops 8000000 | bytes 2904324 | tf_op jit(solution)/shard_map/pallas_call | solution.py:284
  4.3 26.5 %all_to_all.25.refs_0_.refs_1_.refs_2_ = bf16[32,40,128]{2,1,0:T(8,128)(2,1)S(1)} all-to-all(bf16[32,40,128]{2,1,0:T(8,128)(2,1)} %get-tuple-element.15), channel_id=1, replica_groups={{0,2,4,6,8,10,12,14,16,18,20,22,24,26,28,30,32,34,36,38,40,42,44,46,48,..., dimensions={0} | all-to-all | bytes 655360 | tf_op jit(solution)/shard_map/all_to_all | solution.py:314
  30.8 4.4 %collective-permute-start = (bf16[32,40,128]{2,1,0:T(8,128)(2,1)S(1)}, bf16[32,40,128]{2,1,0:T(8,128)(2,1)S(1)}, u32[]{:S(2)}, u32[]{:S(2)}) collective-permute-start(bf16[32,40,128]{2,1,0:T(8,128)(2,1)S(1)} %all_to_all.25.refs_0_.refs_1_.refs_2_), channel_id=1, source_target_pairs={{0,1},{1,0},{2,3},{3,2},{4,5},{5,4},{6,7},{7,6},{8,9},{9,8},{10,11... | collective-permute-start | bytes 983048 | tf_op jit(solution)/shard_map/ppermute | solution.py:345
  35.2 1.2 %collective-permute-done.refs_1_.refs_2_.refs_3_ = bf16[32,40,128]{2,1,0:T(8,128)(2,1)S(1)} collective-permute-done((bf16[32,40,128]{2,1,0:T(8,128)(2,1)S(1)}, bf16[32,40,128]{2,1,0:T(8,128)(2,1)S(1)}, u32[]{:S(2)}, u32[]{:S(2)}) %collective-permute-start) | collective-permute-done | bytes 327712 | tf_op jit(solution)/shard_map/ppermute | solution.py:345
  36.4 0.8 shard_map.94
  37.2 0.0 copy-start.1
  37.3 16.3 %all_to_all.26 = f16[32,8,640]{2,1,0:T(8,128)(2,1)S(1)} all-to-all(f16[32,8,640]{2,1,0:T(8,128)(2,1)S(1)} %convert_element_type.6), channel_id=1, replica_groups={{0,2,4,6,8,10,12,14,16,18,20,22,24,26,28,30,32,34,36,38,40,42,44,46,48,..., dimensions={0} | all-to-all | bytes 655360 | tf_op jit(solution)/shard_map/all_to_all | solution.py:314
  53.6 0.1 convert_reduce_fusion.refs_1_
  53.7 0.2 shard_map.95
  53.9 17.6 %all_to_all.27.refs_0_ = bf16[32,8,640]{2,1,0:T(8,128)(2,1)S(1)} all-to-all(bf16[32,8,640]{2,1,0:T(8,128)(2,1)S(1)} %shard_map.95), channel_id=1, replica_groups={{0,2,4,6,8,10,12,14,16,18,20,22,24,26,28,30,32,34,36,38,40,42,44,46,48,..., dimensions={0} | all-to-all | bytes 655360 | tf_op jit(solution)/shard_map/all_to_all | solution.py:314
  71.5 0.0 copy-start
  71.5 0.0 copy-start.2
  71.5 0.0 copy-start.3
  71.5 0.0 copy-start.4
  71.5 0.0 copy-start.5
  71.5 4.5 %collective-permute-start.1 = (bf16[32,8,640]{2,1,0:T(8,128)(2,1)S(1)}, bf16[32,8,640]{2,1,0:T(8,128)(2,1)S(1)}, u32[]{:S(2)}, u32[]{:S(2)}) collective-permute-start(bf16[32,8,640]{2,1,0:T(8,128)(2,1)S(1)} %all_to_all.27.refs_0_), channel_id=1, source_target_pairs={{0,1},{1,0},{2,3},{3,2},{4,5},{5,4},{6,7},{7,6},{8,9},{9,8},{10,11... | collective-permute-start | bytes 983048 | tf_op jit(solution)/shard_map/ppermute | solution.py:362
  76.0 1.7 %shard_map.96 = (f32[256,128]{1,0:T(8,128)S(1)}, f32[256,128]{1,0:T(8,128)S(1)}, f32[512,128]{1,0:T(8,128)S(1)}, f32[1,128]{1,0:T(1,128)S(1)}) custom-call(bf16[32,8,640]{2,1,0:T(8,128)(2,1)S(1)} %all_to_all.27.refs_0_, bf16[32,40,128]{2,1,0:T(8,128)(2,1)S(1)} %all_to_all.25.refs_0_.refs_1_.refs_2_, ...), custom_call_target="tpu_custom_call" | custom-call | flops 200000000 | bytes 1507840 | tf_op jit(solution)/shard_map/pallas_call | solution.py:284
  77.7 0.0 collective-permute-done.1.refs_1_
  77.7 0.0 copy-done.1
  77.7 1.7 %shard_map.97 = bf16[32,40,128]{2,1,0:T(8,128)(2,1)S(1)} custom-call(s32[1]{0:T(128)} %bitcast.1.me_ref.refs_0_, bf16[32,8,640]{2,1,0:T(8,128)(2,1)S(1)} %collective-permute-done.1.refs_1_, bf16[32,40,128]{2,1,0:T(8,128)(2,1)S(1)} %all_to_all.25.refs_0_.refs_1_.refs_2_, bf16[32,40,128]{2,1,0:T(8,128)(2,1)S(1)} %collective-permute-done.refs_1_.refs_2_.refs_3_, ...), custom_call_target="tpu_custom_call" | custom-call | flops 200000000 | bytes 1851908 | tf_op jit(solution)/shard_map/pallas_call | solution.py:284
  79.4 16.8 %all_to_all.28.in_ref = bf16[32,40,128]{2,1,0:T(8,128)(2,1)S(1)} all-to-all(bf16[32,40,128]{2,1,0:T(8,128)(2,1)S(1)} %shard_map.97), channel_id=1, replica_groups={{0,2,4,6,8,10,12,14,16,18,20,22,24,26,28,30,32,34,36,38,40,42,44,46,48,..., dimensions={0} | all-to-all | bytes 655360 | tf_op jit(solution)/shard_map/all_to_all | solution.py:314
  96.2 0.7 shard_map.99
  96.9 9.8 %all-to-all-start.4 = ((f32[8,32,128]{2,1,0:T(8,128)}), f32[8,32,128]{2,1,0:T(8,128)S(1)}, u32[]{:S(2)}, u32[]{:S(2)}) async-start(f32[8,32,128]{2,1,0:T(8,128)} %shard_map.99), calls=%async_computation.4 | async-start | bytes 262144 | tf_op jit(solution)/shard_map/all_to_all | solution.py:387
  106.7 0.0 copy-done
  106.7 0.0 copy-done.2
  106.7 0.0 copy-done.3
  106.7 0.0 copy-done.4
  106.7 0.0 copy-done.5
  106.7 4.1 %shard_map.98 = (bf16[8,32,4096]{2,1,0:T(8,128)(2,1)}, f32[8,4096]{1,0:T(8,128)}, f32[16,4096]{1,0:T(8,128)}) custom-call(s32[8]{0:T(128)S(1)} %bitcast.14, bf16[32,40,128]{2,1,0:T(8,128)(2,1)S(1)} %all_to_all.28.in_ref, bf16[8,32,4096]{2,1,0:T(8,128)(2,1)S(1)} %bitcast.10, f32[1,4096]{1,0:T(1,128)S(1)} %bitcast.13, f32[8,4096]{1,0:T(8,128)S(1)} %copy-done.2, ...), custom_call_target="tpu_custom_call" | custom-call | flops 10000000 | bytes 5197856 | tf_op jit(solution)/shard_map/pallas_call | solution.py:284
  110.8 5.2 %all-to-all-done.4 = f32[8,32,128]{2,1,0:T(8,128)S(1)} async-done(((f32[8,32,128]{2,1,0:T(8,128)}), f32[8,32,128]{2,1,0:T(8,128)S(1)}, u32[]{:S(2)}, u32[]{:S(2)}) %all-to-all-start.4) | async-done | bytes 131104 | tf_op jit(solution)/shard_map/all_to_all | solution.py:387
  116.0 0.6 reduce_sum.19
  (1 shorter events, 0.0 us)
Async XLA Ops:
  30.8 5.6 %collective-permute-start = (bf16[32,40,128]{2,1,0:T(8,128)(2,1)S(1)}, bf16[32,40,128]{2,1,0:T(8,128)(2,1)S(1)}, u32[]{:S(2)}, u32[]{:S(2)}) collective-permute-start(bf16[32,40,128]{2,1,0:T(8,128)(2,1)S(1)} %all_to_all.25.refs_0_.refs_1_.refs_2_), channel_id=1, source_target_pairs={{0,1},{1,0},{2,3},{3,2},{4,5},{5,4},{6,7},{7,6},{8,9},{9,8},{10,11... | collective-permute-start | bytes 983048 | tf_op jit(solution)/shard_map/ppermute | solution.py:345
  37.2 40.5 %copy-start.1 = (f32[4096]{0:T(1024)S(1)}, f32[4096]{0:T(1024)}, u32[]{:S(2)}) copy-start(f32[4096]{0:T(1024)} %param.8) | copy-start | bytes 49156
  71.5 35.2 %copy-start = (bf16[1,8,32,4096]{3,2,1,0:T(8,128)(2,1)S(1)}, bf16[1,8,32,4096]{3,2,1,0:T(8,128)(2,1)}, u32[]{:S(2)}) copy-start(bf16[1,8,32,4096]{3,2,1,0:T(8,128)(2,1)} %x_hbm.1) | copy-start | bytes 6291460
  71.5 35.2 %copy-start.2 = (f32[8,4096]{1,0:T(8,128)S(1)}, f32[8,4096]{1,0:T(8,128)}, u32[]{:S(2)}) copy-start(f32[8,4096]{1,0:T(8,128)} %get-tuple-element.20.unit_ref) | copy-start | bytes 393220
  71.5 35.2 %copy-start.3 = (f32[8,32,128]{2,1,0:T(8,128)S(1)}, f32[8,32,128]{2,1,0:T(8,128)}, u32[]{:S(2)}) copy-start(f32[8,32,128]{2,1,0:T(8,128)} %get-tuple-element.21.inv_ref) | copy-start | bytes 393220
  71.5 35.3 %copy-start.4 = (f32[8,128]{1,0:T(8,128)S(1)}, f32[8,128]{1,0:T(8,128)}, u32[]{:S(2)}) copy-start(f32[8,128]{1,0:T(8,128)} %get-tuple-element.22.norm_ref) | copy-start | bytes 12292
  71.5 35.3 %copy-start.5 = (s32[1,8]{1,0:T(1,128)S(1)}, s32[1,8]{1,0:T(1,128)}, u32[]{:S(2)}) copy-start(s32[1,8]{1,0:T(1,128)} %len_hbm.1) | copy-start | bytes 100
  71.5 6.2 %collective-permute-start.1 = (bf16[32,8,640]{2,1,0:T(8,128)(2,1)S(1)}, bf16[32,8,640]{2,1,0:T(8,128)(2,1)S(1)}, u32[]{:S(2)}, u32[]{:S(2)}) collective-permute-start(bf16[32,8,640]{2,1,0:T(8,128)(2,1)S(1)} %all_to_all.27.refs_0_), channel_id=1, source_target_pairs={{0,1},{1,0},{2,3},{3,2},{4,5},{5,4},{6,7},{7,6},{8,9},{9,8},{10,11... | collective-permute-start | bytes 983048 | tf_op jit(solution)/shard_map/ppermute | solution.py:362
  96.9 19.1 %all-to-all-start.4 = ((f32[8,32,128]{2,1,0:T(8,128)}), f32[8,32,128]{2,1,0:T(8,128)S(1)}, u32[]{:S(2)}, u32[]{:S(2)}) async-start(f32[8,32,128]{2,1,0:T(8,128)} %shard_map.99), calls=%async_computation.4 | async-start | bytes 262144 | tf_op jit(solution)/shard_map/all_to_all | solution.py:387

commit v8 on v7

--- a/solution.py
+++ b/solution.py
@@ -9,6 +9,7 @@
 QUERY_SCALE = 512.0
 POOL_SCALE = 16.0
 LANES = 128
+PART = 8
 F32 = jnp.float32
 BF16 = jnp.bfloat16
 F16 = jnp.float16
@@ -17,8 +18,8 @@
 
 
 def embed_kernel(
-    me_ref, len_hbm, x_hbm, gain_hbm, pos_hbm, pool_hbm, ids_hbm, out_ref, unit_ref, inv_ref, norm_ref,
-    len_ref, x_ref, gain_ref, pos_ref, pool_ref, ids_ref, row_ref, x_sem, small_sem,
+    me_ref, len_hbm, x_hbm, gain_hbm, pos_hbm, pool_hbm, ids_hbm,
+    out_hbm, unit_hbm, inv_hbm, norm_hbm, out_ref, unit_ref, inv_ref, norm_ref, out_sem, len_ref, x_ref, gain_ref, pos_ref, pool_ref, ids_ref, row_ref, x_sem, small_sem,
 ):
     queries, width = unit_ref.shape
     tokens = x_ref.shape[1]
@@ -74,6 +75,12 @@
         square += pooled * pooled
     norm = lax.rsqrt(jnp.sum(square, axis=1, keepdims=True) + 1e-06)
     norm_ref[...] = jnp.broadcast_to(norm, norm_ref.shape)
+    done = [
+        pltpu.make_async_copy(inv_ref, inv_hbm, out_sem.at[0]),
+        pltpu.make_async_copy(norm_ref, norm_hbm, out_sem.at[1]),
+    ]
+    for copy in done:
+        copy.start()
     ids = ids_ref[:, 0, :]
     hard = ids.shape[0]
     bits = (2 * queries - 1).bit_length()
@@ -97,6 +104,16 @@
         unit_ref[:, cols] = unit
         rows = [unit, id_rows, pos_ref[0, :, cols].astype(F32), pool_ref[0, :, cols].astype(F32)]
         out_ref[k] = jnp.concatenate(rows, axis=0).astype(BF16)
+        if (k + 1) % PART == 0:
+            part = pl.ds(k + 1 - PART, PART)
+            done.append(
+                pltpu.make_async_copy(out_ref.at[part], out_hbm.at[part], out_sem.at[3 + k // PART])
+            )
+            done[-1].start()
+    done.append(pltpu.make_async_copy(unit_ref, unit_hbm, out_sem.at[2]))
+    done[-1].start()
+    for copy in done:
+        copy.wait()
 
 
 def rows_of(block, first, last):
@@ -231,7 +248,8 @@
 
 
 def backward_kernel(
-    len_ref, in_ref, x_ref, gain_ref, unit_ref, inv_ref, norm_ref, grad_ref, key_ref, pool_ref, h_ref, row_ref
+    len_ref, in_ref, x_ref, gain_ref, unit_ref, inv_ref, norm_ref, grad_hbm, key_hbm, pool_hbm,
+    h_ref, row_ref, grad_ref, key_ref, pool_ref, grad_sem, small_sem,
 ):
     queries, width = unit_ref.shape
     tokens = x_ref.shape[1]
@@ -246,6 +264,12 @@
         g = block[:q]
         h_ref[:, cols] = g
         dots += g * unit_ref[:, cols]
+    small = [
+        pltpu.make_async_copy(key_ref, key_hbm, small_sem.at[0]),
+        pltpu.make_async_copy(pool_ref, pool_hbm, small_sem.at[1]),
+    ]
+    for copy in small:
+        copy.start()
     along = jnp.sum(dots, axis=1, keepdims=True)
     norm = norm_ref[:, :1]
     for k in range(chunks):
@@ -269,12 +293,17 @@
             cols = slice(k * LANES, (k + 1) * LANES)
             x = x_ref[i, :, cols].astype(F32)
             grad_ref[i, :, cols] = (scale * row_ref[i, :, cols] - back * x).astype(BF16)
+        pltpu.make_async_copy(grad_ref.at[i], grad_hbm.at[i], grad_sem.at[i]).start()
         return carry
 
     lax.fori_loop(0, queries, one_query, 0)
-
-
-def call(kernel, outs, args, flops, smem=(), hbm=(), scratch=(), vmem=40):
+    for i in range(queries):
+        pltpu.make_async_copy(grad_ref.at[i], grad_hbm.at[i], grad_sem.at[i]).wait()
+    for copy in small:
+        copy.wait()
+
+
+def call(kernel, outs, args, flops, smem=(), hbm=(), scratch=(), vmem=40, out_hbm=False):
     def space(i):
         return pltpu.SMEM if i in smem else pltpu.HBM if i in hbm else pltpu.VMEM
 
@@ -285,7 +314,7 @@
         kernel,
         out_shape=list(outs),
         in_specs=[pl.BlockSpec(memory_space=space(i)) for i in range(len(args))],
-        out_specs=[pl.BlockSpec(memory_space=pltpu.VMEM)] * len(outs),
+        out_specs=[pl.BlockSpec(memory_space=pltpu.HBM if out_hbm else pltpu.VMEM)] * len(outs),
         scratch_shapes=list(scratch),
         compiler_params=pltpu.CompilerParams(vmem_limit_bytes=vmem * 1024 * 1024),
         cost_estimate=pl.CostEstimate(flops=flops, bytes_accessed=size, transcendentals=0),
@@ -329,6 +358,11 @@
         (0,),
         (1, 2, 3, 4, 5, 6),
         [
+            pltpu.VMEM((chips, 5 * queries, LANES), BF16),
+            pltpu.VMEM((queries, width), F32),
+            pltpu.VMEM((queries, tokens, LANES), F32),
+            pltpu.VMEM((queries, LANES), F32),
+            pltpu.SemaphoreType.DMA((3 + chips // PART,)),
             pltpu.SMEM((1, queries), jnp.int32),
             pltpu.VMEM((queries, tokens, width), BF16),
             pltpu.VMEM((1, width), F32),
@@ -340,6 +374,7 @@
             pltpu.SemaphoreType.DMA((5,)),
         ],
         60,
+        True,
     )
     got = among_chips(out)
     gotx = lax.ppermute(got, "dp", pair)
@@ -396,7 +431,16 @@
         10_000_000,
         (0,),
         (),
-        [pltpu.VMEM((queries, width), F32), pltpu.VMEM((queries, 1, width), F32)],
+        [
+            pltpu.VMEM((queries, width), F32),
+            pltpu.VMEM((queries, 1, width), F32),
+            pltpu.VMEM((queries, tokens, width), BF16),
+            pltpu.VMEM((queries, width), F32),
+            pltpu.VMEM((2 * queries, width), F32),
+            pltpu.SemaphoreType.DMA((queries,)),
+            pltpu.SemaphoreType.DMA((2,)),
+        ],
+        out_hbm=True,
     )
     gain_grad = jnp.sum(gain_groups, axis=0).reshape(width)
     return query_grad[None], key_grad[None], pool_grad[None], gain_grad

time: 118 us -> 118 us (level)
  no operation moved by 1% of the time
where the time goes in v8:
time: 118 us; the launch traced here: 117 us
  blocking collectives  77.2 us (65%)
  starting transfers between devices  18.6 us (16%)
  Pallas kernels  12.3 us (10%)
  waiting for transfers between devices  6.98 us (6%)
    all_to_all x4, blocking collectives, among_chips(): lax.all_to_all(x, 'dp', 0, 0, tiled=True, axis_index_groups=same_core)  77.2 us
    pallas_call x7, Pallas kernels, call(): pl.pallas_call(kernel, out_shape=list(outs), in_specs=[pl.BlockSpec(memor...  12.3 us
    all_to_all x1, starting transfers between devices, local(): gain_groups = lax.all_to_all(gain_sent, 'rep', 0, 0, tiled=True)  9.77 us
    all_to_all x1, waiting for transfers between devices, local(): gain_groups = lax.all_to_all(gain_sent, 'rep', 0, 0, tiled=True)  5.74 us
    ppermute x1, starting transfers between devices, local(): weightsx = lax.ppermute(weights, 'dp', pair)  4.47 us
    ppermute x1, starting transfers between devices, local(): gotx = lax.ppermute(got, 'dp', pair)  4.38 us
  transfers between devices with their start and end apart: 3, of which 2 were waited for; matrix products, arithmetic and copies ran while one was open for 0% of the time, Pallas kernels for 5%

profile of v8, /device:TPU:1, one launch (start us, length us, event | category | flops | bytes accessed | tf_op | source)
XLA Modules:
  0.0 116.7 jit_solution(1743452438523358589)
XLA Ops:
  0.6 3.6 %shard_map.93 = (bf16[32,40,128]{2,1,0:T(8,128)(2,1)}, f32[8,4096]{1,0:T(8,128)}, f32[8,32,128]{2,1,0:T(8,128)}, f32[8,128]{1,0:T(8,128)}) custom-call(s32[1]{0:T(128)} %bitcast.1.me_ref.refs_0_, s32[1,8]{1,0:T(1,128)} %len_hbm.1, bf16[1,8,32,4096]{3,2,1,0:T(8,128)(2,1)} %x_hbm.1, f32[1,4096]{1,0:T(1,128)} %bitcast.11, bf16[1,8,4096]{2,1,0:T(8,128)(2,1)} %pos_hbm.1, ...), custom_call_target="tpu_custom_call" | custom-call | flops 8000000 | bytes 2904324 | tf_op jit(solution)/shard_map/pallas_call | solution.py:313
  4.3 26.5 %all_to_all.25.refs_0_.refs_1_.refs_2_ = bf16[32,40,128]{2,1,0:T(8,128)(2,1)S(1)} all-to-all(bf16[32,40,128]{2,1,0:T(8,128)(2,1)} %get-tuple-element.15), channel_id=1, replica_groups={{0,2,4,6,8,10,12,14,16,18,20,22,24,26,28,30,32,34,36,38,40,42,44,46,48,..., dimensions={0} | all-to-all | bytes 655360 | tf_op jit(solution)/shard_map/all_to_all | solution.py:343
  30.8 4.4 %collective-permute-start = (bf16[32,40,128]{2,1,0:T(8,128)(2,1)S(1)}, bf16[32,40,128]{2,1,0:T(8,128)(2,1)S(1)}, u32[]{:S(2)}, u32[]{:S(2)}) collective-permute-start(bf16[32,40,128]{2,1,0:T(8,128)(2,1)S(1)} %all_to_all.25.refs_0_.refs_1_.refs_2_), channel_id=1, source_target_pairs={{0,1},{1,0},{2,3},{3,2},{4,5},{5,4},{6,7},{7,6},{8,9},{9,8},{10,11... | collective-permute-start | bytes 983048 | tf_op jit(solution)/shard_map/ppermute | solution.py:380
  35.2 1.2 %collective-permute-done.refs_1_.refs_2_.refs_3_ = bf16[32,40,128]{2,1,0:T(8,128)(2,1)S(1)} collective-permute-done((bf16[32,40,128]{2,1,0:T(8,128)(2,1)S(1)}, bf16[32,40,128]{2,1,0:T(8,128)(2,1)S(1)}, u32[]{:S(2)}, u32[]{:S(2)}) %collective-permute-start) | collective-permute-done | bytes 327712 | tf_op jit(solution)/shard_map/ppermute | solution.py:380
  36.4 0.8 shard_map.94
  37.3 0.0 copy-start.1
  37.3 16.3 %all_to_all.26 = f16[32,8,640]{2,1,0:T(8,128)(2,1)S(1)} all-to-all(f16[32,8,640]{2,1,0:T(8,128)(2,1)S(1)} %convert_element_type.6), channel_id=1, replica_groups={{0,2,4,6,8,10,12,14,16,18,20,22,24,26,28,30,32,34,36,38,40,42,44,46,48,..., dimensions={0} | all-to-all | bytes 655360 | tf_op jit(solution)/shard_map/all_to_all | solution.py:343
  53.6 0.1 convert_reduce_fusion.refs_1_
  53.7 0.2 shard_map.95
  53.9 17.6 %all_to_all.27.refs_0_ = bf16[32,8,640]{2,1,0:T(8,128)(2,1)S(1)} all-to-all(bf16[32,8,640]{2,1,0:T(8,128)(2,1)S(1)} %shard_map.95), channel_id=1, replica_groups={{0,2,4,6,8,10,12,14,16,18,20,22,24,26,28,30,32,34,36,38,40,42,44,46,48,..., dimensions={0} | all-to-all | bytes 655360 | tf_op jit(solution)/shard_map/all_to_all | solution.py:343
  71.5 0.0 copy-start
  71.5 0.0 copy-start.2
  71.5 0.0 copy-start.3
  71.5 0.0 copy-start.4
  71.5 0.0 copy-start.5
  71.5 4.5 %collective-permute-start.1 = (bf16[32,8,640]{2,1,0:T(8,128)(2,1)S(1)}, bf16[32,8,640]{2,1,0:T(8,128)(2,1)S(1)}, u32[]{:S(2)}, u32[]{:S(2)}) collective-permute-start(bf16[32,8,640]{2,1,0:T(8,128)(2,1)S(1)} %all_to_all.27.refs_0_), channel_id=1, source_target_pairs={{0,1},{1,0},{2,3},{3,2},{4,5},{5,4},{6,7},{7,6},{8,9},{9,8},{10,11... | collective-permute-start | bytes 983048 | tf_op jit(solution)/shard_map/ppermute | solution.py:397
  76.0 1.7 %shard_map.96 = (f32[256,128]{1,0:T(8,128)S(1)}, f32[256,128]{1,0:T(8,128)S(1)}, f32[512,128]{1,0:T(8,128)S(1)}, f32[1,128]{1,0:T(1,128)S(1)}) custom-call(bf16[32,8,640]{2,1,0:T(8,128)(2,1)S(1)} %all_to_all.27.refs_0_, bf16[32,40,128]{2,1,0:T(8,128)(2,1)S(1)} %all_to_all.25.refs_0_.refs_1_.refs_2_, ...), custom_call_target="tpu_custom_call" | custom-call | flops 200000000 | bytes 1507840 | tf_op jit(solution)/shard_map/pallas_call | solution.py:313
  77.7 0.0 collective-permute-done.1.refs_1_
  77.7 0.0 copy-done.1
  77.7 1.7 %shard_map.97 = bf16[32,40,128]{2,1,0:T(8,128)(2,1)S(1)} custom-call(s32[1]{0:T(128)} %bitcast.1.me_ref.refs_0_, bf16[32,8,640]{2,1,0:T(8,128)(2,1)S(1)} %collective-permute-done.1.refs_1_, bf16[32,40,128]{2,1,0:T(8,128)(2,1)S(1)} %all_to_all.25.refs_0_.refs_1_.refs_2_, bf16[32,40,128]{2,1,0:T(8,128)(2,1)S(1)} %collective-permute-done.refs_1_.refs_2_.refs_3_, ...), custom_call_target="tpu_custom_call" | custom-call | flops 200000000 | bytes 1851908 | tf_op jit(solution)/shard_map/pallas_call | solution.py:313
  79.5 16.8 %all_to_all.28.in_ref = bf16[32,40,128]{2,1,0:T(8,128)(2,1)S(1)} all-to-all(bf16[32,40,128]{2,1,0:T(8,128)(2,1)S(1)} %shard_map.97), channel_id=1, replica_groups={{0,2,4,6,8,10,12,14,16,18,20,22,24,26,28,30,32,34,36,38,40,42,44,46,48,..., dimensions={0} | all-to-all | bytes 655360 | tf_op jit(solution)/shard_map/all_to_all | solution.py:343
  96.3 0.7 shard_map.99
  96.9 9.8 %all-to-all-start.4 = ((f32[8,32,128]{2,1,0:T(8,128)}), f32[8,32,128]{2,1,0:T(8,128)S(1)}, u32[]{:S(2)}, u32[]{:S(2)}) async-start(f32[8,32,128]{2,1,0:T(8,128)} %shard_map.99), calls=%async_computation.4 | async-start | bytes 262144 | tf_op jit(solution)/shard_map/all_to_all | solution.py:422
  106.7 0.0 copy-done
  106.7 0.0 copy-done.2
  106.7 0.0 copy-done.3
  106.7 0.0 copy-done.4
  106.8 0.0 copy-done.5
  106.8 3.5 %shard_map.98 = (bf16[8,32,4096]{2,1,0:T(8,128)(2,1)}, f32[8,4096]{1,0:T(8,128)}, f32[16,4096]{1,0:T(8,128)}) custom-call(s32[8]{0:T(128)S(1)} %bitcast.14, bf16[32,40,128]{2,1,0:T(8,128)(2,1)S(1)} %all_to_all.28.in_ref, bf16[8,32,4096]{2,1,0:T(8,128)(2,1)S(1)} %bitcast.10, f32[1,4096]{1,0:T(1,128)S(1)} %bitcast.13, f32[8,4096]{1,0:T(8,128)S(1)} %copy-done.2, ...), custom_call_target="tpu_custom_call" | custom-call | flops 10000000 | bytes 5197856 | tf_op jit(solution)/shard_map/pallas_call | solution.py:313
  110.3 5.7 %all-to-all-done.4 = f32[8,32,128]{2,1,0:T(8,128)S(1)} async-done(((f32[8,32,128]{2,1,0:T(8,128)}), f32[8,32,128]{2,1,0:T(8,128)S(1)}, u32[]{:S(2)}, u32[]{:S(2)}) %all-to-all-start.4) | async-done | bytes 131104 | tf_op jit(solution)/shard_map/all_to_all | solution.py:422
  116.1 0.6 reduce_sum.19
  (1 shorter events, 0.0 us)
Async XLA Ops:
  30.8 5.6 %collective-permute-start = (bf16[32,40,128]{2,1,0:T(8,128)(2,1)S(1)}, bf16[32,40,128]{2,1,0:T(8,128)(2,1)S(1)}, u32[]{:S(2)}, u32[]{:S(2)}) collective-permute-start(bf16[32,40,128]{2,1,0:T(8,128)(2,1)S(1)} %all_to_all.25.refs_0_.refs_1_.refs_2_), channel_id=1, source_target_pairs={{0,1},{1,0},{2,3},{3,2},{4,5},{5,4},{6,7},{7,6},{8,9},{9,8},{10,11... | collective-permute-start | bytes 983048 | tf_op jit(solution)/shard_map/ppermute | solution.py:380
  37.3 40.5 %copy-start.1 = (f32[4096]{0:T(1024)S(1)}, f32[4096]{0:T(1024)}, u32[]{:S(2)}) copy-start(f32[4096]{0:T(1024)} %param.8) | copy-start | bytes 49156
  71.5 35.2 %copy-start = (bf16[1,8,32,4096]{3,2,1,0:T(8,128)(2,1)S(1)}, bf16[1,8,32,4096]{3,2,1,0:T(8,128)(2,1)}, u32[]{:S(2)}) copy-start(bf16[1,8,32,4096]{3,2,1,0:T(8,128)(2,1)} %x_hbm.1) | copy-start | bytes 6291460
  71.5 35.2 %copy-start.2 = (f32[8,4096]{1,0:T(8,128)S(1)}, f32[8,4096]{1,0:T(8,128)}, u32[]{:S(2)}) copy-start(f32[8,4096]{1,0:T(8,128)} %get-tuple-element.20.unit_ref) | copy-start | bytes 393220
  71.5 35.3 %copy-start.3 = (f32[8,32,128]{2,1,0:T(8,128)S(1)}, f32[8,32,128]{2,1,0:T(8,128)}, u32[]{:S(2)}) copy-start(f32[8,32,128]{2,1,0:T(8,128)} %get-tuple-element.21.inv_ref) | copy-start | bytes 393220
  71.5 35.3 %copy-start.4 = (f32[8,128]{1,0:T(8,128)S(1)}, f32[8,128]{1,0:T(8,128)}, u32[]{:S(2)}) copy-start(f32[8,128]{1,0:T(8,128)} %get-tuple-element.22.norm_ref) | copy-start | bytes 12292
  71.5 35.3 %copy-start.5 = (s32[1,8]{1,0:T(1,128)S(1)}, s32[1,8]{1,0:T(1,128)}, u32[]{:S(2)}) copy-start(s32[1,8]{1,0:T(1,128)} %len_hbm.1) | copy-start | bytes 100
  71.5 6.2 %collective-permute-start.1 = (bf16[32,8,640]{2,1,0:T(8,128)(2,1)S(1)}, bf16[32,8,640]{2,1,0:T(8,128)(2,1)S(1)}, u32[]{:S(2)}, u32[]{:S(2)}) collective-permute-start(bf16[32,8,640]{2,1,0:T(8,128)(2,1)S(1)} %all_to_all.27.refs_0_), channel_id=1, source_target_pairs={{0,1},{1,0},{2,3},{3,2},{4,5},{5,4},{6,7},{7,6},{8,9},{9,8},{10,11... | collective-permute-start | bytes 983048 | tf_op jit(solution)/shard_map/ppermute | solution.py:397
  96.9 19.1 %all-to-all-start.4 = ((f32[8,32,128]{2,1,0:T(8,128)}), f32[8,32,128]{2,1,0:T(8,128)S(1)}, u32[]{:S(2)}, u32[]{:S(2)}) async-start(f32[8,32,128]{2,1,0:T(8,128)} %shard_map.99), calls=%async_computation.4 | async-start | bytes 262144 | tf_op jit(solution)/shard_map/all_to_all | solution.py:422

commit v9 on v7

--- a/solution.py
+++ b/solution.py
@@ -90,12 +90,15 @@
             x.astype(F32).astype(BF16), to, BY_COLUMN, preferred_element_type=F32
         )
 
-    id_rows = lay(place >> 5, 0) + lay(place & 31, hard)
+    count = jnp.zeros(place.shape, jnp.int32)
+    for m in range(hard):
+        count += (place == place[m : m + 1]).astype(jnp.int32)
+    id_rows = lay(place >> 5, 0) + lay(place & 31, hard) + lay(count, 2 * hard)
     for k in range(chunks):
         cols = slice(k * LANES, (k + 1) * LANES)
         unit = unit_ref[:, cols] * norm
         unit_ref[:, cols] = unit
-        rows = [unit, id_rows, pos_ref[0, :, cols].astype(F32), pool_ref[0, :, cols].astype(F32)]
+        rows = [pool_ref[0, :, cols].astype(F32), unit, pos_ref[0, :, cols].astype(F32), id_rows]
         out_ref[k] = jnp.concatenate(rows, axis=0).astype(BF16)
 
 
@@ -103,8 +106,7 @@
     return block[:, first:last].reshape(block.shape[0] * (last - first), LANES)
 
 
-def ids_of(block, q, hard):
-    rows = rows_of(block, q, 2 * q)
+def ids_of(rows, hard):
     lane = lax.broadcasted_iota(jnp.int32, rows.shape, 1)
     ids = rows * 32.0 + pltpu.roll(rows, LANES - hard, 1)
     return jnp.where(lane < hard, ids, 0.0).astype(jnp.int32)
@@ -115,20 +117,24 @@
     q = rows // 5
     half = chips * q
     n = 2 * half
-    a = got_ref[...].astype(F32)
-    b = gotx_ref[...].astype(F32)
+    a = got_ref[:, 2 * q :].astype(F32)
+    b = gotx_ref[:, 2 * q :].astype(F32)
     e = rows_of(a, 0, q).astype(BF16)
-    p = jnp.concatenate([rows_of(a, 2 * q, 3 * q), rows_of(b, 2 * q, 3 * q)], axis=0).astype(BF16)
-    m = jnp.concatenate([rows_of(a, 3 * q, 5 * q), rows_of(b, 3 * q, 5 * q)], axis=0).astype(BF16)
-    ids = ids_of(a, q, hard)
+    p = jnp.concatenate([rows_of(a, q, 2 * q), rows_of(b, q, 2 * q)], axis=0).astype(BF16)
+    own_pool = got_ref[:, : 2 * q].reshape(n, LANES)
+    other_pool = gotx_ref[:, : 2 * q].reshape(n, LANES)
+    ids = ids_of(rows_of(a, 2 * q, 3 * q), hard)
     sim = lax.dot_general(e, p, BY_ROW, preferred_element_type=F32) / TEMPERATURE
     sim_ref[:, :, :n] = sim.reshape(chips, q, n)
-    pool = lax.dot_general(e, m, BY_ROW, preferred_element_type=F32)
+    own_sim = lax.dot_general(e, own_pool, BY_ROW, preferred_element_type=F32)
+    other_sim = lax.dot_general(e, other_pool, BY_ROW, preferred_element_type=F32)
     tail = jnp.zeros((half, LANES), F32)
     within, tile = ids & (LANES - 1), ids >> 7
     for k in range(2 * n // LANES):
+        part = own_sim if k < n // LANES else other_sim
+        first = k * LANES % n
         picked = jnp.take_along_axis(
-            pool[:, k * LANES : (k + 1) * LANES], within, axis=1, mode="promise_in_bounds"
+            part[:, first : first + LANES], within, axis=1, mode="promise_in_bounds"
         )
         tail = jnp.where(tile == k, picked, tail)
     lane = lax.broadcasted_iota(jnp.int32, (half, LANES), 1)
@@ -154,27 +160,28 @@
         out_ref[k] = sent
 
 
-def share(w, ids, hard, own_cols, other_cols, a, b, e, pos):
-    q = a.shape[1] // 5
+def share(w, flip, hard, own_cols, other_cols, pos_all, pools, e, pos, id_rows):
     half = w.shape[0]
     n = 2 * half
     tail = w[:, n:]
     from_own, from_other = w[:, own_cols].astype(BF16), w[:, other_cols].astype(BF16)
+    ids = ids_of(id_rows, hard) ^ flip
+    weights = tail * pltpu.roll(id_rows, LANES - 2 * hard, 1)
     column = lax.broadcasted_iota(jnp.int32, (half, n), 1)
     own_spread = jnp.zeros((half, n), F32)
     other_spread = jnp.zeros((half, n), F32)
     for m in range(hard):
-        one, weight = ids[:, m : m + 1], tail[:, m : m + 1]
-        own_spread += jnp.where(column == one, weight, 0.0)
-        other_spread += jnp.where(column == one - n, weight, 0.0)
+        one, weight = ids[:, m : m + 1], weights[:, m : m + 1]
+        own_spread = jnp.where(column == one, weight, own_spread)
+        other_spread = jnp.where(column == one - n, weight, other_spread)
     own_spread = own_spread.astype(BF16)
     other_spread = other_spread.astype(BF16)
 
-    def dot(left, block, first, last):
-        return jnp.dot(left, rows_of(block, first, last).astype(BF16), preferred_element_type=F32)
-
-    numerator = dot(from_own, a, 2 * q, 3 * q) + dot(from_other, b, 2 * q, 3 * q)
-    numerator += dot(own_spread, a, 3 * q, 5 * q) + dot(other_spread, b, 3 * q, 5 * q)
+    def dot(left, right):
+        return jnp.dot(left, right, preferred_element_type=F32)
+
+    numerator = dot(from_own, pos_all[0].astype(BF16)) + dot(from_other, pos_all[1].astype(BF16))
+    numerator += dot(own_spread, pools[0]) + dot(other_spread, pools[1])
     along = tail[:, hard : hard + 1] + tail[:, hard + 1 : hard + 2]
     emb_grad = (numerator - pos) / TEMPERATURE - along * e
     eh = e.astype(BF16)
@@ -183,15 +190,23 @@
     return emb_grad, key, pool, jnp.sum(emb_grad * e, axis=0, keepdims=True)
 
 
+def blocks(got_ref, gotx_ref, q):
+    n = got_ref.shape[0] * 2 * q
+    a = got_ref[:, 2 * q :].astype(F32)
+    b = gotx_ref[:, 2 * q :].astype(F32)
+    pools = got_ref[:, : 2 * q].reshape(n, LANES), gotx_ref[:, : 2 * q].reshape(n, LANES)
+    return a, b, (rows_of(a, q, 2 * q), rows_of(b, q, 2 * q)), pools
+
+
 def own_kernel(hard, w_ref, got_ref, gotx_ref, emb_ref, key_ref, pool_ref, gain_ref):
     chips, q, width = w_ref.shape
     half = chips * q
-    a = got_ref[...].astype(F32)
-    b = gotx_ref[...].astype(F32)
+    a, _, pos_all, pools = blocks(got_ref, gotx_ref, q)
     w = w_ref[...].astype(F32).reshape(half, width)
     e = rows_of(a, 0, q)
     emb_ref[...], key, pool_ref[...], gain_ref[...] = share(
-        w, ids_of(a, q, hard), hard, slice(0, half), slice(half, 2 * half), a, b, e, rows_of(a, 2 * q, 3 * q)
+        w, 0, hard, slice(0, half), slice(half, 2 * half), pos_all, pools, e, pos_all[0],
+        rows_of(a, 2 * q, 3 * q),
     )
     key_ref[...] = key - e
 
@@ -201,13 +216,11 @@
 ):
     chips, q, width = wx_ref.shape
     half = chips * q
-    a = got_ref[...].astype(F32)
-    b = gotx_ref[...].astype(F32)
+    _, b, pos_all, pools = blocks(got_ref, gotx_ref, q)
     w = wx_ref[...].astype(F32).reshape(half, width)
-    ids = ids_of(b, q, hard) ^ (2 * half)
-    e = rows_of(b, 0, q)
     _, key, pool, gain_part = share(
-        w, ids, hard, slice(half, 2 * half), slice(0, half), a, b, e, rows_of(b, 2 * q, 3 * q)
+        w, 2 * half, hard, slice(half, 2 * half), slice(0, half), pos_all, pools, rows_of(b, 0, q), pos_all[1],
+        rows_of(b, 2 * q, 3 * q),
     )
     emb_grad = emb_ref[...]
     key = (key + key_ref[...]) / TEMPERATURE

time: 118 us -> 118 us (level)
  no operation moved by 1% of the time
where the time goes in v9:
time: 118 us; the launch traced here: 117 us
  blocking collectives  77.2 us (65%)
  starting transfers between devices  18.6 us (16%)
  Pallas kernels  12.7 us (11%)
  waiting for transfers between devices  6.46 us (5%)
    all_to_all x4, blocking collectives, among_chips(): lax.all_to_all(x, 'dp', 0, 0, tiled=True, axis_index_groups=same_core)  77.2 us
    pallas_call x7, Pallas kernels, call(): pl.pallas_call(kernel, out_shape=list(outs), in_specs=[pl.BlockSpec(memor...  12.7 us
    all_to_all x1, starting transfers between devices, local(): gain_groups = lax.all_to_all(gain_sent, 'rep', 0, 0, tiled=True)  9.77 us
    all_to_all x1, waiting for transfers between devices, local(): gain_groups = lax.all_to_all(gain_sent, 'rep', 0, 0, tiled=True)  5.22 us
    ppermute x1, starting transfers between devices, local(): weightsx = lax.ppermute(weights, 'dp', pair)  4.47 us
    ppermute x1, starting transfers between devices, local(): gotx = lax.ppermute(got, 'dp', pair)  4.38 us
  transfers between devices with their start and end apart: 3, of which 2 were waited for; matrix products, arithmetic and copies ran while one was open for 0% of the time, Pallas kernels for 5%

profile of v9, /device:TPU:1, one launch (start us, length us, event | category | flops | bytes accessed | tf_op | source)
XLA Modules:
  0.0 116.5 jit_solution(6499515164787472827)
XLA Ops:
  0.6 3.6 %shard_map.93 = (bf16[32,40,128]{2,1,0:T(8,128)(2,1)}, f32[8,4096]{1,0:T(8,128)}, f32[8,32,128]{2,1,0:T(8,128)}, f32[8,128]{1,0:T(8,128)}) custom-call(s32[1]{0:T(128)} %bitcast.1.me_ref.refs_0_, s32[1,8]{1,0:T(1,128)} %len_hbm.1, bf16[1,8,32,4096]{3,2,1,0:T(8,128)(2,1)} %x_hbm.1, f32[1,4096]{1,0:T(1,128)} %bitcast.11, bf16[1,8,4096]{2,1,0:T(8,128)(2,1)} %pos_hbm.1, ...), custom_call_target="tpu_custom_call" | custom-call | flops 8000000 | bytes 2904324 | tf_op jit(solution)/shard_map/pallas_call | solution.py:297
  4.3 26.5 %all_to_all.25.refs_0_.refs_1_.refs_2_ = bf16[32,40,128]{2,1,0:T(8,128)(2,1)S(1)} all-to-all(bf16[32,40,128]{2,1,0:T(8,128)(2,1)} %get-tuple-element.15), channel_id=1, replica_groups={{0,2,4,6,8,10,12,14,16,18,20,22,24,26,28,30,32,34,36,38,40,42,44,46,48,..., dimensions={0} | all-to-all | bytes 655360 | tf_op jit(solution)/shard_map/all_to_all | solution.py:327
  30.8 4.4 %collective-permute-start = (bf16[32,40,128]{2,1,0:T(8,128)(2,1)S(1)}, bf16[32,40,128]{2,1,0:T(8,128)(2,1)S(1)}, u32[]{:S(2)}, u32[]{:S(2)}) collective-permute-start(bf16[32,40,128]{2,1,0:T(8,128)(2,1)S(1)} %all_to_all.25.refs_0_.refs_1_.refs_2_), channel_id=1, source_target_pairs={{0,1},{1,0},{2,3},{3,2},{4,5},{5,4},{6,7},{7,6},{8,9},{9,8},{10,11... | collective-permute-start | bytes 983048 | tf_op jit(solution)/shard_map/ppermute | solution.py:358
  35.2 1.2 %collective-permute-done.refs_1_.refs_2_.refs_3_ = bf16[32,40,128]{2,1,0:T(8,128)(2,1)S(1)} collective-permute-done((bf16[32,40,128]{2,1,0:T(8,128)(2,1)S(1)}, bf16[32,40,128]{2,1,0:T(8,128)(2,1)S(1)}, u32[]{:S(2)}, u32[]{:S(2)}) %collective-permute-start) | collective-permute-done | bytes 327712 | tf_op jit(solution)/shard_map/ppermute | solution.py:358
  36.4 0.8 shard_map.94
  37.2 0.0 copy-start.1
  37.3 16.3 %all_to_all.26 = f16[32,8,640]{2,1,0:T(8,128)(2,1)S(1)} all-to-all(f16[32,8,640]{2,1,0:T(8,128)(2,1)S(1)} %convert_element_type.6), channel_id=1, replica_groups={{0,2,4,6,8,10,12,14,16,18,20,22,24,26,28,30,32,34,36,38,40,42,44,46,48,..., dimensions={0} | all-to-all | bytes 655360 | tf_op jit(solution)/shard_map/all_to_all | solution.py:327
  53.6 0.1 convert_reduce_fusion.refs_1_
  53.7 0.2 shard_map.95
  53.9 17.6 %all_to_all.27.refs_0_ = bf16[32,8,640]{2,1,0:T(8,128)(2,1)S(1)} all-to-all(bf16[32,8,640]{2,1,0:T(8,128)(2,1)S(1)} %shard_map.95), channel_id=1, replica_groups={{0,2,4,6,8,10,12,14,16,18,20,22,24,26,28,30,32,34,36,38,40,42,44,46,48,..., dimensions={0} | all-to-all | bytes 655360 | tf_op jit(solution)/shard_map/all_to_all | solution.py:327
  71.5 0.0 copy-start
  71.5 0.0 copy-start.2
  71.5 0.0 copy-start.3
  71.5 0.0 copy-start.4
  71.5 0.0 copy-start.5
  71.5 4.5 %collective-permute-start.1 = (bf16[32,8,640]{2,1,0:T(8,128)(2,1)S(1)}, bf16[32,8,640]{2,1,0:T(8,128)(2,1)S(1)}, u32[]{:S(2)}, u32[]{:S(2)}) collective-permute-start(bf16[32,8,640]{2,1,0:T(8,128)(2,1)S(1)} %all_to_all.27.refs_0_), channel_id=1, source_target_pairs={{0,1},{1,0},{2,3},{3,2},{4,5},{5,4},{6,7},{7,6},{8,9},{9,8},{10,11... | collective-permute-start | bytes 983048 | tf_op jit(solution)/shard_map/ppermute | solution.py:375
  76.0 1.7 %shard_map.96 = (f32[256,128]{1,0:T(8,128)S(1)}, f32[256,128]{1,0:T(8,128)S(1)}, f32[512,128]{1,0:T(8,128)S(1)}, f32[1,128]{1,0:T(1,128)S(1)}) custom-call(bf16[32,8,640]{2,1,0:T(8,128)(2,1)S(1)} %all_to_all.27.refs_0_, bf16[32,40,128]{2,1,0:T(8,128)(2,1)S(1)} %all_to_all.25.refs_0_.refs_1_.refs_2_, ...), custom_call_target="tpu_custom_call" | custom-call | flops 200000000 | bytes 1507840 | tf_op jit(solution)/shard_map/pallas_call | solution.py:297
  77.7 0.0 collective-permute-done.1.refs_1_
  77.7 0.0 copy-done.1
  77.7 1.7 %shard_map.97 = bf16[32,40,128]{2,1,0:T(8,128)(2,1)S(1)} custom-call(s32[1]{0:T(128)} %bitcast.1.me_ref.refs_0_, bf16[32,8,640]{2,1,0:T(8,128)(2,1)S(1)} %collective-permute-done.1.refs_1_, bf16[32,40,128]{2,1,0:T(8,128)(2,1)S(1)} %all_to_all.25.refs_0_.refs_1_.refs_2_, bf16[32,40,128]{2,1,0:T(8,128)(2,1)S(1)} %collective-permute-done.refs_1_.refs_2_.refs_3_, ...), custom_call_target="tpu_custom_call" | custom-call | flops 200000000 | bytes 1851908 | tf_op jit(solution)/shard_map/pallas_call | solution.py:297
  79.3 16.8 %all_to_all.28.in_ref = bf16[32,40,128]{2,1,0:T(8,128)(2,1)S(1)} all-to-all(bf16[32,40,128]{2,1,0:T(8,128)(2,1)S(1)} %shard_map.97), channel_id=1, replica_groups={{0,2,4,6,8,10,12,14,16,18,20,22,24,26,28,30,32,34,36,38,40,42,44,46,48,..., dimensions={0} | all-to-all | bytes 655360 | tf_op jit(solution)/shard_map/all_to_all | solution.py:327
  96.1 0.7 shard_map.99
  96.8 9.8 %all-to-all-start.4 = ((f32[8,32,128]{2,1,0:T(8,128)}), f32[8,32,128]{2,1,0:T(8,128)S(1)}, u32[]{:S(2)}, u32[]{:S(2)}) async-start(f32[8,32,128]{2,1,0:T(8,128)} %shard_map.99), calls=%async_computation.4 | async-start | bytes 262144 | tf_op jit(solution)/shard_map/all_to_all | solution.py:400
  106.6 0.0 copy-done
  106.6 0.0 copy-done.2
  106.6 0.0 copy-done.3
  106.6 0.0 copy-done.4
  106.6 0.0 copy-done.5
  106.6 4.1 %shard_map.98 = (bf16[8,32,4096]{2,1,0:T(8,128)(2,1)}, f32[8,4096]{1,0:T(8,128)}, f32[16,4096]{1,0:T(8,128)}) custom-call(s32[8]{0:T(128)S(1)} %bitcast.14, bf16[32,40,128]{2,1,0:T(8,128)(2,1)S(1)} %all_to_all.28.in_ref, bf16[8,32,4096]{2,1,0:T(8,128)(2,1)S(1)} %bitcast.10, f32[1,4096]{1,0:T(1,128)S(1)} %bitcast.13, f32[8,4096]{1,0:T(8,128)S(1)} %copy-done.2, ...), custom_call_target="tpu_custom_call" | custom-call | flops 10000000 | bytes 5197856 | tf_op jit(solution)/shard_map/pallas_call | solution.py:297
  110.7 5.2 %all-to-all-done.4 = f32[8,32,128]{2,1,0:T(8,128)S(1)} async-done(((f32[8,32,128]{2,1,0:T(8,128)}), f32[8,32,128]{2,1,0:T(8,128)S(1)}, u32[]{:S(2)}, u32[]{:S(2)}) %all-to-all-start.4) | async-done | bytes 131104 | tf_op jit(solution)/shard_map/all_to_all | solution.py:400
  115.9 0.6 reduce_sum.19
  (1 shorter events, 0.0 us)
Async XLA Ops:
  30.8 5.6 %collective-permute-start = (bf16[32,40,128]{2,1,0:T(8,128)(2,1)S(1)}, bf16[32,40,128]{2,1,0:T(8,128)(2,1)S(1)}, u32[]{:S(2)}, u32[]{:S(2)}) collective-permute-start(bf16[32,40,128]{2,1,0:T(8,128)(2,1)S(1)} %all_to_all.25.refs_0_.refs_1_.refs_2_), channel_id=1, source_target_pairs={{0,1},{1,0},{2,3},{3,2},{4,5},{5,4},{6,7},{7,6},{8,9},{9,8},{10,11... | collective-permute-start | bytes 983048 | tf_op jit(solution)/shard_map/ppermute | solution.py:358
  37.2 40.4 %copy-start.1 = (f32[4096]{0:T(1024)S(1)}, f32[4096]{0:T(1024)}, u32[]{:S(2)}) copy-start(f32[4096]{0:T(1024)} %param.8) | copy-start | bytes 49156
  71.5 35.1 %copy-start = (bf16[1,8,32,4096]{3,2,1,0:T(8,128)(2,1)S(1)}, bf16[1,8,32,4096]{3,2,1,0:T(8,128)(2,1)}, u32[]{:S(2)}) copy-start(bf16[1,8,32,4096]{3,2,1,0:T(8,128)(2,1)} %x_hbm.1) | copy-start | bytes 6291460
  71.5 35.1 %copy-start.2 = (f32[8,4096]{1,0:T(8,128)S(1)}, f32[8,4096]{1,0:T(8,128)}, u32[]{:S(2)}) copy-start(f32[8,4096]{1,0:T(8,128)} %get-tuple-element.20.unit_ref) | copy-start | bytes 393220
  71.5 35.1 %copy-start.3 = (f32[8,32,128]{2,1,0:T(8,128)S(1)}, f32[8,32,128]{2,1,0:T(8,128)}, u32[]{:S(2)}) copy-start(f32[8,32,128]{2,1,0:T(8,128)} %get-tuple-element.21.inv_ref) | copy-start | bytes 393220
  71.5 35.1 %copy-start.4 = (f32[8,128]{1,0:T(8,128)S(1)}, f32[8,128]{1,0:T(8,128)}, u32[]{:S(2)}) copy-start(f32[8,128]{1,0:T(8,128)} %get-tuple-element.22.norm_ref) | copy-start | bytes 12292
  71.5 35.1 %copy-start.5 = (s32[1,8]{1,0:T(1,128)S(1)}, s32[1,8]{1,0:T(1,128)}, u32[]{:S(2)}) copy-start(s32[1,8]{1,0:T(1,128)} %len_hbm.1) | copy-start | bytes 100
  71.5 6.2 %collective-permute-start.1 = (bf16[32,8,640]{2,1,0:T(8,128)(2,1)S(1)}, bf16[32,8,640]{2,1,0:T(8,128)(2,1)S(1)}, u32[]{:S(2)}, u32[]{:S(2)}) collective-permute-start(bf16[32,8,640]{2,1,0:T(8,128)(2,1)S(1)} %all_to_all.27.refs_0_), channel_id=1, source_target_pairs={{0,1},{1,0},{2,3},{3,2},{4,5},{5,4},{6,7},{7,6},{8,9},{9,8},{10,11... | collective-permute-start | bytes 983048 | tf_op jit(solution)/shard_map/ppermute | solution.py:375
  96.8 19.1 %all-to-all-start.4 = ((f32[8,32,128]{2,1,0:T(8,128)}), f32[8,32,128]{2,1,0:T(8,128)S(1)}, u32[]{:S(2)}, u32[]{:S(2)}) async-start(f32[8,32,128]{2,1,0:T(8,128)} %shard_map.99), calls=%async_computation.4 | async-start | bytes 262144 | tf_op jit(solution)/shard_map/all_to_all | solution.py:400

commit v10 on v9

--- a/solution.py
+++ b/solution.py
@@ -112,33 +112,43 @@
     return jnp.where(lane < hard, ids, 0.0).astype(jnp.int32)
 
 
-def similar_kernel(hard, got_ref, gotx_ref, sim_ref):
+def half_similar(hard, e, pos, pool, ids, first):
+    sim = lax.dot_general(e, pos, BY_ROW, preferred_element_type=F32)
+    mined = lax.dot_general(e, pool, BY_ROW, preferred_element_type=F32)
+    tail = jnp.zeros(ids.shape, F32)
+    within, tile = ids & (LANES - 1), ids >> 7
+    for k in range(pool.shape[0] // LANES):
+        part = mined[:, k * LANES : (k + 1) * LANES]
+        picked = jnp.take_along_axis(part, within, axis=1, mode="promise_in_bounds")
+        tail = jnp.where(tile == first + k, picked, tail)
+    return sim, tail
+
+
+def own_similar_kernel(hard, got_ref, sim_ref, tail_ref):
+    chips, rows, _ = got_ref.shape
+    q = rows // 5
+    a = got_ref[:, 2 * q :].astype(F32)
+    e, pos = rows_of(a, 0, q).astype(BF16), rows_of(a, q, 2 * q).astype(BF16)
+    pool = got_ref[:, : 2 * q].reshape(chips * 2 * q, LANES)
+    ids = ids_of(rows_of(a, 2 * q, 3 * q), hard)
+    sim_ref[...], tail_ref[...] = half_similar(hard, e, pos, pool, ids, 0)
+
+
+def similar_kernel(hard, got_ref, gotx_ref, own_ref, own_tail_ref, sim_ref):
     chips, rows, _ = got_ref.shape
     q = rows // 5
     half = chips * q
     n = 2 * half
     a = got_ref[:, 2 * q :].astype(F32)
     b = gotx_ref[:, 2 * q :].astype(F32)
-    e = rows_of(a, 0, q).astype(BF16)
-    p = jnp.concatenate([rows_of(a, q, 2 * q), rows_of(b, q, 2 * q)], axis=0).astype(BF16)
-    own_pool = got_ref[:, : 2 * q].reshape(n, LANES)
-    other_pool = gotx_ref[:, : 2 * q].reshape(n, LANES)
+    e, pos = rows_of(a, 0, q).astype(BF16), rows_of(b, q, 2 * q).astype(BF16)
+    pool = gotx_ref[:, : 2 * q].reshape(n, LANES)
     ids = ids_of(rows_of(a, 2 * q, 3 * q), hard)
-    sim = lax.dot_general(e, p, BY_ROW, preferred_element_type=F32) / TEMPERATURE
-    sim_ref[:, :, :n] = sim.reshape(chips, q, n)
-    own_sim = lax.dot_general(e, own_pool, BY_ROW, preferred_element_type=F32)
-    other_sim = lax.dot_general(e, other_pool, BY_ROW, preferred_element_type=F32)
-    tail = jnp.zeros((half, LANES), F32)
-    within, tile = ids & (LANES - 1), ids >> 7
-    for k in range(2 * n // LANES):
-        part = own_sim if k < n // LANES else other_sim
-        first = k * LANES % n
-        picked = jnp.take_along_axis(
-            part[:, first : first + LANES], within, axis=1, mode="promise_in_bounds"
-        )
-        tail = jnp.where(tile == k, picked, tail)
+    sim, tail = half_similar(hard, e, pos, pool, ids, n // LANES)
     lane = lax.broadcasted_iota(jnp.int32, (half, LANES), 1)
-    tail = jnp.where(lane < hard, tail / TEMPERATURE, 0.0)
+    tail = jnp.where(lane < hard, (tail + own_tail_ref[...]) / TEMPERATURE, 0.0)
+    sim_ref[:, :, :half] = (own_ref[...] / TEMPERATURE).reshape(chips, q, half)
+    sim_ref[:, :, half:n] = (sim / TEMPERATURE).reshape(chips, q, half)
     sim_ref[:, :, n:] = tail.reshape(chips, q, LANES)
 
 
@@ -357,11 +367,18 @@
     got = among_chips(out)
     gotx = lax.ppermute(got, "dp", pair)
 
+    half = q_all // 2
+    own = call(
+        bound(own_similar_kernel),
+        [shape((half, half), F32), shape((half, LANES), F32)],
+        [got],
+        50_000_000,
+    )
     (part,) = call(
         bound(similar_kernel),
         [shape((chips, queries, q_all + LANES), F32)],
-        [got, gotx],
-        100_000_000,
+        [got, gotx, *own],
+        50_000_000,
     )
     scores = jnp.sum(among_chips(part.astype(F16)).astype(F32), axis=0)
     (sent,) = call(

time: 118 us -> 118 us (level)
    pallas_call x7 -> x8, Pallas kernels: 12.7 us -> 12.9 us  [call(): pl.pallas_call(kernel, out_shape=list(outs), in_specs=[pl.BlockSpec(memor...]
where the time goes in v10:
time: 118 us; the launch traced here: 116 us
  blocking collectives  77.2 us (65%)
  starting transfers between devices  18.6 us (16%)
  Pallas kernels  12.9 us (11%)
  waiting for transfers between devices  5.95 us (5%)
    all_to_all x4, blocking collectives, among_chips(): lax.all_to_all(x, 'dp', 0, 0, tiled=True, axis_index_groups=same_core)  77.2 us
    pallas_call x8, Pallas kernels, call(): pl.pallas_call(kernel, out_shape=list(outs), in_specs=[pl.BlockSpec(memor...  12.9 us
    all_to_all x1, starting transfers between devices, local(): gain_groups = lax.all_to_all(gain_sent, 'rep', 0, 0, tiled=True)  9.77 us
    all_to_all x1, waiting for transfers between devices, local(): gain_groups = lax.all_to_all(gain_sent, 'rep', 0, 0, tiled=True)  5.22 us
    ppermute x1, starting transfers between devices, local(): weightsx = lax.ppermute(weights, 'dp', pair)  4.47 us
    ppermute x1, starting transfers between devices, local(): gotx = lax.ppermute(got, 'dp', pair)  4.38 us
  transfers between devices with their start and end apart: 3, of which 2 were waited for; matrix products, arithmetic and copies ran while one was open for 0% of the time, Pallas kernels for 5%

profile of v10, /device:TPU:1, one launch (start us, length us, event | category | flops | bytes accessed | tf_op | source)
XLA Modules:
  0.0 116.2 jit_solution(13330459236339452534)
XLA Ops:
  0.6 3.6 %shard_map.93 = (bf16[32,40,128]{2,1,0:T(8,128)(2,1)}, f32[8,4096]{1,0:T(8,128)}, f32[8,32,128]{2,1,0:T(8,128)}, f32[8,128]{1,0:T(8,128)}) custom-call(s32[1]{0:T(128)} %bitcast.1.me_ref.refs_0_, s32[1,8]{1,0:T(1,128)} %len_hbm.1, bf16[1,8,32,4096]{3,2,1,0:T(8,128)(2,1)} %x_hbm.1, f32[1,4096]{1,0:T(1,128)} %bitcast.11, bf16[1,8,4096]{2,1,0:T(8,128)(2,1)} %pos_hbm.1, ...), custom_call_target="tpu_custom_call" | custom-call | flops 8000000 | bytes 2904324 | tf_op jit(solution)/shard_map/pallas_call | solution.py:307
  4.3 26.5 %all_to_all.25.refs_0_.refs_1_.refs_2_ = bf16[32,40,128]{2,1,0:T(8,128)(2,1)S(1)} all-to-all(bf16[32,40,128]{2,1,0:T(8,128)(2,1)} %get-tuple-element.17), channel_id=1, replica_groups={{0,2,4,6,8,10,12,14,16,18,20,22,24,26,28,30,32,34,36,38,40,42,44,46,48,..., dimensions={0} | all-to-all | bytes 655360 | tf_op jit(solution)/shard_map/all_to_all | solution.py:337
  30.8 4.4 %collective-permute-start = (bf16[32,40,128]{2,1,0:T(8,128)(2,1)S(1)}, bf16[32,40,128]{2,1,0:T(8,128)(2,1)S(1)}, u32[]{:S(2)}, u32[]{:S(2)}) collective-permute-start(bf16[32,40,128]{2,1,0:T(8,128)(2,1)S(1)} %all_to_all.25.refs_0_.refs_1_.refs_2_), channel_id=1, source_target_pairs={{0,1},{1,0},{2,3},{3,2},{4,5},{5,4},{6,7},{7,6},{8,9},{9,8},{10,11... | collective-permute-start | bytes 983048 | tf_op jit(solution)/shard_map/ppermute | solution.py:368
  35.2 0.5 shard_map.94
  35.7 0.7 collective-permute-done.refs_1_.refs_2_.refs_3_
  36.4 0.5 shard_map.95
  36.9 0.0 copy-start.1
  37.0 16.3 %all_to_all.26 = f16[32,8,640]{2,1,0:T(8,128)(2,1)S(1)} all-to-all(f16[32,8,640]{2,1,0:T(8,128)(2,1)S(1)} %convert_element_type.6), channel_id=1, replica_groups={{0,2,4,6,8,10,12,14,16,18,20,22,24,26,28,30,32,34,36,38,40,42,44,46,48,..., dimensions={0} | all-to-all | bytes 655360 | tf_op jit(solution)/shard_map/all_to_all | solution.py:337
  53.3 0.1 convert_reduce_fusion.refs_1_
  53.4 0.2 shard_map.96
  53.6 17.6 %all_to_all.27.refs_0_ = bf16[32,8,640]{2,1,0:T(8,128)(2,1)S(1)} all-to-all(bf16[32,8,640]{2,1,0:T(8,128)(2,1)S(1)} %shard_map.96), channel_id=1, replica_groups={{0,2,4,6,8,10,12,14,16,18,20,22,24,26,28,30,32,34,36,38,40,42,44,46,48,..., dimensions={0} | all-to-all | bytes 655360 | tf_op jit(solution)/shard_map/all_to_all | solution.py:337
  71.2 0.0 copy-start
  71.2 0.0 copy-start.2
  71.2 0.0 copy-start.3
  71.2 0.0 copy-start.4
  71.2 0.0 copy-start.5
  71.2 4.5 %collective-permute-start.1 = (bf16[32,8,640]{2,1,0:T(8,128)(2,1)S(1)}, bf16[32,8,640]{2,1,0:T(8,128)(2,1)S(1)}, u32[]{:S(2)}, u32[]{:S(2)}) collective-permute-start(bf16[32,8,640]{2,1,0:T(8,128)(2,1)S(1)} %all_to_all.27.refs_0_), channel_id=1, source_target_pairs={{0,1},{1,0},{2,3},{3,2},{4,5},{5,4},{6,7},{7,6},{8,9},{9,8},{10,11... | collective-permute-start | bytes 983048 | tf_op jit(solution)/shard_map/ppermute | solution.py:392
  75.7 1.7 %shard_map.97 = (f32[256,128]{1,0:T(8,128)S(1)}, f32[256,128]{1,0:T(8,128)S(1)}, f32[512,128]{1,0:T(8,128)S(1)}, f32[1,128]{1,0:T(1,128)S(1)}) custom-call(bf16[32,8,640]{2,1,0:T(8,128)(2,1)S(1)} %all_to_all.27.refs_0_, bf16[32,40,128]{2,1,0:T(8,128)(2,1)S(1)} %all_to_all.25.refs_0_.refs_1_.refs_2_, ...), custom_call_target="tpu_custom_call" | custom-call | flops 200000000 | bytes 1507840 | tf_op jit(solution)/shard_map/pallas_call | solution.py:307
  77.4 0.0 collective-permute-done.1.refs_1_
  77.4 0.0 copy-done.1
  77.4 1.7 %shard_map.98 = bf16[32,40,128]{2,1,0:T(8,128)(2,1)S(1)} custom-call(s32[1]{0:T(128)} %bitcast.1.me_ref.refs_0_, bf16[32,8,640]{2,1,0:T(8,128)(2,1)S(1)} %collective-permute-done.1.refs_1_, bf16[32,40,128]{2,1,0:T(8,128)(2,1)S(1)} %all_to_all.25.refs_0_.refs_1_.refs_2_, bf16[32,40,128]{2,1,0:T(8,128)(2,1)S(1)} %collective-permute-done.refs_1_.refs_2_.refs_3_, ...), custom_call_target="tpu_custom_call" | custom-call | flops 200000000 | bytes 1851908 | tf_op jit(solution)/shard_map/pallas_call | solution.py:307
  79.0 16.8 %all_to_all.28.in_ref = bf16[32,40,128]{2,1,0:T(8,128)(2,1)S(1)} all-to-all(bf16[32,40,128]{2,1,0:T(8,128)(2,1)S(1)} %shard_map.98), channel_id=1, replica_groups={{0,2,4,6,8,10,12,14,16,18,20,22,24,26,28,30,32,34,36,38,40,42,44,46,48,..., dimensions={0} | all-to-all | bytes 655360 | tf_op jit(solution)/shard_map/all_to_all | solution.py:337
  95.8 0.7 shard_map.100
  96.5 9.8 %all-to-all-start.4 = ((f32[8,32,128]{2,1,0:T(8,128)}), f32[8,32,128]{2,1,0:T(8,128)S(1)}, u32[]{:S(2)}, u32[]{:S(2)}) async-start(f32[8,32,128]{2,1,0:T(8,128)} %shard_map.100), calls=%async_computation.4 | async-start | bytes 262144 | tf_op jit(solution)/shard_map/all_to_all | solution.py:417
  106.3 0.0 copy-done
  106.3 0.0 copy-done.2
  106.3 0.0 copy-done.3
  106.3 0.0 copy-done.4
  106.3 0.0 copy-done.5
  106.3 4.1 %shard_map.99 = (bf16[8,32,4096]{2,1,0:T(8,128)(2,1)}, f32[8,4096]{1,0:T(8,128)}, f32[16,4096]{1,0:T(8,128)}) custom-call(s32[8]{0:T(128)S(1)} %bitcast.14, bf16[32,40,128]{2,1,0:T(8,128)(2,1)S(1)} %all_to_all.28.in_ref, bf16[8,32,4096]{2,1,0:T(8,128)(2,1)S(1)} %bitcast.10, f32[1,4096]{1,0:T(1,128)S(1)} %bitcast.13, f32[8,4096]{1,0:T(8,128)S(1)} %copy-done.2, ...), custom_call_target="tpu_custom_call" | custom-call | flops 10000000 | bytes 5197856 | tf_op jit(solution)/shard_map/pallas_call | solution.py:307
  110.4 5.2 %all-to-all-done.4 = f32[8,32,128]{2,1,0:T(8,128)S(1)} async-done(((f32[8,32,128]{2,1,0:T(8,128)}), f32[8,32,128]{2,1,0:T(8,128)S(1)}, u32[]{:S(2)}, u32[]{:S(2)}) %all-to-all-start.4) | async-done | bytes 131104 | tf_op jit(solution)/shard_map/all_to_all | solution.py:417
  115.6 0.6 reduce_sum.19
  (1 shorter events, 0.0 us)
Async XLA Ops:
  30.8 5.6 %collective-permute-start = (bf16[32,40,128]{2,1,0:T(8,128)(2,1)S(1)}, bf16[32,40,128]{2,1,0:T(8,128)(2,1)S(1)}, u32[]{:S(2)}, u32[]{:S(2)}) collective-permute-start(bf16[32,40,128]{2,1,0:T(8,128)(2,1)S(1)} %all_to_all.25.refs_0_.refs_1_.refs_2_), channel_id=1, source_target_pairs={{0,1},{1,0},{2,3},{3,2},{4,5},{5,4},{6,7},{7,6},{8,9},{9,8},{10,11... | collective-permute-start | bytes 983048 | tf_op jit(solution)/shard_map/ppermute | solution.py:368
  36.9 40.4 %copy-start.1 = (f32[4096]{0:T(1024)S(1)}, f32[4096]{0:T(1024)}, u32[]{:S(2)}) copy-start(f32[4096]{0:T(1024)} %param.8) | copy-start | bytes 49156
  71.2 35.1 %copy-start = (bf16[1,8,32,4096]{3,2,1,0:T(8,128)(2,1)S(1)}, bf16[1,8,32,4096]{3,2,1,0:T(8,128)(2,1)}, u32[]{:S(2)}) copy-start(bf16[1,8,32,4096]{3,2,1,0:T(8,128)(2,1)} %x_hbm.1) | copy-start | bytes 6291460
  71.2 35.1 %copy-start.2 = (f32[8,4096]{1,0:T(8,128)S(1)}, f32[8,4096]{1,0:T(8,128)}, u32[]{:S(2)}) copy-start(f32[8,4096]{1,0:T(8,128)} %get-tuple-element.24.unit_ref) | copy-start | bytes 393220
  71.2 35.1 %copy-start.3 = (f32[8,32,128]{2,1,0:T(8,128)S(1)}, f32[8,32,128]{2,1,0:T(8,128)}, u32[]{:S(2)}) copy-start(f32[8,32,128]{2,1,0:T(8,128)} %get-tuple-element.25.inv_ref) | copy-start | bytes 393220
  71.2 35.1 %copy-start.4 = (f32[8,128]{1,0:T(8,128)S(1)}, f32[8,128]{1,0:T(8,128)}, u32[]{:S(2)}) copy-start(f32[8,128]{1,0:T(8,128)} %get-tuple-element.26.norm_ref) | copy-start | bytes 12292
  71.2 35.1 %copy-start.5 = (s32[1,8]{1,0:T(1,128)S(1)}, s32[1,8]{1,0:T(1,128)}, u32[]{:S(2)}) copy-start(s32[1,8]{1,0:T(1,128)} %len_hbm.1) | copy-start | bytes 100
  71.2 6.2 %collective-permute-start.1 = (bf16[32,8,640]{2,1,0:T(8,128)(2,1)S(1)}, bf16[32,8,640]{2,1,0:T(8,128)(2,1)S(1)}, u32[]{:S(2)}, u32[]{:S(2)}) collective-permute-start(bf16[32,8,640]{2,1,0:T(8,128)(2,1)S(1)} %all_to_all.27.refs_0_), channel_id=1, source_target_pairs={{0,1},{1,0},{2,3},{3,2},{4,5},{5,4},{6,7},{7,6},{8,9},{9,8},{10,11... | collective-permute-start | bytes 983048 | tf_op jit(solution)/shard_map/ppermute | solution.py:392
  96.5 19.1 %all-to-all-start.4 = ((f32[8,32,128]{2,1,0:T(8,128)}), f32[8,32,128]{2,1,0:T(8,128)S(1)}, u32[]{:S(2)}, u32[]{:S(2)}) async-start(f32[8,32,128]{2,1,0:T(8,128)} %shard_map.100), calls=%async_computation.4 | async-start | bytes 262144 | tf_op jit(solution)/shard_map/all_to_all | solution.py:417

commit v11 on v10

--- a/solution.py
+++ b/solution.py
@@ -254,7 +254,8 @@
 
 
 def backward_kernel(
-    len_ref, in_ref, x_ref, gain_ref, unit_ref, inv_ref, norm_ref, grad_ref, key_ref, pool_ref, h_ref, row_ref
+    len_ref, in_ref, x_ref, gain_ref, unit_ref, inv_ref, norm_ref, grad_hbm, key_hbm, pool_hbm,
+    h_ref, row_ref, grad_ref, key_ref, pool_ref, grad_sem, small_sem,
 ):
     queries, width = unit_ref.shape
     tokens = x_ref.shape[1]
@@ -269,6 +270,12 @@
         g = block[:q]
         h_ref[:, cols] = g
         dots += g * unit_ref[:, cols]
+    small = [
+        pltpu.make_async_copy(key_ref, key_hbm, small_sem.at[0]),
+        pltpu.make_async_copy(pool_ref, pool_hbm, small_sem.at[1]),
+    ]
+    for copy in small:
+        copy.start()
     along = jnp.sum(dots, axis=1, keepdims=True)
     norm = norm_ref[:, :1]
     for k in range(chunks):
@@ -292,12 +299,17 @@
             cols = slice(k * LANES, (k + 1) * LANES)
             x = x_ref[i, :, cols].astype(F32)
             grad_ref[i, :, cols] = (scale * row_ref[i, :, cols] - back * x).astype(BF16)
+        pltpu.make_async_copy(grad_ref.at[i], grad_hbm.at[i], grad_sem.at[i]).start()
         return carry
 
     lax.fori_loop(0, queries, one_query, 0)
-
-
-def call(kernel, outs, args, flops, smem=(), hbm=(), scratch=(), vmem=40):
+    for i in range(queries):
+        pltpu.make_async_copy(grad_ref.at[i], grad_hbm.at[i], grad_sem.at[i]).wait()
+    for copy in small:
+        copy.wait()
+
+
+def call(kernel, outs, args, flops, smem=(), hbm=(), scratch=(), vmem=40, out_hbm=False):
     def space(i):
         return pltpu.SMEM if i in smem else pltpu.HBM if i in hbm else pltpu.VMEM
 
@@ -308,7 +320,7 @@
         kernel,
         out_shape=list(outs),
         in_specs=[pl.BlockSpec(memory_space=space(i)) for i in range(len(args))],
-        out_specs=[pl.BlockSpec(memory_space=pltpu.VMEM)] * len(outs),
+        out_specs=[pl.BlockSpec(memory_space=pltpu.HBM if out_hbm else pltpu.VMEM)] * len(outs),
         scratch_shapes=list(scratch),
         compiler_params=pltpu.CompilerParams(vmem_limit_bytes=vmem * 1024 * 1024),
         cost_estimate=pl.CostEstimate(flops=flops, bytes_accessed=size, transcendentals=0),
@@ -426,7 +438,16 @@
         10_000_000,
         (0,),
         (),
-        [pltpu.VMEM((queries, width), F32), pltpu.VMEM((queries, 1, width), F32)],
+        [
+            pltpu.VMEM((queries, width), F32),
+            pltpu.VMEM((queries, 1, width), F32),
+            pltpu.VMEM((queries, tokens, width), BF16),
+            pltpu.VMEM((queries, width), F32),
+            pltpu.VMEM((2 * queries, width), F32),
+            pltpu.SemaphoreType.DMA((queries,)),
+            pltpu.SemaphoreType.DMA((2,)),
+        ],
+        out_hbm=True,
     )
     gain_grad = jnp.sum(gain_groups, axis=0).reshape(width)
     return query_grad[None], key_grad[None], pool_grad[None], gain_grad

time: 118 us -> 118 us (level)
  no operation moved by 1% of the time
where the time goes in v11:
time: 118 us; the launch traced here: 116 us
  blocking collectives  77.2 us (65%)
  starting transfers between devices  18.6 us (16%)
  Pallas kernels  12.4 us (11%)
  waiting for transfers between devices  6.46 us (5%)
    all_to_all x4, blocking collectives, among_chips(): lax.all_to_all(x, 'dp', 0, 0, tiled=True, axis_index_groups=same_core)  77.2 us
    pallas_call x8, Pallas kernels, call(): pl.pallas_call(kernel, out_shape=list(outs), in_specs=[pl.BlockSpec(memor...  12.4 us
    all_to_all x1, starting transfers between devices, local(): gain_groups = lax.all_to_all(gain_sent, 'rep', 0, 0, tiled=True)  9.77 us
    all_to_all x1, waiting for transfers between devices, local(): gain_groups = lax.all_to_all(gain_sent, 'rep', 0, 0, tiled=True)  5.74 us
    ppermute x1, starting transfers between devices, local(): weightsx = lax.ppermute(weights, 'dp', pair)  4.47 us
    ppermute x1, starting transfers between devices, local(): gotx = lax.ppermute(got, 'dp', pair)  4.38 us
  transfers between devices with their start and end apart: 3, of which 2 were waited for; matrix products, arithmetic and copies ran while one was open for 0% of the time, Pallas kernels for 5%

profile of v11, /device:TPU:1, one launch (start us, length us, event | category | flops | bytes accessed | tf_op | source)
XLA Modules:
  0.0 116.2 jit_solution(18295293404770779672)
XLA Ops:
  0.6 3.6 %shard_map.93 = (bf16[32,40,128]{2,1,0:T(8,128)(2,1)}, f32[8,4096]{1,0:T(8,128)}, f32[8,32,128]{2,1,0:T(8,128)}, f32[8,128]{1,0:T(8,128)}) custom-call(s32[1]{0:T(128)} %bitcast.1.me_ref.refs_0_, s32[1,8]{1,0:T(1,128)} %len_hbm.1, bf16[1,8,32,4096]{3,2,1,0:T(8,128)(2,1)} %x_hbm.1, f32[1,4096]{1,0:T(1,128)} %bitcast.11, bf16[1,8,4096]{2,1,0:T(8,128)(2,1)} %pos_hbm.1, ...), custom_call_target="tpu_custom_call" | custom-call | flops 8000000 | bytes 2904324 | tf_op jit(solution)/shard_map/pallas_call | solution.py:319
  4.3 26.5 %all_to_all.25.refs_0_.refs_1_.refs_2_ = bf16[32,40,128]{2,1,0:T(8,128)(2,1)S(1)} all-to-all(bf16[32,40,128]{2,1,0:T(8,128)(2,1)} %get-tuple-element.17), channel_id=1, replica_groups={{0,2,4,6,8,10,12,14,16,18,20,22,24,26,28,30,32,34,36,38,40,42,44,46,48,..., dimensions={0} | all-to-all | bytes 655360 | tf_op jit(solution)/shard_map/all_to_all | solution.py:349
  30.8 4.4 %collective-permute-start = (bf16[32,40,128]{2,1,0:T(8,128)(2,1)S(1)}, bf16[32,40,128]{2,1,0:T(8,128)(2,1)S(1)}, u32[]{:S(2)}, u32[]{:S(2)}) collective-permute-start(bf16[32,40,128]{2,1,0:T(8,128)(2,1)S(1)} %all_to_all.25.refs_0_.refs_1_.refs_2_), channel_id=1, source_target_pairs={{0,1},{1,0},{2,3},{3,2},{4,5},{5,4},{6,7},{7,6},{8,9},{9,8},{10,11... | collective-permute-start | bytes 983048 | tf_op jit(solution)/shard_map/ppermute | solution.py:380
  35.2 0.5 shard_map.94
  35.7 0.7 collective-permute-done.refs_1_.refs_2_.refs_3_
  36.4 0.5 shard_map.95
  36.9 0.0 copy-start.1
  37.0 16.3 %all_to_all.26 = f16[32,8,640]{2,1,0:T(8,128)(2,1)S(1)} all-to-all(f16[32,8,640]{2,1,0:T(8,128)(2,1)S(1)} %convert_element_type.6), channel_id=1, replica_groups={{0,2,4,6,8,10,12,14,16,18,20,22,24,26,28,30,32,34,36,38,40,42,44,46,48,..., dimensions={0} | all-to-all | bytes 655360 | tf_op jit(solution)/shard_map/all_to_all | solution.py:349
  53.3 0.1 convert_reduce_fusion.refs_1_
  53.4 0.2 shard_map.96
  53.6 17.6 %all_to_all.27.refs_0_ = bf16[32,8,640]{2,1,0:T(8,128)(2,1)S(1)} all-to-all(bf16[32,8,640]{2,1,0:T(8,128)(2,1)S(1)} %shard_map.96), channel_id=1, replica_groups={{0,2,4,6,8,10,12,14,16,18,20,22,24,26,28,30,32,34,36,38,40,42,44,46,48,..., dimensions={0} | all-to-all | bytes 655360 | tf_op jit(solution)/shard_map/all_to_all | solution.py:349
  71.2 0.0 copy-start
  71.2 0.0 copy-start.2
  71.2 0.0 copy-start.3
  71.2 0.0 copy-start.4
  71.2 0.0 copy-start.5
  71.2 4.5 %collective-permute-start.1 = (bf16[32,8,640]{2,1,0:T(8,128)(2,1)S(1)}, bf16[32,8,640]{2,1,0:T(8,128)(2,1)S(1)}, u32[]{:S(2)}, u32[]{:S(2)}) collective-permute-start(bf16[32,8,640]{2,1,0:T(8,128)(2,1)S(1)} %all_to_all.27.refs_0_), channel_id=1, source_target_pairs={{0,1},{1,0},{2,3},{3,2},{4,5},{5,4},{6,7},{7,6},{8,9},{9,8},{10,11... | collective-permute-start | bytes 983048 | tf_op jit(solution)/shard_map/ppermute | solution.py:404
  75.7 1.7 %shard_map.97 = (f32[256,128]{1,0:T(8,128)S(1)}, f32[256,128]{1,0:T(8,128)S(1)}, f32[512,128]{1,0:T(8,128)S(1)}, f32[1,128]{1,0:T(1,128)S(1)}) custom-call(bf16[32,8,640]{2,1,0:T(8,128)(2,1)S(1)} %all_to_all.27.refs_0_, bf16[32,40,128]{2,1,0:T(8,128)(2,1)S(1)} %all_to_all.25.refs_0_.refs_1_.refs_2_, ...), custom_call_target="tpu_custom_call" | custom-call | flops 200000000 | bytes 1507840 | tf_op jit(solution)/shard_map/pallas_call | solution.py:319
  77.4 0.0 collective-permute-done.1.refs_1_
  77.4 0.0 copy-done.1
  77.4 1.7 %shard_map.98 = bf16[32,40,128]{2,1,0:T(8,128)(2,1)S(1)} custom-call(s32[1]{0:T(128)} %bitcast.1.me_ref.refs_0_, bf16[32,8,640]{2,1,0:T(8,128)(2,1)S(1)} %collective-permute-done.1.refs_1_, bf16[32,40,128]{2,1,0:T(8,128)(2,1)S(1)} %all_to_all.25.refs_0_.refs_1_.refs_2_, bf16[32,40,128]{2,1,0:T(8,128)(2,1)S(1)} %collective-permute-done.refs_1_.refs_2_.refs_3_, ...), custom_call_target="tpu_custom_call" | custom-call | flops 200000000 | bytes 1851908 | tf_op jit(solution)/shard_map/pallas_call | solution.py:319
  79.0 16.8 %all_to_all.28.in_ref = bf16[32,40,128]{2,1,0:T(8,128)(2,1)S(1)} all-to-all(bf16[32,40,128]{2,1,0:T(8,128)(2,1)S(1)} %shard_map.98), channel_id=1, replica_groups={{0,2,4,6,8,10,12,14,16,18,20,22,24,26,28,30,32,34,36,38,40,42,44,46,48,..., dimensions={0} | all-to-all | bytes 655360 | tf_op jit(solution)/shard_map/all_to_all | solution.py:349
  95.8 0.7 shard_map.100
  96.5 9.8 %all-to-all-start.4 = ((f32[8,32,128]{2,1,0:T(8,128)}), f32[8,32,128]{2,1,0:T(8,128)S(1)}, u32[]{:S(2)}, u32[]{:S(2)}) async-start(f32[8,32,128]{2,1,0:T(8,128)} %shard_map.100), calls=%async_computation.4 | async-start | bytes 262144 | tf_op jit(solution)/shard_map/all_to_all | solution.py:429
  106.3 0.0 copy-done
  106.3 0.0 copy-done.2
  106.3 0.0 copy-done.3
  106.3 0.0 copy-done.4
  106.3 0.0 copy-done.5
  106.3 3.5 %shard_map.99 = (bf16[8,32,4096]{2,1,0:T(8,128)(2,1)}, f32[8,4096]{1,0:T(8,128)}, f32[16,4096]{1,0:T(8,128)}) custom-call(s32[8]{0:T(128)S(1)} %bitcast.14, bf16[32,40,128]{2,1,0:T(8,128)(2,1)S(1)} %all_to_all.28.in_ref, bf16[8,32,4096]{2,1,0:T(8,128)(2,1)S(1)} %bitcast.10, f32[1,4096]{1,0:T(1,128)S(1)} %bitcast.13, f32[8,4096]{1,0:T(8,128)S(1)} %copy-done.2, ...), custom_call_target="tpu_custom_call" | custom-call | flops 10000000 | bytes 5197856 | tf_op jit(solution)/shard_map/pallas_call | solution.py:319
  109.9 5.7 %all-to-all-done.4 = f32[8,32,128]{2,1,0:T(8,128)S(1)} async-done(((f32[8,32,128]{2,1,0:T(8,128)}), f32[8,32,128]{2,1,0:T(8,128)S(1)}, u32[]{:S(2)}, u32[]{:S(2)}) %all-to-all-start.4) | async-done | bytes 131104 | tf_op jit(solution)/shard_map/all_to_all | solution.py:429
  115.6 0.6 reduce_sum.19
  (1 shorter events, 0.0 us)
Async XLA Ops:
  30.8 5.6 %collective-permute-start = (bf16[32,40,128]{2,1,0:T(8,128)(2,1)S(1)}, bf16[32,40,128]{2,1,0:T(8,128)(2,1)S(1)}, u32[]{:S(2)}, u32[]{:S(2)}) collective-permute-start(bf16[32,40,128]{2,1,0:T(8,128)(2,1)S(1)} %all_to_all.25.refs_0_.refs_1_.refs_2_), channel_id=1, source_target_pairs={{0,1},{1,0},{2,3},{3,2},{4,5},{5,4},{6,7},{7,6},{8,9},{9,8},{10,11... | collective-permute-start | bytes 983048 | tf_op jit(solution)/shard_map/ppermute | solution.py:380
  36.9 40.4 %copy-start.1 = (f32[4096]{0:T(1024)S(1)}, f32[4096]{0:T(1024)}, u32[]{:S(2)}) copy-start(f32[4096]{0:T(1024)} %param.8) | copy-start | bytes 49156
  71.2 35.1 %copy-start = (bf16[1,8,32,4096]{3,2,1,0:T(8,128)(2,1)S(1)}, bf16[1,8,32,4096]{3,2,1,0:T(8,128)(2,1)}, u32[]{:S(2)}) copy-start(bf16[1,8,32,4096]{3,2,1,0:T(8,128)(2,1)} %x_hbm.1) | copy-start | bytes 6291460
  71.2 35.1 %copy-start.2 = (f32[8,4096]{1,0:T(8,128)S(1)}, f32[8,4096]{1,0:T(8,128)}, u32[]{:S(2)}) copy-start(f32[8,4096]{1,0:T(8,128)} %get-tuple-element.24.unit_ref) | copy-start | bytes 393220
  71.2 35.1 %copy-start.3 = (f32[8,32,128]{2,1,0:T(8,128)S(1)}, f32[8,32,128]{2,1,0:T(8,128)}, u32[]{:S(2)}) copy-start(f32[8,32,128]{2,1,0:T(8,128)} %get-tuple-element.25.inv_ref) | copy-start | bytes 393220
  71.2 35.1 %copy-start.4 = (f32[8,128]{1,0:T(8,128)S(1)}, f32[8,128]{1,0:T(8,128)}, u32[]{:S(2)}) copy-start(f32[8,128]{1,0:T(8,128)} %get-tuple-element.26.norm_ref) | copy-start | bytes 12292
  71.2 35.1 %copy-start.5 = (s32[1,8]{1,0:T(1,128)S(1)}, s32[1,8]{1,0:T(1,128)}, u32[]{:S(2)}) copy-start(s32[1,8]{1,0:T(1,128)} %len_hbm.1) | copy-start | bytes 100
  71.2 6.2 %collective-permute-start.1 = (bf16[32,8,640]{2,1,0:T(8,128)(2,1)S(1)}, bf16[32,8,640]{2,1,0:T(8,128)(2,1)S(1)}, u32[]{:S(2)}, u32[]{:S(2)}) collective-permute-start(bf16[32,8,640]{2,1,0:T(8,128)(2,1)S(1)} %all_to_all.27.refs_0_), channel_id=1, source_target_pairs={{0,1},{1,0},{2,3},{3,2},{4,5},{5,4},{6,7},{7,6},{8,9},{9,8},{10,11... | collective-permute-start | bytes 983048 | tf_op jit(solution)/shard_map/ppermute | solution.py:404
  96.5 19.1 %all-to-all-start.4 = ((f32[8,32,128]{2,1,0:T(8,128)}), f32[8,32,128]{2,1,0:T(8,128)S(1)}, u32[]{:S(2)}, u32[]{:S(2)}) async-start(f32[8,32,128]{2,1,0:T(8,128)} %shard_map.100), calls=%async_computation.4 | async-start | bytes 262144 | tf_op jit(solution)/shard_map/all_to_all | solution.py:429
